TPU v7x, 32 devices: a whole 2x2x4 slice. The times are simulated.
32 devices in a mesh: rep: 4 (over y, x), blk: 8 (over z, core).
Axes of the slice: x: 2, y: 2, z: 4, core: 2. Of those that a mesh axis runs over, the one named last changes fastest.
Arguments:
- feats: bfloat16 [128, 128, 256], P('blk'), may hold values from -6 to 6
- requests: int32 [8, 8], P('blk'), may hold values from 0 to 15
- tile_dest: int32 [8, 64], P('blk'), may hold values from 0 to 15, as said below
- tile_slot: int32 [8, 64], P('blk'), may hold values from 0 to 7, as said below
- tile_vals: bfloat16 [8, 64, 128, 128], P('blk', None, 'rep'), may hold values from -0.25 to 0.25
- w_self: bfloat16 [256, 256], replicated, may hold values from -0.375 to 0.375
- w_neigh: bfloat16 [256, 256], replicated, may hold values from -0.375 to 0.375
- bias: float32 [256], replicated, may hold values from -3 to 3
- cotangent: bfloat16 [128, 128, 256], P('blk', 'rep'), may hold values from -6 to 6
Outputs:
- hidden: bfloat16 [128, 128, 256], P('blk', 'rep')
- grad_self: float32 [256, 256], replicated
- grad_neigh: float32 [256, 256], replicated
- grad_bias: float32 [256], replicated
- feat_grad: bfloat16 [128, 128, 256], P('blk', 'rep')
Inputs may be any that keep to these rules, and one draw needn't show every extreme that they name: `tile_slot`: for each reader b, every owner index is named by exactly 8 of its tiles. `tile_dest`: no two tiles of one reader have both the same destination block and the same owner.
All inputs are finite; a program needn't handle non-finite values.
Results may differ from a plain program's by a relative error of at most 0.015.
Values may be sent and summed in bfloat16 or wider, within the bound.
No kernel may reach another device: no remote copies, remote signals or barrier semaphores. Data moves between devices by JAX's collectives and lax.ppermute only.
A program may use at most 128 MiB of HBM per device.

v0:
```python
import math

import jax
import jax.numpy as jnp
from jax import lax
from jax.sharding import PartitionSpec as P


def collect_blocks(arrivals, send_list, blk_dev):
    onehot = (send_list[:, None] == jnp.arange(blk_dev, dtype=jnp.int32)[None, :]).astype(
        jnp.float32
    )
    return jnp.einsum("rb,rjd->bjd", onehot, arrivals, precision=lax.Precision.HIGHEST)


def on_device(feats, requests, tile_dest, tile_slot, tile_vals, w_self, w_neigh, bias, cotangent):
    owners = lax.axis_size("blk")
    replicas = lax.axis_size("rep")
    blk_dev, tile_rows, features = feats.shape
    quarter = tile_rows // replicas
    per_owner = blk_dev // 2
    rep_index = lax.axis_index("rep")
    send_list = requests[0]
    slot_owner = tile_slot[0]
    ordering = jnp.argsort(slot_owner, stable=True)
    sorted_dest = jnp.take(tile_dest[0], ordering, axis=0)
    grouped = jnp.take(tile_vals[0], ordering, axis=0).reshape(
        owners, per_owner, quarter, tile_rows
    )
    dest_onehot = sorted_dest[:, None] == jnp.arange(blk_dev, dtype=jnp.int32)[None, :]
    own_rows = lax.dynamic_slice_in_dim(feats, rep_index * quarter, quarter, 1)
    outgoing = jnp.take(feats, send_list, axis=0)
    sources = lax.all_to_all(outgoing, "blk", split_axis=0, concat_axis=0, tiled=True)
    products = jnp.einsum("okij,ojd->okid", grouped, sources, preferred_element_type=jnp.float32)
    products = products.reshape(owners * per_owner, quarter * features)
    summed = jnp.dot(dest_onehot.astype(jnp.float32).T, products, precision=lax.Precision.HIGHEST)
    aggregate = summed.reshape(blk_dev, quarter, features).astype(jnp.bfloat16)
    row_count = blk_dev * quarter
    feat_rows = own_rows.reshape(row_count, features)
    agg_rows = aggregate.reshape(row_count, features)
    preact = jnp.dot(feat_rows, w_self, preferred_element_type=jnp.float32)
    preact = preact + jnp.dot(agg_rows, w_neigh, preferred_element_type=jnp.float32) + bias
    hidden = jax.nn.silu(preact).astype(jnp.bfloat16).reshape(blk_dev, quarter, features)
    gating = jax.nn.sigmoid(preact)
    grad_rows = cotangent.reshape(row_count, features).astype(jnp.float32)
    grad_pre = (grad_rows * gating * (1.0 + preact * (1.0 - gating))).astype(jnp.bfloat16)
    grad_scale = 1.0 / math.sqrt(owners * blk_dev * tile_rows)
    self_local = (
        jnp.einsum("nd,ne->de", feat_rows, grad_pre, preferred_element_type=jnp.float32)
        * grad_scale
    )
    neigh_local = (
        jnp.einsum("nd,ne->de", agg_rows, grad_pre, preferred_element_type=jnp.float32) * grad_scale
    )
    bias_local = jnp.sum(grad_pre.astype(jnp.float32), axis=0) * grad_scale
    grad_self, grad_neigh, grad_bias = lax.psum(
        (self_local, neigh_local, bias_local), ("rep", "blk")
    )
    back_rows = jnp.einsum(
        "ne,de->nd", grad_pre, w_neigh, preferred_element_type=jnp.float32
    ).astype(jnp.bfloat16)
    back_flat = back_rows.reshape(blk_dev, quarter * features)
    picked = jnp.dot(
        dest_onehot.astype(jnp.bfloat16), back_flat, preferred_element_type=jnp.float32
    ).astype(jnp.bfloat16)
    picked = picked.reshape(owners, per_owner, quarter, features)
    contributions = jnp.einsum(
        "okij,okid->ojd", grouped, picked, preferred_element_type=jnp.float32
    )
    self_term = jnp.einsum("ne,de->nd", grad_pre, w_self, preferred_element_type=jnp.float32)
    arrivals = lax.all_to_all(
        contributions.astype(jnp.bfloat16), "blk", split_axis=0, concat_axis=0, tiled=True
    ).astype(contributions.dtype)
    collected = collect_blocks(arrivals, send_list, blk_dev)
    neighbour = lax.psum_scatter(
        collected.astype(jnp.bfloat16), "rep", scatter_dimension=1, tiled=True
    ).astype(jnp.float32)
    feat_grad = (self_term.reshape(blk_dev, quarter, features) + neighbour).astype(jnp.bfloat16)
    return (hidden, grad_self, grad_neigh, grad_bias, feat_grad)


def solution(mesh):
    in_specs = (
        P("blk", None, None),
        P("blk", None),
        P("blk", None),
        P("blk", None),
        P("blk", None, "rep", None),
        P(),
        P(),
        P(),
        P("blk", "rep", None),
    )
    out_specs = (P("blk", "rep", None), P(), P(), P(), P("blk", "rep", None))
    return jax.shard_map(
        on_device, mesh=mesh, in_specs=in_specs, out_specs=out_specs, check_vma=False
    )
```

profile of v0, /device:TPU:0, one launch (start us, length us, event | category | flops | bytes accessed | tf_op | source)
XLA Modules:
  0.0 201.5 jit_solution(5034229738717873831)
XLA Ops:
  8.0 0.8 fusion.23
  8.8 0.7 compare_and_fusion
  9.5 0.6 gather_fusion.2
  10.1 0.9 broadcast_select_fusion
  11.0 6.3 %all-to-all-start = ((bf16[8,128,256]{2,1,0:T(8,128)(2,1)}), bf16[8,128,256]{2,1,0:T(8,128)(2,1)S(1)}, u32[]{:S(2)}, u32[]{:S(2)}) async-start(bf16[8,128,256]{2,1,0:T(8,128)(2,1)} %broadcast_select_fusion), calls=%async_computation | async-start | bytes 1048576 | tf_op jit(solution)/shard_map/all_to_all | solution.py:33
  17.3 0.0 reduce-scatter.2.cloned.1.call-start
  17.4 2.0 %sort.17 = (s32[64]{0:T(128)}, s32[64]{0:T(128)S(1)}) sort(s32[64]{0:T(128)S(1)} %bitcast.74, s32[64]{0:T(128)S(1)} %iota.10), dimensions={0}, to_apply=%region_0.0 | sort | flops 384 | bytes 1024 | tf_op jit(solution)/shard_map/jit(argsort)/sort | solution.py:25
  19.4 0.8 gather_fusion
  20.2 0.1 broadcast_in_dim.36
  20.3 0.7 gather_fusion.1
  21.0 0.2 fusion.27
  21.3 11.4 %all-to-all-done = bf16[8,128,256]{2,1,0:T(8,128)(2,1)S(1)} async-done(((bf16[8,128,256]{2,1,0:T(8,128)(2,1)}), bf16[8,128,256]{2,1,0:T(8,128)(2,1)S(1)}, u32[]{:S(2)}, u32[]{:S(2)}) %all-to-all-start) | async-done | bytes 524320 | tf_op jit(solution)/shard_map/all_to_all | solution.py:33
  32.7 0.5 convolution_bitcast_fusion
  33.2 2.0 fusion.5
  35.2 0.1 copy.21
  35.3 1.1 convert_reduce_fusion
  36.4 0.3 convolution_convert_fusion.2
  36.7 0.1 reshape.89
  36.8 0.5 convolution_convert_fusion
  37.3 0.5 fusion.3
  37.8 17.8 %all_to_all.10 = bf16[8,128,256]{2,1,0:T(8,128)(2,1)S(1)} all-to-all(bf16[8,128,256]{2,1,0:T(8,128)(2,1)S(1)} %fusion.3), channel_id=1, replica_groups=mesh['rep'=4,'blk'=8] {'blk'}, dimensions={0} | all-to-all | bytes 1048576 | tf_op jit(solution)/shard_map/all_to_all | solution.py:71
  55.6 1.6 convolution_convert_fusion.1
  57.2 0.0 all-reduce.3.cloned.1.call-start
  57.2 1.0 convolution_multiply_fusion
  58.2 1.0 convolution_multiply_fusion.1
  59.2 0.3 fusion.28
  59.5 38.5 %psum.23 = f32[256]{0:T(256)} all-reduce(f32[256]{0:T(256)S(1)} %broadcast_multiply_fusion), channel_id=1, replica_groups=mesh['rep'=4,'blk'=8] {'rep','blk'}, use_global_device_ids=true, to_apply=%region_4.5 | all-reduce | flops 256 | bytes 2048 | tf_op jit(solution)/shard_map/psum | solution.py:56
  98.0 1.2 fusion.12
  99.2 0.8 copy.25
  100.0 90.7 %all-reduce.3.cloned.1.call-done = (f32[256,256]{1,0:T(8,128)}, f32[256,256]{1,0:T(8,128)}) async-done(((f32[256,256]{1,0:T(8,128)}, f32[256,256]{1,0:T(8,128)}), (f32[256,256]{1,0:T(8,128)}, f32[256,256]{1,0:T(8,128)})) %all-reduce.3.cloned.1.call-update) | async-done | bytes 524304 | tf_op jit(solution)/shard_map/psum | solution.py:56
  190.7 1.7 copy.48
  192.3 1.7 copy.49
  (28 shorter events, 0.1 us)
Async XLA Ops:
  8.0 1.5 copy-start
  8.0 9.4 %copy-start.8 = (s32[1,64]{1,0:T(1,128)S(1)}, s32[1,64]{1,0:T(1,128)}, u32[]{:S(2)}) copy-start(s32[1,64]{1,0:T(1,128)} %param.12) | copy-start | bytes 772
  8.0 11.4 %copy-start.1 = (s32[1,64]{1,0:T(1,128)S(1)}, s32[1,64]{1,0:T(1,128)}, u32[]{:S(2)}) copy-start(s32[1,64]{1,0:T(1,128)} %param.11) | copy-start | bytes 772
  8.0 12.3 %copy-start.3 = (bf16[1,64,32,128]{3,2,1,0:T(8,128)(2,1)S(1)}, bf16[1,64,32,128]{3,2,1,0:T(8,128)(2,1)}, u32[]{:S(2)}) copy-start(bf16[1,64,32,128]{3,2,1,0:T(8,128)(2,1)} %param.13) | copy-start | bytes 1572868
  10.1 10.9 %copy-start.2 = (bf16[256,256]{1,0:T(8,128)(2,1)S(1)}, bf16[256,256]{1,0:T(8,128)(2,1)}, u32[]{:S(2)}) copy-start(bf16[256,256]{1,0:T(8,128)(2,1)} %param.14) | copy-start | bytes 393220
  11.0 21.7 %all-to-all-start = ((bf16[8,128,256]{2,1,0:T(8,128)(2,1)}), bf16[8,128,256]{2,1,0:T(8,128)(2,1)S(1)}, u32[]{:S(2)}, u32[]{:S(2)}) async-start(bf16[8,128,256]{2,1,0:T(8,128)(2,1)} %broadcast_select_fusion), calls=%async_computation | async-start | bytes 1048576 | tf_op jit(solution)/shard_map/all_to_all | solution.py:33
  17.3 80.6 %reduce-scatter.2.cloned.1.call-start = ((), (), s32[]{:S(2)}) async-start(), calls=%async_computation.3 | async-start | bytes 1310720 | tf_op jit(solution)/shard_map/reduce_scatter | solution.py:75
  33.2 2.1 %copy-start.4 = (bf16[256,256]{1,0:T(8,128)(2,1)S(1)}, bf16[256,256]{1,0:T(8,128)(2,1)}, u32[]{:S(2)}) copy-start(bf16[256,256]{1,0:T(8,128)(2,1)} %param.15) | copy-start | bytes 393220
  33.2 2.1 %copy-start.6 = (bf16[16,32,256]{2,1,0:T(8,128)(2,1)S(1)}, bf16[16,32,256]{2,1,0:T(8,128)(2,1)}, u32[]{:S(2)}) copy-start(bf16[16,32,256]{2,1,0:T(8,128)(2,1)} %param.17) | copy-start | bytes 786436
  33.2 2.1 %copy-start.7 = (f32[256]{0:T(256)S(1)}, f32[256]{0:T(256)}, u32[]{:S(2)}) copy-start(f32[256]{0:T(256)} %param.16) | copy-start | bytes 3076
  36.8 18.8 %copy-start.5 = (s32[1,8]{1,0:T(1,128)S(1)}, s32[1,8]{1,0:T(1,128)}, u32[]{:S(2)}) copy-start(s32[1,8]{1,0:T(1,128)} %param.10) | copy-start | bytes 100
  57.2 133.5 %all-reduce.3.cloned.1.call-start = ((), (), s32[]{:S(2)}) async-start(), calls=%async_computation.4 | async-start | bytes 1048576 | tf_op jit(solution)/shard_map/psum | solution.py:56
Sparse Core Ops, SparseCore 0:
  57.3 26.9 reduce-scatter.1
Sparse Core Ops, SparseCore 1:
  63.7 127.0 all-reduce.2
where the time goes:
time: 202 us; the launch traced here: 201 us
  waiting for transfers between devices  102 us (50%)
  blocking collectives  56.3 us (28%)
  between operations  15.7 us (8%)
  matrix products  8.76 us (4%)
  local copies, waits for them, and re-layouts  6.51 us (3%)
  starting transfers between devices  6.41 us (3%)
  other arithmetic  5.64 us (3%)
    psum x1, waiting for transfers between devices, on_device(): lax.psum((self_local, neigh_local, bias_local), ('rep', 'blk'))  90.7 us
    psum x1, blocking collectives, on_device(): lax.psum((self_local, neigh_local, bias_local), ('rep', 'blk'))  38.5 us
    all_to_all x1, blocking collectives, on_device(): lax.all_to_all(contributions.astype(jnp.bfloat16), 'blk', split_axis=0, c...  17.8 us
    all_to_all x1, waiting for transfers between devices, on_device(): lax.all_to_all(outgoing, 'blk', split_axis=0, concat_axis=0, tiled=True)  11.4 us
    all_to_all x1, starting transfers between devices, on_device(): lax.all_to_all(outgoing, 'blk', split_axis=0, concat_axis=0, tiled=True)  6.33 us
    unnamed x21, local copies, waits for them, and re-layouts  4.17 us
  transfers between devices with their start and end apart: 3, of which 2 were waited for; matrix products, arithmetic and copies ran while one was open for 4% of the time, Pallas kernels for 0%

commit v1 on v0

v1 whole, which is shorter than its diff:
```python
import math

import jax
import jax.numpy as jnp
from jax import lax
from jax.experimental import pallas as pl
from jax.experimental.pallas import tpu as pltpu
from jax.sharding import PartitionSpec as P

BF16 = jnp.bfloat16
F32 = jnp.float32
PAD = 16
LIMIT = 56 * 1024 * 1024
NT = (((1,), (1,)), ((), ()))

VMEM = pl.BlockSpec(memory_space=pltpu.VMEM)
SMEM = pl.BlockSpec(memory_space=pltpu.SMEM)
ANY = pl.BlockSpec(memory_space=pl.ANY)


def call(body, in_specs, out_shape, out_specs, scratch=(), name=None, flops=0, bytes_accessed=0):
    return pl.pallas_call(
        body,
        in_specs=in_specs,
        out_shape=out_shape,
        out_specs=out_specs,
        scratch_shapes=scratch,
        name=name,
        cost_estimate=pl.CostEstimate(
            flops=flops, bytes_accessed=bytes_accessed, transcendentals=0
        ),
        compiler_params=pltpu.CompilerParams(vmem_limit_bytes=LIMIT),
    )


def struct(shape, dtype):
    return jax.ShapeDtypeStruct(shape, dtype)


def aligned(index, size):
    return pl.ds(pl.multiple_of(index * size, size), size)


def dot(a, b):
    return jnp.dot(a, b, preferred_element_type=F32)


def butterfly_sum(terms):
    while len(terms) > 1:
        terms = [terms[i] + terms[i + 1] for i in range(0, len(terms), 2)]
    return terms[0]


def split_rows(row):
    high = row.astype(BF16)
    low = (row - high.astype(F32)).astype(BF16)
    place = lax.broadcasted_iota(jnp.int32, (PAD, row.shape[1]), 0)
    spread = jnp.where(place == 0, high.astype(F32), 0.0)
    spread = jnp.where(place == 1, low.astype(F32), spread)
    return spread.astype(BF16)


def join_rows(rows):
    return jnp.sum(rows.astype(F32), axis=0, keepdims=True)


def swap(array, axis, size, distance):
    return lax.ppermute(array, axis, [(i, i ^ distance) for i in range(size)])


def prepare_kernel(
    dest, slot, tiles, feats, w_self, bias, dense, dense_t, rows_t, pre_self, rows, sem
):
    tile_count, quarter, width = tiles.shape[1:]
    owners = dense.shape[1] // width
    rep = lax.axis_index("rep")
    copy = pltpu.make_async_copy(feats.at[:, aligned(rep, quarter), :], rows, sem)
    copy.start()
    dense[...] = jnp.zeros_like(dense)

    def place(t, carry):
        dense[aligned(dest[0, t], quarter), aligned(slot[0, t], width)] = tiles[0, t]
        return carry

    lax.fori_loop(0, tile_count, place, 0)

    def turn(o, carry):
        dense_t[aligned(o, width), :] = dense[:, aligned(o, width)].T
        return carry

    lax.fori_loop(0, owners, turn, 0)
    copy.wait()
    own = rows[...].reshape(rows.shape[0] * quarter, rows.shape[2])
    rows_t[...] = own.T
    pre_self[...] = dot(own, w_self[...]) + bias[...]


def layer_kernel(
    grad_scale, owners, dense, dense_t, sources, rows_t, pre_self, cotangent, w_self, w_neigh,
    hidden, self_term, *rest
):
    messages, contributions, gradients = rest[:-2], rest[-2], rest[-1]
    replicas = len(messages)
    features = w_self.shape[0]
    width = contributions.shape[1]
    quarter = width // replicas
    share = features // replicas
    zs = owners // 2
    rep = lax.axis_index("rep")
    agg = dot(dense[...], sources[...]).astype(BF16)
    preact = pre_self[...] + dot(agg, w_neigh[...])
    gating = jax.nn.sigmoid(preact)
    hidden[...] = (preact * gating).astype(BF16).reshape(hidden.shape)
    grads = cotangent[...].reshape(preact.shape).astype(F32)
    grad_pre = (grads * gating * (1.0 + preact * (1.0 - gating))).astype(BF16)
    back = lax.dot_general(grad_pre, w_neigh[...], NT, preferred_element_type=F32).astype(BF16)

    def contribute(o, carry):
        contributions[o] = dot(dense_t[aligned(o, width), :], back).astype(BF16)
        return carry

    lax.fori_loop(0, owners, contribute, 0, unroll=owners <= 8)
    gradients[0] = (dot(rows_t[...], grad_pre) * grad_scale).astype(BF16)
    gradients[1] = (dot(agg.T, grad_pre) * grad_scale).astype(BF16)
    bias_rows = split_rows(
        jnp.sum(grad_pre.astype(F32), axis=0, keepdims=True) * grad_scale
    )
    base = owners * quarter
    for k, message in enumerate(messages):
        target = rep ^ k
        for core in range(2):
            for z in range(zs):
                start = (core * zs + z) * quarter
                message[start : start + quarter] = contributions[
                    2 * z + core, aligned(target, quarter), :
                ]
        for half in range(2):
            start = base + half * share
            message[start : start + share] = gradients[half, aligned(target, share), :]
        message[base + 2 * share :] = bias_rows
    self_term[...] = lax.dot_general(grad_pre, w_self[...], NT, preferred_element_type=F32)


def rep_sum_kernel(share, *refs):
    arrived, keep, send = refs[:-2], refs[-2], refs[-1]
    core = lax.axis_index("blk") % 2
    rows = keep.shape[0] - PAD - share
    base = 2 * rows
    bias_rows = split_rows(butterfly_sum([join_rows(a[base + 2 * share :]) for a in arrived]))
    for out, side in ((keep, core), (send, 1 - core)):
        total = sum(a[aligned(side, rows), :].astype(F32) for a in arrived)
        out[:rows] = total.astype(BF16)
        place = pl.ds(pl.multiple_of(base + side * share, PAD), share)
        total = sum(a[place, :].astype(F32) for a in arrived)
        out[rows : rows + share] = total.astype(BF16)
        out[rows + share :] = bias_rows


def core_join_kernel(share, keep, got, *messages):
    zs = len(messages)
    z = lax.axis_index("blk") // 2
    rows = keep.shape[0] - PAD - share
    quarter = rows // zs
    grads = keep[rows : rows + share].astype(F32) + got[rows : rows + share].astype(F32)
    grads = grads.astype(BF16)
    bias_rows = split_rows(join_rows(keep[rows + share :]) + join_rows(got[rows + share :]))
    for k, message in enumerate(messages):
        place = aligned(z ^ k, quarter)
        message[:quarter] = keep[place, :]
        message[quarter : 2 * quarter] = got[place, :]
        message[2 * quarter : 2 * quarter + share] = grads
        message[2 * quarter + share :] = bias_rows


def finish_kernel(share, requests, self_term, *refs):
    arrived, (feat_grad, piece, grad_bias, total) = refs[:-4], refs[-4:]
    quarter = total.shape[1]
    blk = lax.axis_index("blk")
    base = 2 * quarter
    piece[...] = butterfly_sum([a[base : base + share].astype(F32) for a in arrived]).astype(BF16)
    bias_sum = butterfly_sum([join_rows(a[base + share :]) for a in arrived])
    grad_bias[...] = bias_sum
    total[...] = self_term[...].reshape(total.shape)
    for k, message in enumerate(arrived):
        for other in range(2):
            block = requests[0, blk ^ (2 * k + other)]
            total[block] += message[other * quarter : (other + 1) * quarter].astype(F32)
    feat_grad[...] = total[...].astype(BF16)


def gather_kernel(*refs):
    pieces, out = refs[:-1], refs[-1]
    share = pieces[0].shape[0]
    rep = lax.axis_index("rep")
    for k, piece in enumerate(pieces):
        out[aligned(rep ^ k, share), :] = piece[...]


def widen_kernel(mine, other, grad_self, grad_neigh):
    core = lax.axis_index("blk") % 2
    first = core == 0
    a = mine[...].astype(F32)
    b = other[...].astype(F32)
    grad_self[...] = jnp.where(first, a, b)
    grad_neigh[...] = jnp.where(first, b, a)


def on_device(feats, requests, tile_dest, tile_slot, tile_vals, w_self, w_neigh, bias, cotangent):
    owners = lax.axis_size("blk")
    replicas = lax.axis_size("rep")
    zs = owners // 2
    blk_dev, width, features = feats.shape
    quarter = width // replicas
    row_count = blk_dev * quarter
    share = features // replicas
    grad_scale = 1.0 / math.sqrt(owners * blk_dev * width)

    outgoing = feats.at[requests[0]].get(mode="promise_in_bounds")
    sources = lax.all_to_all(outgoing, "blk", split_axis=0, concat_axis=0, tiled=True)
    dense, dense_t, rows_t, pre_self = call(
        prepare_kernel,
        [SMEM, SMEM, VMEM, ANY, VMEM, VMEM],
        (
            struct((row_count, owners * width), BF16),
            struct((owners * width, row_count), BF16),
            struct((features, row_count), BF16),
            struct((row_count, features), F32),
        ),
        (VMEM,) * 4,
        (pltpu.VMEM((blk_dev, quarter, features), BF16), pltpu.SemaphoreType.DMA),
        name="prepare",
        flops=2 * row_count * features * features,
        bytes_accessed=4 * 1024 * 1024,
    )(tile_dest, tile_slot, tile_vals, feats, w_self, bias.reshape(1, features))

    message_rows = owners * quarter + 2 * share + PAD
    outs = call(
        lambda *refs: layer_kernel(grad_scale, owners, *refs),
        [VMEM] * 8,
        (
            struct((blk_dev, quarter, features), BF16),
            struct((row_count, features), F32),
        )
        + (struct((message_rows, features), BF16),) * replicas,
        (VMEM,) * (2 + replicas),
        (
            pltpu.VMEM((owners, width, features), BF16),
            pltpu.VMEM((2, features, features), BF16),
        ),
        name="layer",
        flops=4 * row_count * features * owners * width,
        bytes_accessed=6 * 1024 * 1024,
    )(
        dense, dense_t, sources.reshape(owners * width, features), rows_t, pre_self, cotangent,
        w_self, w_neigh,
    )
    hidden, self_term, messages = outs[0], outs[1], outs[2:]
    arrived = [messages[0]] + [
        swap(messages[k], "rep", replicas, k) for k in range(1, replicas)
    ]
    half = struct((zs * quarter + share + PAD, features), BF16)
    keep, send = call(
        lambda *refs: rep_sum_kernel(share, *refs),
        [VMEM] * replicas,
        (half, half),
        (VMEM, VMEM),
        name="rep_sum",
        bytes_accessed=1024 * 1024,
    )(*arrived)
    got = swap(send, "blk", owners, 1)
    parcels = call(
        lambda *refs: core_join_kernel(share, *refs),
        [VMEM, VMEM],
        (struct((2 * quarter + share + PAD, features), BF16),) * zs,
        (VMEM,) * zs,
        name="core_join",
        bytes_accessed=512 * 1024,
    )(keep, got)
    landed = [parcels[0]] + [swap(parcels[k], "blk", owners, 2 * k) for k in range(1, zs)]
    feat_grad, piece, grad_bias = call(
        lambda *refs: finish_kernel(share, *refs),
        [SMEM, VMEM] + [VMEM] * zs,
        (
            struct((blk_dev, quarter, features), BF16),
            struct((share, features), BF16),
            struct((1, features), F32),
        ),
        (VMEM,) * 3,
        (pltpu.VMEM((blk_dev, quarter, features), F32),),
        name="finish",
        bytes_accessed=1024 * 1024,
    )(requests, self_term, *landed)
    pieces = [piece] + [swap(piece, "rep", replicas, k) for k in range(1, replicas)]
    whole = struct((features, features), F32)
    mine = call(
        gather_kernel,
        [VMEM] * replicas,
        struct((features, features), BF16),
        VMEM,
        name="gather_pieces",
    )(*pieces)
    other = swap(mine, "blk", owners, 1)
    grad_self, grad_neigh = call(
        widen_kernel, [VMEM, VMEM], (whole, whole), (VMEM, VMEM), name="widen"
    )(mine, other)
    return (hidden, grad_self, grad_neigh, grad_bias.reshape(features), feat_grad)


def solution(mesh):
    in_specs = (
        P("blk", None, None),
        P("blk", None),
        P("blk", None),
        P("blk", None),
        P("blk", None, "rep", None),
        P(),
        P(),
        P(),
        P("blk", "rep", None),
    )
    out_specs = (P("blk", "rep", None), P(), P(), P(), P("blk", "rep", None))
    return jax.shard_map(
        on_device, mesh=mesh, in_specs=in_specs, out_specs=out_specs, check_vma=False
    )
```

time: 202 us -> 75.3 us (0.37)
  waiting for transfers between devices: 102 us -> 31.6 us
  blocking collectives: 56.3 us -> 0 us
  Pallas kernels: 0 us -> 17.5 us
  between operations: 15.7 us -> 0.67 us
  starting transfers between devices: 6.41 us -> 17.7 us
  matrix products: 8.76 us -> 0 us
  other arithmetic: 5.64 us -> 0.67 us
    psum x1 -> x0, waiting for transfers between devices: 90.7 us -> none  [on_device(): lax.psum((self_local, neigh_local, bias_local), ('rep', 'blk'))]
    psum x1 -> x0, blocking collectives: 38.5 us -> none  [on_device(): lax.psum((self_local, neigh_local, bias_local), ('rep', 'blk'))]
    ppermute x0 -> x11, waiting for transfers between devices: none -> 20.3 us  [swap(): return lax.ppermute(array, axis, [(i, i ^ distance) for i in range(size)])]
    all_to_all x1 -> x0, blocking collectives: 17.8 us -> none  [on_device(): lax.all_to_all(contributions.astype(jnp.bfloat16), 'blk', split_axis=0, c...]
    pallas_call x0 -> x7, Pallas kernels: none -> 17.5 us  [the longest x1 4.57 us: on_device(): call(lambda *refs: layer_kernel(grad_scale, owners, *refs), [VMEM] * 8, (...]
    ppermute x0 -> x11, starting transfers between devices: none -> 11.4 us  [swap(): return lax.ppermute(array, axis, [(i, i ^ distance) for i in range(size)])]
    dot_general x11 -> x0, matrix products: 8.76 us -> none  [the longest x1 1.96 us: on_device(): jnp.dot(dest_onehot.astype(jnp.float32).T, products, precision=lax.Precis...]
    sort x1 -> x0, other arithmetic: 2.03 us -> none  [on_device(): ordering = jnp.argsort(slot_owner, stable=True)]
  transfers between devices with their start and end apart: 3 -> 12, of which waited for: 2 -> 10; matrix products, arithmetic and copies ran while one was open for 4% -> 0% of each run, Pallas kernels for 0% -> 5%
where the time goes in v1:
time: 75.3 us; the launch traced here: 74.9 us
  waiting for transfers between devices  31.6 us (42%)
  starting transfers between devices  17.7 us (24%)
  Pallas kernels  17.5 us (23%)
  local copies, waits for them, and re-layouts  6.73 us (9%)
    ppermute x11, waiting for transfers between devices, swap(): return lax.ppermute(array, axis, [(i, i ^ distance) for i in range(size)])  20.3 us
    ppermute x11, starting transfers between devices, swap(): return lax.ppermute(array, axis, [(i, i ^ distance) for i in range(size)])  11.4 us
    all_to_all x1, waiting for transfers between devices, on_device(): lax.all_to_all(outgoing, 'blk', split_axis=0, concat_axis=0, tiled=True)  11.3 us
    all_to_all x1, starting transfers between devices, on_device(): lax.all_to_all(outgoing, 'blk', split_axis=0, concat_axis=0, tiled=True)  6.33 us
    pallas_call x1, Pallas kernels, on_device(): call(lambda *refs: layer_kernel(grad_scale, owners, *refs), [VMEM] * 8, (...  4.57 us
    unnamed x24, local copies, waits for them, and re-layouts  4.11 us
    pallas_call x1, Pallas kernels, on_device(): call(prepare_kernel, [SMEM, SMEM, VMEM, ANY, VMEM, VMEM], (struct((row_co...  4.02 us
    gather x1, local copies, waits for them, and re-layouts, on_device(): outgoing = feats.at[requests[0]].get(mode='promise_in_bounds')  2.62 us
  transfers between devices with their start and end apart: 12, of which 10 were waited for; matrix products, arithmetic and copies ran while one was open for 0% of the time, Pallas kernels for 5%

profile of v1, /device:TPU:0, one launch (start us, length us, event | category | flops | bytes accessed | tf_op | source)
XLA Modules:
  0.0 74.9 jit_solution(5427147625043298344)
XLA Ops:
  0.6 0.7 fusion
  1.3 2.6 %gather_fusion = bf16[8,128,256]{2,1,0:T(8,128)(2,1)} fusion(bf16[16,128,256]{2,1,0:T(8,128)(2,1)} %feats.1, s32[1024]{0:T(1024)S(1)} %pad_clamp_fusion), kind=kCustom, calls=%fused_computation | custom fusion | bytes 1048608 | tf_op jit(solution)/shard_map/gather | solution.py:218
  3.9 6.3 %all-to-all-start = ((bf16[8,128,256]{2,1,0:T(8,128)(2,1)}), bf16[8,128,256]{2,1,0:T(8,128)(2,1)S(1)}, u32[]{:S(2)}, u32[]{:S(2)}) async-start(bf16[8,128,256]{2,1,0:T(8,128)(2,1)} %gather_fusion), calls=%async_computation | async-start | bytes 1048576 | tf_op jit(solution)/shard_map/all_to_all | solution.py:219
  10.2 4.0 %prepare.1 = (bf16[512,1024]{1,0:T(8,128)(2,1)}, bf16[1024,512]{1,0:T(8,128)(2,1)}, bf16[256,512]{1,0:T(8,128)(2,1)}, f32[512,256]{1,0:T(8,128)}) custom-call(s32[1,64]{1,0:T(1,128)} %dest.1, s32[1,64]{1,0:T(1,128)} %slot.1, bf16[1,64,32,128]{3,2,1,0:T(8,128)(2,1)} %tiles.1, bf16[16,128,256]{2,1,0:T(8,128)(2,1)} %feats.1, bf16[256,256]{1,0:T(8,128)(2,1)} %refs_6_.1, ...), custom_call_target="tpu_custom_call" | custom-call | flops 67108864 | bytes 4194304 | tf_op jit(solution)/shard_map/prepare/pallas_call | solution.py:220
  14.3 11.3 %all-to-all-done = bf16[8,128,256]{2,1,0:T(8,128)(2,1)S(1)} async-done(((bf16[8,128,256]{2,1,0:T(8,128)(2,1)}), bf16[8,128,256]{2,1,0:T(8,128)(2,1)S(1)}, u32[]{:S(2)}, u32[]{:S(2)}) %all-to-all-start) | async-done | bytes 524320 | tf_op jit(solution)/shard_map/all_to_all | solution.py:219
  25.6 0.8 %copy-done = bf16[8,128,256]{2,1,0:T(8,128)(2,1)} copy-done((bf16[8,128,256]{2,1,0:T(8,128)(2,1)}, bf16[8,128,256]{2,1,0:T(8,128)(2,1)S(1)}, u32[]{:S(2)}) %copy-start) | copy-done | bytes 524312
  26.4 4.6 %layer.1 = (bf16[16,32,256]{2,1,0:T(8,128)(2,1)}, f32[512,256]{1,0:T(8,128)}, bf16[400,256]{1,0:T(8,128)(2,1)}, bf16[400,256]{1,0:T(8,128)(2,1)}, bf16[400,256]{1,0:T(8,128)(2,1)}, /*index=5*/bf16[400,256]{1,0:T(8,128)(2,1)}) custom-call(bf16[512,1024]{1,0:T(8,128)(2,1)} %get-tuple-element.26.refs_0_, bf16[1024,512]{1,0:T(8,128)(2,1)} %get-tuple-element.27.refs_1_, ...), custom_call_target="tpu_custom_call" | custom-call | flops 536870912 | bytes 6291456 | tf_op jit(solution)/shard_map/layer/pallas_call | solution.py:237
  31.0 1.5 %collective-permute-start = (bf16[400,256]{1,0:T(8,128)(2,1)}, bf16[400,256]{1,0:T(8,128)(2,1)S(1)}, u32[]{:S(2)}, u32[]{:S(2)}) collective-permute-start(bf16[400,256]{1,0:T(8,128)(2,1)} %get-tuple-element.33), channel_id=1, source_target_pairs={{0,8},{8,0},{16,24},{24,16},{1,9},{9,1},{17,25},{25,17},{2,10},{10... | collective-permute-start | bytes 614408 | tf_op jit(solution)/shard_map/ppermute | solution.py:68
  32.5 1.5 %collective-permute-start.1 = (bf16[400,256]{1,0:T(8,128)(2,1)}, bf16[400,256]{1,0:T(8,128)(2,1)S(1)}, u32[]{:S(2)}, u32[]{:S(2)}) collective-permute-start(bf16[400,256]{1,0:T(8,128)(2,1)} %get-tuple-element.34), channel_id=1, source_target_pairs={{0,16},{8,24},{16,0},{24,8},{1,17},{9,25},{17,1},{25,9},{2,18},{10... | collective-permute-start | bytes 614408 | tf_op jit(solution)/shard_map/ppermute | solution.py:68
  34.5 4.7 %collective-permute-done.refs_1_ = bf16[400,256]{1,0:T(8,128)(2,1)S(1)} collective-permute-done((bf16[400,256]{1,0:T(8,128)(2,1)}, bf16[400,256]{1,0:T(8,128)(2,1)S(1)}, u32[]{:S(2)}, u32[]{:S(2)}) %collective-permute-start) | collective-permute-done | bytes 204832 | tf_op jit(solution)/shard_map/ppermute | solution.py:68
  39.2 4.2 %collective-permute-done.1.refs_2_ = bf16[400,256]{1,0:T(8,128)(2,1)S(1)} collective-permute-done((bf16[400,256]{1,0:T(8,128)(2,1)}, bf16[400,256]{1,0:T(8,128)(2,1)S(1)}, u32[]{:S(2)}, u32[]{:S(2)}) %collective-permute-start.1) | collective-permute-done | bytes 204832 | tf_op jit(solution)/shard_map/ppermute | solution.py:68
  43.4 0.7 copy-done.2
  44.2 2.0 %rep_sum.1 = (bf16[208,256]{1,0:T(8,128)(2,1)}, bf16[208,256]{1,0:T(8,128)(2,1)}) custom-call(bf16[400,256]{1,0:T(8,128)(2,1)} %get-tuple-element.32.refs_0_, bf16[400,256]{1,0:T(8,128)(2,1)} %copy-done.1, bf16[400,256]{1,0:T(8,128)(2,1)} %copy-done.2, bf16[400,256]{1,0:T(8,128)(2,1)} %copy-done.3), custom_call_target="tpu_custom_call" | custom-call | bytes 1048576 | tf_op jit(solution)/shard_map/rep_sum/pallas_call | solution.py:262
  46.2 1.5 %collective-permute-done.3.refs_1_ = bf16[208,256]{1,0:T(8,128)(2,1)S(1)} collective-permute-done((bf16[208,256]{1,0:T(8,128)(2,1)}, bf16[208,256]{1,0:T(8,128)(2,1)S(1)}, u32[]{:S(2)}, u32[]{:S(2)}) %collective-permute-start.3) | collective-permute-done | bytes 106528 | tf_op jit(solution)/shard_map/ppermute | solution.py:68
  47.7 0.6 copy-done.5
  48.3 1.7 %core_join.1 = (bf16[144,256]{1,0:T(8,128)(2,1)}, bf16[144,256]{1,0:T(8,128)(2,1)}, bf16[144,256]{1,0:T(8,128)(2,1)}, bf16[144,256]{1,0:T(8,128)(2,1)}) custom-call(bf16[208,256]{1,0:T(8,128)(2,1)} %get-tuple-element.36.refs_0_, bf16[208,256]{1,0:T(8,128)(2,1)} %copy-done.5), custom_call_target="tpu_custom_call" | custom-call | bytes 524288 | tf_op jit(solution)/shard_map/core_join/pallas_call | solution.py:271
  50.0 2.2 %collective-permute-start.5 = (bf16[144,256]{1,0:T(8,128)(2,1)}, bf16[144,256]{1,0:T(8,128)(2,1)S(1)}, u32[]{:S(2)}, u32[]{:S(2)}) collective-permute-start(bf16[144,256]{1,0:T(8,128)(2,1)} %get-tuple-element.40), channel_id=1, source_target_pairs={{0,4},{1,5},{2,6},{3,7},{4,0},{5,1},{6,2},{7,3},{8,12},{9,13},{10,... | collective-permute-start | bytes 221192 | tf_op jit(solution)/shard_map/ppermute | solution.py:68
  52.3 2.1 %collective-permute-start.6 = (bf16[144,256]{1,0:T(8,128)(2,1)}, bf16[144,256]{1,0:T(8,128)(2,1)S(1)}, u32[]{:S(2)}, u32[]{:S(2)}) collective-permute-start(bf16[144,256]{1,0:T(8,128)(2,1)} %get-tuple-element.41), channel_id=1, source_target_pairs={{0,6},{1,7},{2,4},{3,5},{4,2},{5,3},{6,0},{7,1},{8,14},{9,15},{10,... | collective-permute-start | bytes 221192 | tf_op jit(solution)/shard_map/ppermute | solution.py:68
  54.4 1.2 %collective-permute-done.4.refs_3_ = bf16[144,256]{1,0:T(8,128)(2,1)S(1)} collective-permute-done((bf16[144,256]{1,0:T(8,128)(2,1)}, bf16[144,256]{1,0:T(8,128)(2,1)S(1)}, u32[]{:S(2)}, u32[]{:S(2)}) %collective-permute-start.4) | collective-permute-done | bytes 73760 | tf_op jit(solution)/shard_map/ppermute | solution.py:68
  55.6 3.8 %collective-permute-done.5.refs_4_ = bf16[144,256]{1,0:T(8,128)(2,1)S(1)} collective-permute-done((bf16[144,256]{1,0:T(8,128)(2,1)}, bf16[144,256]{1,0:T(8,128)(2,1)S(1)}, u32[]{:S(2)}, u32[]{:S(2)}) %collective-permute-start.5) | collective-permute-done | bytes 73760 | tf_op jit(solution)/shard_map/ppermute | solution.py:68
  59.4 0.6 copy-done.7
  60.0 2.0 %finish.1 = (bf16[16,32,256]{2,1,0:T(8,128)(2,1)}, bf16[64,256]{1,0:T(8,128)(2,1)}, f32[1,256]{1,0:T(1,128)}) custom-call(s32[1,8]{1,0:T(1,128)} %refs_0_.1, f32[512,256]{1,0:T(8,128)} %get-tuple-element.31.refs_1_, bf16[144,256]{1,0:T(8,128)(2,1)} %get-tuple-element.38.refs_2_, bf16[144,256]{1,0:T(8,128)(2,1)} %copy-done.6, bf16[144,256]{1,0:T(8,128)(2,1)} %copy-done.7, ...), custom_call_target="tpu_custom_call" | custom-call | bytes 1048576 | tf_op jit(solution)/shard_map/finish/pallas_call | solution.py:280
  62.0 1.5 %collective-permute-start.9 = (bf16[64,256]{1,0:T(8,128)(2,1)}, bf16[64,256]{1,0:T(8,128)(2,1)S(1)}, u32[]{:S(2)}, u32[]{:S(2)}) collective-permute-start(bf16[64,256]{1,0:T(8,128)(2,1)} %get-tuple-element.42.refs_0_), channel_id=1, source_target_pairs={{0,24},{8,16},{16,8},{24,0},{1,25},{9,17},{17,9},{25,1},{2,26},{10... | collective-permute-start | bytes 98312 | tf_op jit(solution)/shard_map/ppermute | solution.py:68
  63.5 1.2 %collective-permute-start.8 = (bf16[64,256]{1,0:T(8,128)(2,1)}, bf16[64,256]{1,0:T(8,128)(2,1)S(1)}, u32[]{:S(2)}, u32[]{:S(2)}) collective-permute-start(bf16[64,256]{1,0:T(8,128)(2,1)} %get-tuple-element.42.refs_0_), channel_id=1, source_target_pairs={{0,16},{8,24},{16,0},{24,8},{1,17},{9,25},{17,1},{25,9},{2,18},{10... | collective-permute-start | bytes 98312 | tf_op jit(solution)/shard_map/ppermute | solution.py:68
  64.6 0.8 %collective-permute-start.7 = (bf16[64,256]{1,0:T(8,128)(2,1)}, bf16[64,256]{1,0:T(8,128)(2,1)S(1)}, u32[]{:S(2)}, u32[]{:S(2)}) collective-permute-start(bf16[64,256]{1,0:T(8,128)(2,1)} %get-tuple-element.42.refs_0_), channel_id=1, source_target_pairs={{0,8},{8,0},{16,24},{24,16},{1,9},{9,1},{17,25},{25,17},{2,10},{10... | collective-permute-start | bytes 98312 | tf_op jit(solution)/shard_map/ppermute | solution.py:68
  65.5 1.5 %collective-permute-done.9.refs_3_ = bf16[64,256]{1,0:T(8,128)(2,1)S(1)} collective-permute-done((bf16[64,256]{1,0:T(8,128)(2,1)}, bf16[64,256]{1,0:T(8,128)(2,1)S(1)}, u32[]{:S(2)}, u32[]{:S(2)}) %collective-permute-start.9) | collective-permute-done | bytes 32800 | tf_op jit(solution)/shard_map/ppermute | solution.py:68
  67.6 1.1 %collective-permute-done.7.refs_1_ = bf16[64,256]{1,0:T(8,128)(2,1)S(1)} collective-permute-done((bf16[64,256]{1,0:T(8,128)(2,1)}, bf16[64,256]{1,0:T(8,128)(2,1)S(1)}, u32[]{:S(2)}, u32[]{:S(2)}) %collective-permute-start.7) | collective-permute-done | bytes 32800 | tf_op jit(solution)/shard_map/ppermute | solution.py:68
  68.8 0.6 copy-done.11
  69.4 1.5 %gather_pieces.1.mine = bf16[256,256]{1,0:T(8,128)(2,1)} custom-call(bf16[64,256]{1,0:T(8,128)(2,1)} %get-tuple-element.42.refs_0_, bf16[64,256]{1,0:T(8,128)(2,1)} %copy-done.11, bf16[64,256]{1,0:T(8,128)(2,1)} %copy-done.10, bf16[64,256]{1,0:T(8,128)(2,1)} %copy-done.9), custom_call_target="tpu_custom_call" | custom-call | tf_op jit(solution)/shard_map/gather_pieces/pallas_call | solution.py:295
  70.9 1.6 %collective-permute-done.10.other = bf16[256,256]{1,0:T(8,128)(2,1)S(1)} collective-permute-done((bf16[256,256]{1,0:T(8,128)(2,1)}, bf16[256,256]{1,0:T(8,128)(2,1)S(1)}, u32[]{:S(2)}, u32[]{:S(2)}) %collective-permute-start.10) | collective-permute-done | bytes 131104 | tf_op jit(solution)/shard_map/ppermute | solution.py:68
  72.4 0.6 copy-done.4
  73.1 1.8 %widen.1 = (f32[256,256]{1,0:T(8,128)}, f32[256,256]{1,0:T(8,128)}) custom-call(bf16[256,256]{1,0:T(8,128)(2,1)} %gather_pieces.1.mine, bf16[256,256]{1,0:T(8,128)(2,1)} %copy-done.4), custom_call_target="tpu_custom_call" | custom-call | tf_op jit(solution)/shard_map/widen/pallas_call | solution.py:303
  (26 shorter events, 1.2 us)
Async XLA Ops:
  3.9 21.7 %all-to-all-start = ((bf16[8,128,256]{2,1,0:T(8,128)(2,1)}), bf16[8,128,256]{2,1,0:T(8,128)(2,1)S(1)}, u32[]{:S(2)}, u32[]{:S(2)}) async-start(bf16[8,128,256]{2,1,0:T(8,128)(2,1)} %gather_fusion), calls=%async_computation | async-start | bytes 1048576 | tf_op jit(solution)/shard_map/all_to_all | solution.py:219
  25.6 0.8 %copy-start = (bf16[8,128,256]{2,1,0:T(8,128)(2,1)}, bf16[8,128,256]{2,1,0:T(8,128)(2,1)S(1)}, u32[]{:S(2)}) copy-start(bf16[8,128,256]{2,1,0:T(8,128)(2,1)S(1)} %all-to-all-done) | copy-start | bytes 1572868
  31.0 8.2 %collective-permute-start = (bf16[400,256]{1,0:T(8,128)(2,1)}, bf16[400,256]{1,0:T(8,128)(2,1)S(1)}, u32[]{:S(2)}, u32[]{:S(2)}) collective-permute-start(bf16[400,256]{1,0:T(8,128)(2,1)} %get-tuple-element.33), channel_id=1, source_target_pairs={{0,8},{8,0},{16,24},{24,16},{1,9},{9,1},{17,25},{25,17},{2,10},{10... | collective-permute-start | bytes 614408 | tf_op jit(solution)/shard_map/ppermute | solution.py:68
  32.5 10.9 %collective-permute-start.1 = (bf16[400,256]{1,0:T(8,128)(2,1)}, bf16[400,256]{1,0:T(8,128)(2,1)S(1)}, u32[]{:S(2)}, u32[]{:S(2)}) collective-permute-start(bf16[400,256]{1,0:T(8,128)(2,1)} %get-tuple-element.34), channel_id=1, source_target_pairs={{0,16},{8,24},{16,0},{24,8},{1,17},{9,25},{17,1},{25,9},{2,18},{10... | collective-permute-start | bytes 614408 | tf_op jit(solution)/shard_map/ppermute | solution.py:68
  34.0 9.4 %collective-permute-start.2 = (bf16[400,256]{1,0:T(8,128)(2,1)}, bf16[400,256]{1,0:T(8,128)(2,1)S(1)}, u32[]{:S(2)}, u32[]{:S(2)}) collective-permute-start(bf16[400,256]{1,0:T(8,128)(2,1)} %get-tuple-element.35), channel_id=1, source_target_pairs={{0,24},{8,16},{16,8},{24,0},{1,25},{9,17},{17,9},{25,1},{2,26},{10... | collective-permute-start | bytes 614408 | tf_op jit(solution)/shard_map/ppermute | solution.py:68
  39.2 4.2 %copy-start.1 = (bf16[400,256]{1,0:T(8,128)(2,1)}, bf16[400,256]{1,0:T(8,128)(2,1)S(1)}, u32[]{:S(2)}) copy-start(bf16[400,256]{1,0:T(8,128)(2,1)S(1)} %collective-permute-done.refs_1_) | copy-start | bytes 614404
  43.4 0.7 copy-start.2
  43.4 0.7 copy-start.3
  46.2 1.5 %collective-permute-start.3 = (bf16[208,256]{1,0:T(8,128)(2,1)}, bf16[208,256]{1,0:T(8,128)(2,1)S(1)}, u32[]{:S(2)}, u32[]{:S(2)}) collective-permute-start(bf16[208,256]{1,0:T(8,128)(2,1)} %get-tuple-element.37), channel_id=1, source_target_pairs={{0,1},{1,0},{2,3},{3,2},{4,5},{5,4},{6,7},{7,6},{8,9},{9,8},{10,11... | collective-permute-start | bytes 319496 | tf_op jit(solution)/shard_map/ppermute | solution.py:68
  47.7 0.6 copy-start.5
  50.0 5.6 %collective-permute-start.4 = (bf16[144,256]{1,0:T(8,128)(2,1)}, bf16[144,256]{1,0:T(8,128)(2,1)S(1)}, u32[]{:S(2)}, u32[]{:S(2)}) collective-permute-start(bf16[144,256]{1,0:T(8,128)(2,1)} %get-tuple-element.39), channel_id=1, source_target_pairs={{0,2},{1,3},{2,0},{3,1},{4,6},{5,7},{6,4},{7,5},{8,10},{9,11},{10,... | collective-permute-start | bytes 221192 | tf_op jit(solution)/shard_map/ppermute | solution.py:68
  50.0 9.4 %collective-permute-start.5 = (bf16[144,256]{1,0:T(8,128)(2,1)}, bf16[144,256]{1,0:T(8,128)(2,1)S(1)}, u32[]{:S(2)}, u32[]{:S(2)}) collective-permute-start(bf16[144,256]{1,0:T(8,128)(2,1)} %get-tuple-element.40), channel_id=1, source_target_pairs={{0,4},{1,5},{2,6},{3,7},{4,0},{5,1},{6,2},{7,3},{8,12},{9,13},{10,... | collective-permute-start | bytes 221192 | tf_op jit(solution)/shard_map/ppermute | solution.py:68
  52.3 7.1 %collective-permute-start.6 = (bf16[144,256]{1,0:T(8,128)(2,1)}, bf16[144,256]{1,0:T(8,128)(2,1)S(1)}, u32[]{:S(2)}, u32[]{:S(2)}) collective-permute-start(bf16[144,256]{1,0:T(8,128)(2,1)} %get-tuple-element.41), channel_id=1, source_target_pairs={{0,6},{1,7},{2,4},{3,5},{4,2},{5,3},{6,0},{7,1},{8,14},{9,15},{10,... | collective-permute-start | bytes 221192 | tf_op jit(solution)/shard_map/ppermute | solution.py:68
  55.6 3.8 %copy-start.6 = (bf16[144,256]{1,0:T(8,128)(2,1)}, bf16[144,256]{1,0:T(8,128)(2,1)S(1)}, u32[]{:S(2)}) copy-start(bf16[144,256]{1,0:T(8,128)(2,1)S(1)} %collective-permute-done.4.refs_3_) | copy-start | bytes 221188
  59.4 0.6 copy-start.7
  59.4 0.6 copy-start.8
  62.0 5.0 %collective-permute-start.9 = (bf16[64,256]{1,0:T(8,128)(2,1)}, bf16[64,256]{1,0:T(8,128)(2,1)S(1)}, u32[]{:S(2)}, u32[]{:S(2)}) collective-permute-start(bf16[64,256]{1,0:T(8,128)(2,1)} %get-tuple-element.42.refs_0_), channel_id=1, source_target_pairs={{0,24},{8,16},{16,8},{24,0},{1,25},{9,17},{17,9},{25,1},{2,26},{10... | collective-permute-start | bytes 98312 | tf_op jit(solution)/shard_map/ppermute | solution.py:68
  63.5 4.1 %collective-permute-start.8 = (bf16[64,256]{1,0:T(8,128)(2,1)}, bf16[64,256]{1,0:T(8,128)(2,1)S(1)}, u32[]{:S(2)}, u32[]{:S(2)}) collective-permute-start(bf16[64,256]{1,0:T(8,128)(2,1)} %get-tuple-element.42.refs_0_), channel_id=1, source_target_pairs={{0,16},{8,24},{16,0},{24,8},{1,17},{9,25},{17,1},{25,9},{2,18},{10... | collective-permute-start | bytes 98312 | tf_op jit(solution)/shard_map/ppermute | solution.py:68
  64.6 4.1 %collective-permute-start.7 = (bf16[64,256]{1,0:T(8,128)(2,1)}, bf16[64,256]{1,0:T(8,128)(2,1)S(1)}, u32[]{:S(2)}, u32[]{:S(2)}) collective-permute-start(bf16[64,256]{1,0:T(8,128)(2,1)} %get-tuple-element.42.refs_0_), channel_id=1, source_target_pairs={{0,8},{8,0},{16,24},{24,16},{1,9},{9,1},{17,25},{25,17},{2,10},{10... | collective-permute-start | bytes 98312 | tf_op jit(solution)/shard_map/ppermute | solution.py:68
  67.0 1.7 %copy-start.9 = (bf16[64,256]{1,0:T(8,128)(2,1)}, bf16[64,256]{1,0:T(8,128)(2,1)S(1)}, u32[]{:S(2)}) copy-start(bf16[64,256]{1,0:T(8,128)(2,1)S(1)} %collective-permute-done.9.refs_3_) | copy-start | bytes 98308
  67.6 1.2 %copy-start.10 = (bf16[64,256]{1,0:T(8,128)(2,1)}, bf16[64,256]{1,0:T(8,128)(2,1)S(1)}, u32[]{:S(2)}) copy-start(bf16[64,256]{1,0:T(8,128)(2,1)S(1)} %collective-permute-done.8.refs_2_) | copy-start | bytes 98308
  68.8 0.6 copy-start.11
  70.9 1.6 %collective-permute-start.10 = (bf16[256,256]{1,0:T(8,128)(2,1)}, bf16[256,256]{1,0:T(8,128)(2,1)S(1)}, u32[]{:S(2)}, u32[]{:S(2)}) collective-permute-start(bf16[256,256]{1,0:T(8,128)(2,1)} %gather_pieces.1.mine), channel_id=1, source_target_pairs={{0,1},{1,0},{2,3},{3,2},{4,5},{5,4},{6,7},{7,6},{8,9},{9,8},{10,11... | collective-permute-start | bytes 393224 | tf_op jit(solution)/shard_map/ppermute | solution.py:68
  72.4 0.6 copy-start.4

commit v2 on v1

--- a/solution.py
+++ b/solution.py
@@ -10,27 +10,37 @@
 BF16 = jnp.bfloat16
 F32 = jnp.float32
 PAD = 16
-LIMIT = 56 * 1024 * 1024
+MIB = 1024 * 1024
 NT = (((1,), (1,)), ((), ()))
 
 VMEM = pl.BlockSpec(memory_space=pltpu.VMEM)
 SMEM = pl.BlockSpec(memory_space=pltpu.SMEM)
-ANY = pl.BlockSpec(memory_space=pl.ANY)
-
-
-def call(body, in_specs, out_shape, out_specs, scratch=(), name=None, flops=0, bytes_accessed=0):
-    return pl.pallas_call(
-        body,
-        in_specs=in_specs,
-        out_shape=out_shape,
-        out_specs=out_specs,
-        scratch_shapes=scratch,
-        name=name,
-        cost_estimate=pl.CostEstimate(
-            flops=flops, bytes_accessed=bytes_accessed, transcendentals=0
-        ),
-        compiler_params=pltpu.CompilerParams(vmem_limit_bytes=LIMIT),
-    )
+HBM = pl.BlockSpec(memory_space=pltpu.HBM)
+
+
+def size_of(array):
+    return math.prod(array.shape) * jnp.dtype(array.dtype).itemsize
+
+
+def call(body, in_specs, out_shape, out_specs, scratch=(), name=None, flops=0, limit=0):
+    def run(*operands):
+        moved = sum(size_of(a) for a in jax.tree.leaves((operands, out_shape)))
+        return pl.pallas_call(
+            body,
+            in_specs=in_specs,
+            out_shape=out_shape,
+            out_specs=out_specs,
+            scratch_shapes=scratch,
+            name=name,
+            cost_estimate=pl.CostEstimate(
+                flops=flops, bytes_accessed=moved, transcendentals=0
+            ),
+            compiler_params=pltpu.CompilerParams(
+                vmem_limit_bytes=limit or min(moved + moved // 4 + 2 * MIB, 56 * MIB)
+            ),
+        )(*operands)
+
+    return run
 
 
 def struct(shape, dtype):
@@ -68,59 +78,96 @@
     return lax.ppermute(array, axis, [(i, i ^ distance) for i in range(size)])
 
 
+def pick_kernel(requests_in, feats, out, requests, sems):
+    pltpu.sync_copy(requests_in, requests)
+    copies = [
+        pltpu.make_async_copy(feats.at[requests[0, reader]], out.at[reader], sems.at[reader])
+        for reader in range(out.shape[0])
+    ]
+    for copy in copies:
+        copy.start()
+    for copy in copies:
+        copy.wait()
+
+
 def prepare_kernel(
-    dest, slot, tiles, feats, w_self, bias, dense, dense_t, rows_t, pre_self, rows, sem
+    owners, dest, slot, tiles, feats, w_self, w_neigh, cotangent, packed, rows, sem
 ):
     tile_count, quarter, width = tiles.shape[1:]
-    owners = dense.shape[1] // width
+    row_count = packed.shape[1]
+    features = w_self.shape[0]
+    per_slab = row_count // width
+    slabs = owners // per_slab
     rep = lax.axis_index("rep")
     copy = pltpu.make_async_copy(feats.at[:, aligned(rep, quarter), :], rows, sem)
     copy.start()
-    dense[...] = jnp.zeros_like(dense)
+    packed[:slabs] = jnp.zeros((slabs, row_count, row_count), packed.dtype)
 
     def place(t, carry):
-        dense[aligned(dest[0, t], quarter), aligned(slot[0, t], width)] = tiles[0, t]
+        owner = slot[0, t]
+        packed[
+            owner // per_slab, aligned(dest[0, t], quarter), aligned(owner % per_slab, width)
+        ] = tiles[0, t]
         return carry
 
     lax.fori_loop(0, tile_count, place, 0)
 
-    def turn(o, carry):
-        dense_t[aligned(o, width), :] = dense[:, aligned(o, width)].T
+    def turn(slab, carry):
+        packed[slabs + slab] = packed[slab].T
         return carry
 
-    lax.fori_loop(0, owners, turn, 0)
+    lax.fori_loop(0, slabs, turn, 0)
     copy.wait()
-    own = rows[...].reshape(rows.shape[0] * quarter, rows.shape[2])
-    rows_t[...] = own.T
-    pre_self[...] = dot(own, w_self[...]) + bias[...]
-
-
-def layer_kernel(
-    grad_scale, owners, dense, dense_t, sources, rows_t, pre_self, cotangent, w_self, w_neigh,
-    hidden, self_term, *rest
-):
-    messages, contributions, gradients = rest[:-2], rest[-2], rest[-1]
-    replicas = len(messages)
-    features = w_self.shape[0]
+    own = rows[...].reshape(row_count, features)
+    packed[2 * slabs, :, :features] = own
+    packed[2 * slabs, :, features:] = cotangent[...].reshape(row_count, features)
+    packed[2 * slabs + 1, :features] = own.T
+    packed[2 * slabs + 1, features:, :features] = w_self[...]
+    packed[2 * slabs + 1, features:, features:] = w_neigh[...]
+
+
+def layer_kernel(grad_scale, owners, replicas, sources, packed, bias, *refs):
+    preact_out, grad_pre_out, messages = refs[0], refs[1], refs[2 : 2 + replicas]
+    contributions, gradients = refs[2 + replicas :]
+    row_count, features = preact_out.shape
     width = contributions.shape[1]
     quarter = width // replicas
     share = features // replicas
+    per_slab = row_count // width
+    slabs = owners // per_slab
     zs = owners // 2
     rep = lax.axis_index("rep")
-    agg = dot(dense[...], sources[...]).astype(BF16)
-    preact = pre_self[...] + dot(agg, w_neigh[...])
+    rows = packed[2 * slabs, :, :features]
+    cotangent = packed[2 * slabs, :, features:]
+    rows_t = packed[2 * slabs + 1, :features]
+    w_self = packed[2 * slabs + 1, features:, :features]
+    w_neigh = packed[2 * slabs + 1, features:, features:]
+    agg = dot(packed[0], sources[:row_count])
+    if slabs <= 4:
+        for slab in range(1, slabs):
+            agg += dot(packed[slab], sources[slab * row_count : (slab + 1) * row_count])
+    else:
+        agg = lax.fori_loop(
+            1, slabs, lambda i, a: a + dot(packed[i], sources[aligned(i, row_count), :]), agg
+        )
+    agg = agg.astype(BF16)
+    preact = dot(rows, w_self) + dot(agg, w_neigh) + bias[...]
+    preact_out[...] = preact
     gating = jax.nn.sigmoid(preact)
-    hidden[...] = (preact * gating).astype(BF16).reshape(hidden.shape)
-    grads = cotangent[...].reshape(preact.shape).astype(F32)
-    grad_pre = (grads * gating * (1.0 + preact * (1.0 - gating))).astype(BF16)
-    back = lax.dot_general(grad_pre, w_neigh[...], NT, preferred_element_type=F32).astype(BF16)
-
-    def contribute(o, carry):
-        contributions[o] = dot(dense_t[aligned(o, width), :], back).astype(BF16)
+    grad_pre = (
+        cotangent.astype(F32) * gating * (1.0 + preact * (1.0 - gating))
+    ).astype(BF16)
+    grad_pre_out[...] = grad_pre
+    back = lax.dot_general(grad_pre, w_neigh, NT, preferred_element_type=F32).astype(BF16)
+
+    def contribute(slab, carry):
+        contributions[pl.ds(slab * per_slab, per_slab)] = (
+            dot(packed[slabs + slab], back).astype(BF16).reshape(per_slab, width, features)
+        )
         return carry
 
-    lax.fori_loop(0, owners, contribute, 0, unroll=owners <= 8)
-    gradients[0] = (dot(rows_t[...], grad_pre) * grad_scale).astype(BF16)
+    lax.fori_loop(0, slabs, contribute, 0, unroll=slabs <= 4)
+    gradients[0] = (dot(rows_t, grad_pre) * grad_scale).astype(BF16)
     gradients[1] = (dot(agg.T, grad_pre) * grad_scale).astype(BF16)
     bias_rows = split_rows(
         jnp.sum(grad_pre.astype(F32), axis=0, keepdims=True) * grad_scale
@@ -138,7 +185,12 @@
             start = base + half * share
             message[start : start + share] = gradients[half, aligned(target, share), :]
         message[base + 2 * share :] = bias_rows
-    self_term[...] = lax.dot_general(grad_pre, w_self[...], NT, preferred_element_type=F32)
+
+
+def own_kernel(preact, grad_pre, w_self, hidden, self_term):
+    value = preact[...]
+    hidden[...] = (value * jax.nn.sigmoid(value)).astype(BF16).reshape(hidden.shape)
+    self_term[...] = lax.dot_general(grad_pre[...], w_self[...], NT, preferred_element_type=F32)
 
 
 def rep_sum_kernel(share, *refs):
@@ -172,14 +224,19 @@
         message[2 * quarter + share :] = bias_rows
 
 
-def finish_kernel(share, requests, self_term, *refs):
-    arrived, (feat_grad, piece, grad_bias, total) = refs[:-4], refs[-4:]
+def piece_kernel(*refs):
+    arrived, (piece, grad_bias) = refs[:-2], refs[-2:]
+    share = piece.shape[0]
+    base = arrived[0].shape[0] - PAD - share
+    piece[...] = butterfly_sum([a[base : base + share].astype(F32) for a in arrived]).astype(BF16)
+    grad_bias[...] = butterfly_sum([join_rows(a[base + share :]) for a in arrived])
+
+
+def finish_kernel(requests_in, self_term, *refs):
+    arrived, (feat_grad, total, requests) = refs[:-3], refs[-3:]
+    pltpu.sync_copy(requests_in, requests)
     quarter = total.shape[1]
     blk = lax.axis_index("blk")
-    base = 2 * quarter
-    piece[...] = butterfly_sum([a[base : base + share].astype(F32) for a in arrived]).astype(BF16)
-    bias_sum = butterfly_sum([join_rows(a[base + share :]) for a in arrived])
-    grad_bias[...] = bias_sum
     total[...] = self_term[...].reshape(total.shape)
     for k, message in enumerate(arrived):
         for other in range(2):
@@ -215,32 +272,31 @@
     share = features // replicas
     grad_scale = 1.0 / math.sqrt(owners * blk_dev * width)
 
-    outgoing = feats.at[requests[0]].get(mode="promise_in_bounds")
+    outgoing = call(
+        pick_kernel,
+        [HBM, HBM],
+        struct((owners, width, features), BF16),
+        VMEM,
+        (pltpu.SMEM((1, owners), jnp.int32), pltpu.SemaphoreType.DMA((owners,))),
+        name="pick",
+        limit=56 * MIB,
+    )(requests, feats)
     sources = lax.all_to_all(outgoing, "blk", split_axis=0, concat_axis=0, tiled=True)
-    dense, dense_t, rows_t, pre_self = call(
-        prepare_kernel,
-        [SMEM, SMEM, VMEM, ANY, VMEM, VMEM],
-        (
-            struct((row_count, owners * width), BF16),
-            struct((owners * width, row_count), BF16),
-            struct((features, row_count), BF16),
-            struct((row_count, features), F32),
-        ),
-        (VMEM,) * 4,
+    per_slab = row_count // width
+    packed = call(
+        lambda *refs: prepare_kernel(owners, *refs),
+        [SMEM, SMEM, VMEM, HBM, VMEM, VMEM, VMEM],
+        struct((2 * (owners // per_slab) + 2, row_count, row_count), BF16),
+        VMEM,
         (pltpu.VMEM((blk_dev, quarter, features), BF16), pltpu.SemaphoreType.DMA),
         name="prepare",
-        flops=2 * row_count * features * features,
-        bytes_accessed=4 * 1024 * 1024,
-    )(tile_dest, tile_slot, tile_vals, feats, w_self, bias.reshape(1, features))
+    )(tile_dest, tile_slot, tile_vals, feats, w_self, w_neigh, cotangent)
 
     message_rows = owners * quarter + 2 * share + PAD
     outs = call(
-        lambda *refs: layer_kernel(grad_scale, owners, *refs),
-        [VMEM] * 8,
-        (
-            struct((blk_dev, quarter, features), BF16),
-            struct((row_count, features), F32),
-        )
+        lambda *refs: layer_kernel(grad_scale, owners, replicas, *refs),
+        [VMEM] * 3,
+        (struct((row_count, features), F32), struct((row_count, features), BF16))
         + (struct((message_rows, features), BF16),) * replicas,
         (VMEM,) * (2 + replicas),
         (
@@ -249,15 +305,20 @@
         ),
         name="layer",
         flops=4 * row_count * features * owners * width,
-        bytes_accessed=6 * 1024 * 1024,
-    )(
-        dense, dense_t, sources.reshape(owners * width, features), rows_t, pre_self, cotangent,
-        w_self, w_neigh,
-    )
-    hidden, self_term, messages = outs[0], outs[1], outs[2:]
+    )(sources.reshape(owners * width, features), packed, bias.reshape(1, features))
+    messages = outs[2:]
+    hidden, self_term = call(
+        own_kernel,
+        [VMEM] * 3,
+        (struct((blk_dev, quarter, features), BF16), struct((row_count, features), F32)),
+        (VMEM, VMEM),
+        name="own",
+        flops=2 * row_count * features * features,
+    )(outs[0], outs[1], w_self)
     arrived = [messages[0]] + [
         swap(messages[k], "rep", replicas, k) for k in range(1, replicas)
     ]
+    arrived[-1], self_term = lax.optimization_barrier((arrived[-1], self_term))
     half = struct((zs * quarter + share + PAD, features), BF16)
     keep, send = call(
         lambda *refs: rep_sum_kernel(share, *refs),
@@ -265,7 +326,6 @@
         (half, half),
         (VMEM, VMEM),
         name="rep_sum",
-        bytes_accessed=1024 * 1024,
     )(*arrived)
     got = swap(send, "blk", owners, 1)
     parcels = call(
@@ -274,23 +334,28 @@
         (struct((2 * quarter + share + PAD, features), BF16),) * zs,
         (VMEM,) * zs,
         name="core_join",
-        bytes_accessed=512 * 1024,
     )(keep, got)
     landed = [parcels[0]] + [swap(parcels[k], "blk", owners, 2 * k) for k in range(1, zs)]
-    feat_grad, piece, grad_bias = call(
-        lambda *refs: finish_kernel(share, *refs),
-        [SMEM, VMEM] + [VMEM] * zs,
+    piece, grad_bias = call(
+        piece_kernel,
+        [VMEM] * zs,
+        (struct((share, features), BF16), struct((1, features), F32)),
+        (VMEM, VMEM),
+        name="piece",
+    )(*landed)
+    feat_grad = call(
+        finish_kernel,
+        [HBM, VMEM] + [VMEM] * zs,
+        struct((blk_dev, quarter, features), BF16),
+        VMEM,
         (
-            struct((blk_dev, quarter, features), BF16),
-            struct((share, features), BF16),
-            struct((1, features), F32),
+            pltpu.VMEM((blk_dev, quarter, features), F32),
+            pltpu.SMEM((1, owners), jnp.int32),
         ),
-        (VMEM,) * 3,
-        (pltpu.VMEM((blk_dev, quarter, features), F32),),
         name="finish",
-        bytes_accessed=1024 * 1024,
     )(requests, self_term, *landed)
     pieces = [piece] + [swap(piece, "rep", replicas, k) for k in range(1, replicas)]
+    pieces[-1], feat_grad = lax.optimization_barrier((pieces[-1], feat_grad))
     whole = struct((features, features), F32)
     mine = call(
         gather_kernel,

time: 75.3 us -> 60.8 us (0.81)
  waiting for transfers between devices: 31.6 us -> 24.1 us
  Pallas kernels: 17.5 us -> 11.2 us
    pallas_call x7 -> x10, Pallas kernels: 17.5 us -> 11.2 us  [run(): pl.pallas_call(body, in_specs=in_specs, out_shape=out_shape, out_specs=ou...]
    all_to_all x1, waiting for transfers between devices: 11.3 us -> 6.99 us  [on_device(): lax.all_to_all(outgoing, 'blk', split_axis=0, concat_axis=0, tiled=True)]
    ppermute x11, waiting for transfers between devices: 20.3 us -> 17.1 us  [swap(): return lax.ppermute(array, axis, [(i, i ^ distance) for i in range(size)])]
    gather x1 -> x0, local copies, waits for them, and re-layouts: 2.62 us -> none  [on_device(): outgoing = feats.at[requests[0]].get(mode='promise_in_bounds')]
    unnamed x24 -> x20, local copies, waits for them, and re-layouts: 4.11 us -> 6.35 us
  transfers between devices with their start and end apart: 12 -> 12, of which waited for: 10 -> 9; matrix products, arithmetic and copies ran while one was open for 0% -> 0% of each run, Pallas kernels for 5% -> 7%
where the time goes in v2:
time: 60.8 us; the launch traced here: 60.3 us
  waiting for transfers between devices  24.1 us (40%)
  starting transfers between devices  18 us (30%)
  Pallas kernels  11.2 us (18%)
  local copies, waits for them, and re-layouts  6.35 us (10%)
  between operations  0.74 us (1%)
    ppermute x11, waiting for transfers between devices, swap(): return lax.ppermute(array, axis, [(i, i ^ distance) for i in range(size)])  17.1 us
    ppermute x11, starting transfers between devices, swap(): return lax.ppermute(array, axis, [(i, i ^ distance) for i in range(size)])  11.6 us
    pallas_call x10, Pallas kernels, run(): pl.pallas_call(body, in_specs=in_specs, out_shape=out_shape, out_specs=ou...  11.2 us
    all_to_all x1, waiting for transfers between devices, on_device(): lax.all_to_all(outgoing, 'blk', split_axis=0, concat_axis=0, tiled=True)  6.99 us
    unnamed x20, local copies, waits for them, and re-layouts  6.35 us
    all_to_all x1, starting transfers between devices, on_device(): lax.all_to_all(outgoing, 'blk', split_axis=0, concat_axis=0, tiled=True)  6.34 us
  transfers between devices with their start and end apart: 12, of which 9 were waited for; matrix products, arithmetic and copies ran while one was open for 0% of the time, Pallas kernels for 7%

profile of v2, /device:TPU:0, one launch (start us, length us, event | category | flops | bytes accessed | tf_op | source)
XLA Modules:
  0.0 60.3 jit_solution(12029674955925840564)
XLA Ops:
  0.6 2.6 %pick.1 = bf16[8,128,256]{2,1,0:T(8,128)(2,1)} custom-call(s32[1,8]{1,0:T(1,128)} %requests_in.3, bf16[16,128,256]{2,1,0:T(8,128)(2,1)} %refs_3_.1), custom_call_target="tpu_custom_call" | custom-call | bytes 1572896 | tf_op jit(solution)/shard_map/pick/pallas_call | solution.py:28
  3.3 6.3 %all-to-all-start = ((bf16[8,128,256]{2,1,0:T(8,128)(2,1)}), bf16[8,128,256]{2,1,0:T(8,128)(2,1)}, u32[]{:S(2)}, u32[]{:S(2)}) async-start(bf16[8,128,256]{2,1,0:T(8,128)(2,1)} %pick.1), calls=%async_computation | async-start | bytes 1048576 | tf_op jit(solution)/shard_map/all_to_all | solution.py:284
  9.6 1.2 %copy-done = bf16[16,128,256]{2,1,0:T(8,128)(2,1)S(1)} copy-done((bf16[16,128,256]{2,1,0:T(8,128)(2,1)S(1)}, bf16[16,128,256]{2,1,0:T(8,128)(2,1)}, u32[]{:S(2)}) %copy-start) | copy-done | bytes 1048600
  10.8 0.9 %copy-done.1 = bf16[256,256]{1,0:T(8,128)(2,1)S(1)} copy-done((bf16[256,256]{1,0:T(8,128)(2,1)S(1)}, bf16[256,256]{1,0:T(8,128)(2,1)}, u32[]{:S(2)}) %copy-start.1) | copy-done | bytes 131096
  11.7 1.0 %copy-done.3 = bf16[1,64,32,128]{3,2,1,0:T(8,128)(2,1)S(1)} copy-done((bf16[1,64,32,128]{3,2,1,0:T(8,128)(2,1)S(1)}, bf16[1,64,32,128]{3,2,1,0:T(8,128)(2,1)}, u32[]{:S(2)}) %copy-start.3) | copy-done | bytes 524312
  12.8 0.9 %copy-done.4 = bf16[16,32,256]{2,1,0:T(8,128)(2,1)S(1)} copy-done((bf16[16,32,256]{2,1,0:T(8,128)(2,1)S(1)}, bf16[16,32,256]{2,1,0:T(8,128)(2,1)}, u32[]{:S(2)}) %copy-start.4) | copy-done | bytes 262168
  13.7 0.9 %copy-done.5 = bf16[256,256]{1,0:T(8,128)(2,1)S(1)} copy-done((bf16[256,256]{1,0:T(8,128)(2,1)S(1)}, bf16[256,256]{1,0:T(8,128)(2,1)}, u32[]{:S(2)}) %copy-start.5) | copy-done | bytes 131096
  14.6 0.7 %copy-done.8 = s32[1,64]{1,0:T(1,128)S(1)} copy-done((s32[1,64]{1,0:T(1,128)S(1)}, s32[1,64]{1,0:T(1,128)}, u32[]{:S(2)}) %copy-start.8) | copy-done | bytes 280
  15.3 0.7 %copy-done.9 = s32[1,64]{1,0:T(1,128)S(1)} copy-done((s32[1,64]{1,0:T(1,128)S(1)}, s32[1,64]{1,0:T(1,128)}, u32[]{:S(2)}) %copy-start.9) | copy-done | bytes 280
  15.9 2.1 %prepare.1.refs_1_ = bf16[6,512,512]{2,1,0:T(8,128)(2,1)S(1)} custom-call(s32[1,64]{1,0:T(1,128)S(1)} %copy-done.8, s32[1,64]{1,0:T(1,128)S(1)} %copy-done.9, bf16[1,64,32,128]{3,2,1,0:T(8,128)(2,1)S(1)} %copy-done.3, bf16[16,128,256]{2,1,0:T(8,128)(2,1)S(1)} %copy-done, bf16[256,256]{1,0:T(8,128)(2,1)S(1)} %copy-done.1, bf16[256,256]{1,0:T(8,128)(2,1)S(1)} %copy-done.5, ...), custom_call_target="tpu_custom_call" | custom-call | bytes 5243392 | tf_op jit(solution)/shard_map/prepare/pallas_call | solution.py:28
  18.1 7.0 %all-to-all-done = bf16[8,128,256]{2,1,0:T(8,128)(2,1)} async-done(((bf16[8,128,256]{2,1,0:T(8,128)(2,1)}), bf16[8,128,256]{2,1,0:T(8,128)(2,1)}, u32[]{:S(2)}, u32[]{:S(2)}) %all-to-all-start) | async-done | bytes 524320 | tf_op jit(solution)/shard_map/all_to_all | solution.py:284
  25.1 2.6 %layer.1 = (f32[512,256]{1,0:T(8,128)S(1)}, bf16[512,256]{1,0:T(8,128)(2,1)S(1)}, bf16[400,256]{1,0:T(8,128)(2,1)S(1)}, bf16[400,256]{1,0:T(8,128)(2,1)S(1)}, bf...) custom-call(bf16[1024,256]{1,0:T(8,128)(2,1)} %bitcast.refs_0_, bf16[6,512,512]{2,1,0:T(8,128)(2,1)S(1)} %prepare.1.refs_1_, ...), custom_call_target="tpu_custom_call" | custom-call | flops 536870912 | bytes 5276672 | tf_op jit(solution)/shard_map/layer/pallas_call | solution.py:28
  27.7 2.5 %collective-permute-start.2 = (bf16[400,256]{1,0:T(8,128)(2,1)S(1)}, bf16[400,256]{1,0:T(8,128)(2,1)S(1)}, u32[]{:S(2)}, u32[]{:S(2)}) collective-permute-start(bf16[400,256]{1,0:T(8,128)(2,1)S(1)} %get-tuple-element.33), channel_id=1, source_target_pairs={{0,24},{8,16},{16,8},{24,0},{1,25},{9,17},{17,9},{25,1},{2,26},{10... | collective-permute-start | bytes 614408 | tf_op jit(solution)/shard_map/ppermute | solution.py:78
  30.2 0.5 collective-permute-start
  30.7 0.5 collective-permute-start.1
  31.3 1.0 %own.1 = (bf16[16,32,256]{2,1,0:T(8,128)(2,1)}, f32[512,256]{1,0:T(8,128)S(1)}) custom-call(f32[512,256]{1,0:T(8,128)S(1)} %get-tuple-element.27.preact, bf16[512,256]{1,0:T(8,128)(2,1)S(1)} %get-tuple-element.28.grad_pre, bf16[256,256]{1,0:T(8,128)(2,1)S(1)} %copy-done.2), custom_call_target="tpu_custom_call" | custom-call | flops 67108864 | bytes 1703936 | tf_op jit(solution)/shard_map/own/pallas_call | solution.py:28
  32.2 4.4 %collective-permute-done.2.refs_3_ = bf16[400,256]{1,0:T(8,128)(2,1)S(1)} collective-permute-done((bf16[400,256]{1,0:T(8,128)(2,1)S(1)}, bf16[400,256]{1,0:T(8,128)(2,1)S(1)}, u32[]{:S(2)}, u32[]{:S(2)}) %collective-permute-start.2) | collective-permute-done | bytes 204832 | tf_op jit(solution)/shard_map/ppermute | solution.py:78
  36.6 3.1 %collective-permute-done.refs_1_ = bf16[400,256]{1,0:T(8,128)(2,1)S(1)} collective-permute-done((bf16[400,256]{1,0:T(8,128)(2,1)S(1)}, bf16[400,256]{1,0:T(8,128)(2,1)S(1)}, u32[]{:S(2)}, u32[]{:S(2)}) %collective-permute-start) | collective-permute-done | bytes 204832 | tf_op jit(solution)/shard_map/ppermute | solution.py:78
  40.0 1.3 %collective-permute-done.3.refs_1_ = bf16[208,256]{1,0:T(8,128)(2,1)S(1)} collective-permute-done((bf16[208,256]{1,0:T(8,128)(2,1)S(1)}, bf16[208,256]{1,0:T(8,128)(2,1)S(1)}, u32[]{:S(2)}, u32[]{:S(2)}) %collective-permute-start.3) | collective-permute-done | bytes 106528 | tf_op jit(solution)/shard_map/ppermute | solution.py:78
  41.4 2.2 %collective-permute-start.5 = (bf16[144,256]{1,0:T(8,128)(2,1)S(1)}, bf16[144,256]{1,0:T(8,128)(2,1)S(1)}, u32[]{:S(2)}, u32[]{:S(2)}) collective-permute-start(bf16[144,256]{1,0:T(8,128)(2,1)S(1)} %get-tuple-element.40), channel_id=1, source_target_pairs={{0,4},{1,5},{2,6},{3,7},{4,0},{5,1},{6,2},{7,3},{8,12},{9,13},{10,... | collective-permute-start | bytes 221192 | tf_op jit(solution)/shard_map/ppermute | solution.py:78
  43.6 2.1 %collective-permute-start.6 = (bf16[144,256]{1,0:T(8,128)(2,1)S(1)}, bf16[144,256]{1,0:T(8,128)(2,1)S(1)}, u32[]{:S(2)}, u32[]{:S(2)}) collective-permute-start(bf16[144,256]{1,0:T(8,128)(2,1)S(1)} %get-tuple-element.41), channel_id=1, source_target_pairs={{0,6},{1,7},{2,4},{3,5},{4,2},{5,3},{6,0},{7,1},{8,14},{9,15},{10,... | collective-permute-start | bytes 221192 | tf_op jit(solution)/shard_map/ppermute | solution.py:78
  45.8 1.0 %collective-permute-done.4.refs_1_ = bf16[144,256]{1,0:T(8,128)(2,1)S(1)} collective-permute-done((bf16[144,256]{1,0:T(8,128)(2,1)S(1)}, bf16[144,256]{1,0:T(8,128)(2,1)S(1)}, u32[]{:S(2)}, u32[]{:S(2)}) %collective-permute-start.4) | collective-permute-done | bytes 73760 | tf_op jit(solution)/shard_map/ppermute | solution.py:78
  46.7 3.9 %collective-permute-done.5.refs_2_ = bf16[144,256]{1,0:T(8,128)(2,1)S(1)} collective-permute-done((bf16[144,256]{1,0:T(8,128)(2,1)S(1)}, bf16[144,256]{1,0:T(8,128)(2,1)S(1)}, u32[]{:S(2)}, u32[]{:S(2)}) %collective-permute-start.5) | collective-permute-done | bytes 73760 | tf_op jit(solution)/shard_map/ppermute | solution.py:78
  50.6 0.6 piece.1
  51.2 2.3 %collective-permute-start.9 = (bf16[64,256]{1,0:T(8,128)(2,1)S(1)}, bf16[64,256]{1,0:T(8,128)(2,1)S(1)}, u32[]{:S(2)}, u32[]{:S(2)}) collective-permute-start(bf16[64,256]{1,0:T(8,128)(2,1)S(1)} %get-tuple-element.42.refs_0_), channel_id=1, source_target_pairs={{0,24},{8,16},{16,8},{24,0},{1,25},{9,17},{17,9},{25,1},{2,26},{10... | collective-permute-start | bytes 98312 | tf_op jit(solution)/shard_map/ppermute | solution.py:78
  53.5 0.6 %collective-permute-start.8 = (bf16[64,256]{1,0:T(8,128)(2,1)S(1)}, bf16[64,256]{1,0:T(8,128)(2,1)S(1)}, u32[]{:S(2)}, u32[]{:S(2)}) collective-permute-start(bf16[64,256]{1,0:T(8,128)(2,1)S(1)} %get-tuple-element.42.refs_0_), channel_id=1, source_target_pairs={{0,16},{8,24},{16,0},{24,8},{1,17},{9,25},{17,1},{25,9},{2,18},{10... | collective-permute-start | bytes 98312 | tf_op jit(solution)/shard_map/ppermute | solution.py:78
  54.2 0.5 collective-permute-start.7
  54.7 1.3 %finish.1 = bf16[16,32,256]{2,1,0:T(8,128)(2,1)} custom-call(s32[1,8]{1,0:T(1,128)S(1)} %copy-done.6, f32[512,256]{1,0:T(8,128)S(1)} %get-tuple-element.43.self_term, bf16[144,256]{1,0:T(8,128)(2,1)S(1)} %get-tuple-element.38.refs_0_, bf16[144,256]{1,0:T(8,128)(2,1)S(1)} %collective-permute-done.4.refs_1_, ...), custom_call_target="tpu_custom_call" | custom-call | bytes 1081376 | tf_op jit(solution)/shard_map/finish/pallas_call | solution.py:28
  56.0 1.4 %collective-permute-done.8.refs_2_ = bf16[64,256]{1,0:T(8,128)(2,1)S(1)} collective-permute-done((bf16[64,256]{1,0:T(8,128)(2,1)S(1)}, bf16[64,256]{1,0:T(8,128)(2,1)S(1)}, u32[]{:S(2)}, u32[]{:S(2)}) %collective-permute-start.8) | collective-permute-done | bytes 32800 | tf_op jit(solution)/shard_map/ppermute | solution.py:78
  57.5 0.6 %collective-permute-done.7.refs_1_ = bf16[64,256]{1,0:T(8,128)(2,1)S(1)} collective-permute-done((bf16[64,256]{1,0:T(8,128)(2,1)S(1)}, bf16[64,256]{1,0:T(8,128)(2,1)S(1)}, u32[]{:S(2)}, u32[]{:S(2)}) %collective-permute-start.7) | collective-permute-done | bytes 32800 | tf_op jit(solution)/shard_map/ppermute | solution.py:78
  58.2 1.3 %collective-permute-done.10.other = bf16[256,256]{1,0:T(8,128)(2,1)S(1)} collective-permute-done((bf16[256,256]{1,0:T(8,128)(2,1)S(1)}, bf16[256,256]{1,0:T(8,128)(2,1)S(1)}, u32[]{:S(2)}, u32[]{:S(2)}) %collective-permute-start.10) | collective-permute-done | bytes 131104 | tf_op jit(solution)/shard_map/ppermute | solution.py:78
  59.5 0.8 %widen.1 = (f32[256,256]{1,0:T(8,128)}, f32[256,256]{1,0:T(8,128)}) custom-call(bf16[256,256]{1,0:T(8,128)(2,1)S(1)} %gather_pieces.1.mine, bf16[256,256]{1,0:T(8,128)(2,1)S(1)} %collective-permute-done.10.other), custom_call_target="tpu_custom_call" | custom-call | bytes 786432 | tf_op jit(solution)/shard_map/widen/pallas_call | solution.py:28
  (22 shorter events, 0.4 us)
Async XLA Ops:
  3.3 21.8 %copy-start.7 = (f32[256]{0:T(256)S(1)}, f32[256]{0:T(256)}, u32[]{:S(2)}) copy-start(f32[256]{0:T(256)} %param.16) | copy-start | bytes 3076
  3.3 21.8 %all-to-all-start = ((bf16[8,128,256]{2,1,0:T(8,128)(2,1)}), bf16[8,128,256]{2,1,0:T(8,128)(2,1)}, u32[]{:S(2)}, u32[]{:S(2)}) async-start(bf16[8,128,256]{2,1,0:T(8,128)(2,1)} %pick.1), calls=%async_computation | async-start | bytes 1048576 | tf_op jit(solution)/shard_map/all_to_all | solution.py:284
  9.6 1.2 %copy-start = (bf16[16,128,256]{2,1,0:T(8,128)(2,1)S(1)}, bf16[16,128,256]{2,1,0:T(8,128)(2,1)}, u32[]{:S(2)}) copy-start(bf16[16,128,256]{2,1,0:T(8,128)(2,1)} %refs_3_.1) | copy-start | bytes 3145732
  10.8 0.9 %copy-start.1 = (bf16[256,256]{1,0:T(8,128)(2,1)S(1)}, bf16[256,256]{1,0:T(8,128)(2,1)}, u32[]{:S(2)}) copy-start(bf16[256,256]{1,0:T(8,128)(2,1)} %w_self.1) | copy-start | bytes 393220
  11.7 1.0 %copy-start.3 = (bf16[1,64,32,128]{3,2,1,0:T(8,128)(2,1)S(1)}, bf16[1,64,32,128]{3,2,1,0:T(8,128)(2,1)}, u32[]{:S(2)}) copy-start(bf16[1,64,32,128]{3,2,1,0:T(8,128)(2,1)} %refs_2_.1) | copy-start | bytes 1572868
  12.8 0.9 %copy-start.4 = (bf16[16,32,256]{2,1,0:T(8,128)(2,1)S(1)}, bf16[16,32,256]{2,1,0:T(8,128)(2,1)}, u32[]{:S(2)}) copy-start(bf16[16,32,256]{2,1,0:T(8,128)(2,1)} %refs_6_.1) | copy-start | bytes 786436
  13.7 0.9 %copy-start.5 = (bf16[256,256]{1,0:T(8,128)(2,1)S(1)}, bf16[256,256]{1,0:T(8,128)(2,1)}, u32[]{:S(2)}) copy-start(bf16[256,256]{1,0:T(8,128)(2,1)} %refs_5_.1) | copy-start | bytes 393220
  14.6 0.7 %copy-start.8 = (s32[1,64]{1,0:T(1,128)S(1)}, s32[1,64]{1,0:T(1,128)}, u32[]{:S(2)}) copy-start(s32[1,64]{1,0:T(1,128)} %refs_0_.1) | copy-start | bytes 772
  15.3 0.7 %copy-start.9 = (s32[1,64]{1,0:T(1,128)S(1)}, s32[1,64]{1,0:T(1,128)}, u32[]{:S(2)}) copy-start(s32[1,64]{1,0:T(1,128)} %refs_1_.1) | copy-start | bytes 772
  18.0 13.2 %copy-start.2 = (bf16[256,256]{1,0:T(8,128)(2,1)S(1)}, bf16[256,256]{1,0:T(8,128)(2,1)}, u32[]{:S(2)}) copy-start(bf16[256,256]{1,0:T(8,128)(2,1)} %w_self.1) | copy-start | bytes 393220
  18.1 36.6 %copy-start.6 = (s32[1,8]{1,0:T(1,128)S(1)}, s32[1,8]{1,0:T(1,128)}, u32[]{:S(2)}) copy-start(s32[1,8]{1,0:T(1,128)} %requests_in.3) | copy-start | bytes 100
  27.7 9.0 %collective-permute-start.2 = (bf16[400,256]{1,0:T(8,128)(2,1)S(1)}, bf16[400,256]{1,0:T(8,128)(2,1)S(1)}, u32[]{:S(2)}, u32[]{:S(2)}) collective-permute-start(bf16[400,256]{1,0:T(8,128)(2,1)S(1)} %get-tuple-element.33), channel_id=1, source_target_pairs={{0,24},{8,16},{16,8},{24,0},{1,25},{9,17},{17,9},{25,1},{2,26},{10... | collective-permute-start | bytes 614408 | tf_op jit(solution)/shard_map/ppermute | solution.py:78
  30.2 9.6 %collective-permute-start = (bf16[400,256]{1,0:T(8,128)(2,1)S(1)}, bf16[400,256]{1,0:T(8,128)(2,1)S(1)}, u32[]{:S(2)}, u32[]{:S(2)}) collective-permute-start(bf16[400,256]{1,0:T(8,128)(2,1)S(1)} %get-tuple-element.31), channel_id=1, source_target_pairs={{0,8},{8,0},{16,24},{24,16},{1,9},{9,1},{17,25},{25,17},{2,10},{10... | collective-permute-start | bytes 614408 | tf_op jit(solution)/shard_map/ppermute | solution.py:78
  30.7 9.0 %collective-permute-start.1 = (bf16[400,256]{1,0:T(8,128)(2,1)S(1)}, bf16[400,256]{1,0:T(8,128)(2,1)S(1)}, u32[]{:S(2)}, u32[]{:S(2)}) collective-permute-start(bf16[400,256]{1,0:T(8,128)(2,1)S(1)} %get-tuple-element.32), channel_id=1, source_target_pairs={{0,16},{8,24},{16,0},{24,8},{1,17},{9,25},{17,1},{25,9},{2,18},{10... | collective-permute-start | bytes 614408 | tf_op jit(solution)/shard_map/ppermute | solution.py:78
  39.9 1.4 %collective-permute-start.3 = (bf16[208,256]{1,0:T(8,128)(2,1)S(1)}, bf16[208,256]{1,0:T(8,128)(2,1)S(1)}, u32[]{:S(2)}, u32[]{:S(2)}) collective-permute-start(bf16[208,256]{1,0:T(8,128)(2,1)S(1)} %get-tuple-element.37), channel_id=1, source_target_pairs={{0,1},{1,0},{2,3},{3,2},{4,5},{5,4},{6,7},{7,6},{8,9},{9,8},{10,11... | collective-permute-start | bytes 319496 | tf_op jit(solution)/shard_map/ppermute | solution.py:78
  41.3 5.4 %collective-permute-start.4 = (bf16[144,256]{1,0:T(8,128)(2,1)S(1)}, bf16[144,256]{1,0:T(8,128)(2,1)S(1)}, u32[]{:S(2)}, u32[]{:S(2)}) collective-permute-start(bf16[144,256]{1,0:T(8,128)(2,1)S(1)} %get-tuple-element.39), channel_id=1, source_target_pairs={{0,2},{1,3},{2,0},{3,1},{4,6},{5,7},{6,4},{7,5},{8,10},{9,11},{10,... | collective-permute-start | bytes 221192 | tf_op jit(solution)/shard_map/ppermute | solution.py:78
  41.4 9.2 %collective-permute-start.5 = (bf16[144,256]{1,0:T(8,128)(2,1)S(1)}, bf16[144,256]{1,0:T(8,128)(2,1)S(1)}, u32[]{:S(2)}, u32[]{:S(2)}) collective-permute-start(bf16[144,256]{1,0:T(8,128)(2,1)S(1)} %get-tuple-element.40), channel_id=1, source_target_pairs={{0,4},{1,5},{2,6},{3,7},{4,0},{5,1},{6,2},{7,3},{8,12},{9,13},{10,... | collective-permute-start | bytes 221192 | tf_op jit(solution)/shard_map/ppermute | solution.py:78
  43.6 7.0 %collective-permute-start.6 = (bf16[144,256]{1,0:T(8,128)(2,1)S(1)}, bf16[144,256]{1,0:T(8,128)(2,1)S(1)}, u32[]{:S(2)}, u32[]{:S(2)}) collective-permute-start(bf16[144,256]{1,0:T(8,128)(2,1)S(1)} %get-tuple-element.41), channel_id=1, source_target_pairs={{0,6},{1,7},{2,4},{3,5},{4,2},{5,3},{6,0},{7,1},{8,14},{9,15},{10,... | collective-permute-start | bytes 221192 | tf_op jit(solution)/shard_map/ppermute | solution.py:78
  51.2 4.8 %collective-permute-start.9 = (bf16[64,256]{1,0:T(8,128)(2,1)S(1)}, bf16[64,256]{1,0:T(8,128)(2,1)S(1)}, u32[]{:S(2)}, u32[]{:S(2)}) collective-permute-start(bf16[64,256]{1,0:T(8,128)(2,1)S(1)} %get-tuple-element.42.refs_0_), channel_id=1, source_target_pairs={{0,24},{8,16},{16,8},{24,0},{1,25},{9,17},{17,9},{25,1},{2,26},{10... | collective-permute-start | bytes 98312 | tf_op jit(solution)/shard_map/ppermute | solution.py:78
  53.5 3.9 %collective-permute-start.8 = (bf16[64,256]{1,0:T(8,128)(2,1)S(1)}, bf16[64,256]{1,0:T(8,128)(2,1)S(1)}, u32[]{:S(2)}, u32[]{:S(2)}) collective-permute-start(bf16[64,256]{1,0:T(8,128)(2,1)S(1)} %get-tuple-element.42.refs_0_), channel_id=1, source_target_pairs={{0,16},{8,24},{16,0},{24,8},{1,17},{9,25},{17,1},{25,9},{2,18},{10... | collective-permute-start | bytes 98312 | tf_op jit(solution)/shard_map/ppermute | solution.py:78
  54.2 3.9 %collective-permute-start.7 = (bf16[64,256]{1,0:T(8,128)(2,1)S(1)}, bf16[64,256]{1,0:T(8,128)(2,1)S(1)}, u32[]{:S(2)}, u32[]{:S(2)}) collective-permute-start(bf16[64,256]{1,0:T(8,128)(2,1)S(1)} %get-tuple-element.42.refs_0_), channel_id=1, source_target_pairs={{0,8},{8,0},{16,24},{24,16},{1,9},{9,1},{17,25},{25,17},{2,10},{10... | collective-permute-start | bytes 98312 | tf_op jit(solution)/shard_map/ppermute | solution.py:78
  58.1 1.4 %collective-permute-start.10 = (bf16[256,256]{1,0:T(8,128)(2,1)S(1)}, bf16[256,256]{1,0:T(8,128)(2,1)S(1)}, u32[]{:S(2)}, u32[]{:S(2)}) collective-permute-start(bf16[256,256]{1,0:T(8,128)(2,1)S(1)} %gather_pieces.1.mine), channel_id=1, source_target_pairs={{0,1},{1,0},{2,3},{3,2},{4,5},{5,4},{6,7},{7,6},{8,9},{9,8},{10,11... | collective-permute-start | bytes 393224 | tf_op jit(solution)/shard_map/ppermute | solution.py:78

commit v3 on v2

--- a/solution.py
+++ b/solution.py
@@ -78,15 +78,19 @@
     return lax.ppermute(array, axis, [(i, i ^ distance) for i in range(size)])
 
 
-def pick_kernel(requests_in, feats, out, requests, sems):
+def pick_kernel(requests_in, feats, out, held, requests, sems):
+    count = out.shape[0]
+    into = pltpu.make_async_copy(feats, held, sems.at[0])
+    into.start()
     pltpu.sync_copy(requests_in, requests)
-    copies = [
-        pltpu.make_async_copy(feats.at[requests[0, reader]], out.at[reader], sems.at[reader])
-        for reader in range(out.shape[0])
+    into.wait()
+    away = [
+        pltpu.make_async_copy(held.at[requests[0, i]], out.at[i], sems.at[1 + i])
+        for i in range(count)
     ]
-    for copy in copies:
+    for copy in away:
         copy.start()
-    for copy in copies:
+    for copy in away:
         copy.wait()
 
 
@@ -126,9 +130,9 @@
     packed[2 * slabs + 1, features:, features:] = w_neigh[...]
 
 
-def layer_kernel(grad_scale, owners, replicas, sources, packed, bias, *refs):
+def layer_kernel(grad_scale, owners, replicas, sources_in, packed, bias, *refs):
     preact_out, grad_pre_out, messages = refs[0], refs[1], refs[2 : 2 + replicas]
-    contributions, gradients = refs[2 + replicas :]
+    contributions, gradients, sources, sems = refs[2 + replicas :]
     row_count, features = preact_out.shape
     width = contributions.shape[1]
     quarter = width // replicas
@@ -142,16 +146,27 @@
     rows_t = packed[2 * slabs + 1, :features]
     w_self = packed[2 * slabs + 1, features:, :features]
     w_neigh = packed[2 * slabs + 1, features:, features:]
-    agg = dot(packed[0], sources[:row_count])
-    if slabs <= 4:
-        for slab in range(1, slabs):
-            agg += dot(packed[slab], sources[slab * row_count : (slab + 1) * row_count])
-    else:
-        agg = lax.fori_loop(
-            1, slabs, lambda i, a: a + dot(packed[i], sources[aligned(i, row_count), :]), agg
-        )
-    agg = agg.astype(BF16)
-    preact = dot(rows, w_self) + dot(agg, w_neigh) + bias[...]
+
+    def fetch(slab):
+        place = aligned(slab, row_count)
+        return pltpu.make_async_copy(sources_in.at[place, :], sources.at[place, :], sems.at[slab])
+
+    for slab in range(slabs):
+        fetch(slab).start()
+    preact = dot(rows, w_self) + bias[...]
+    for slab in range(slabs):
+        fetch(slab).wait()
+    half = row_count // 2
+
+    def gather_rows(part):
+        def add(slab, total):
+            return total + dot(packed[slab, part], sources[aligned(slab, row_count), :])
+
+        total = dot(packed[0, part], sources[:row_count])
+        return lax.fori_loop(1, slabs, add, total, unroll=slabs <= 4).astype(BF16)
+
+    agg = jnp.concatenate([gather_rows(slice(0, half)), gather_rows(slice(half, row_count))])
+    preact += dot(agg, w_neigh)
     preact_out[...] = preact
     gating = jax.nn.sigmoid(preact)
     grad_pre = (
@@ -225,16 +240,16 @@
 
 
 def piece_kernel(*refs):
-    arrived, (piece, grad_bias) = refs[:-2], refs[-2:]
+    arrived, piece = refs[:-1], refs[-1]
     share = piece.shape[0]
     base = arrived[0].shape[0] - PAD - share
     piece[...] = butterfly_sum([a[base : base + share].astype(F32) for a in arrived]).astype(BF16)
-    grad_bias[...] = butterfly_sum([join_rows(a[base + share :]) for a in arrived])
 
 
 def finish_kernel(requests_in, self_term, *refs):
-    arrived, (feat_grad, total, requests) = refs[:-3], refs[-3:]
+    arrived, (feat_grad, grad_bias, total, requests) = refs[:-4], refs[-4:]
     pltpu.sync_copy(requests_in, requests)
+    grad_bias[...] = butterfly_sum([join_rows(a[a.shape[0] - PAD :]) for a in arrived])
     quarter = total.shape[1]
     blk = lax.axis_index("blk")
     total[...] = self_term[...].reshape(total.shape)
@@ -276,8 +291,12 @@
         pick_kernel,
         [HBM, HBM],
         struct((owners, width, features), BF16),
-        VMEM,
-        (pltpu.SMEM((1, owners), jnp.int32), pltpu.SemaphoreType.DMA((owners,))),
+        HBM,
+        (
+            pltpu.VMEM(feats.shape, BF16),
+            pltpu.SMEM((1, owners), jnp.int32),
+            pltpu.SemaphoreType.DMA((1 + owners,)),
+        ),
         name="pick",
         limit=56 * MIB,
     )(requests, feats)
@@ -295,13 +314,15 @@
     message_rows = owners * quarter + 2 * share + PAD
     outs = call(
         lambda *refs: layer_kernel(grad_scale, owners, replicas, *refs),
-        [VMEM] * 3,
+        [HBM, VMEM, VMEM],
         (struct((row_count, features), F32), struct((row_count, features), BF16))
         + (struct((message_rows, features), BF16),) * replicas,
         (VMEM,) * (2 + replicas),
         (
             pltpu.VMEM((owners, width, features), BF16),
             pltpu.VMEM((2, features, features), BF16),
+            pltpu.VMEM((owners * width, features), BF16),
+            pltpu.SemaphoreType.DMA((owners // per_slab,)),
         ),
         name="layer",
         flops=4 * row_count * features * owners * width,
@@ -336,18 +357,15 @@
         name="core_join",
     )(keep, got)
     landed = [parcels[0]] + [swap(parcels[k], "blk", owners, 2 * k) for k in range(1, zs)]
-    piece, grad_bias = call(
-        piece_kernel,
-        [VMEM] * zs,
-        (struct((share, features), BF16), struct((1, features), F32)),
-        (VMEM, VMEM),
-        name="piece",
+    landed[-1], hidden = lax.optimization_barrier((landed[-1], hidden))
+    piece = call(
+        piece_kernel, [VMEM] * zs, struct((share, features), BF16), VMEM, name="piece"
     )(*landed)
-    feat_grad = call(
+    feat_grad, grad_bias = call(
         finish_kernel,
         [HBM, VMEM] + [VMEM] * zs,
-        struct((blk_dev, quarter, features), BF16),
-        VMEM,
+        (struct((blk_dev, quarter, features), BF16), struct((1, features), F32)),
+        (VMEM, VMEM),
         (
             pltpu.VMEM((blk_dev, quarter, features), F32),
             pltpu.SMEM((1, owners), jnp.int32),
@@ -355,7 +373,6 @@
         name="finish",
     )(requests, self_term, *landed)
     pieces = [piece] + [swap(piece, "rep", replicas, k) for k in range(1, replicas)]
-    pieces[-1], feat_grad = lax.optimization_barrier((pieces[-1], feat_grad))
     whole = struct((features, features), F32)
     mine = call(
         gather_kernel,
@@ -365,6 +382,7 @@
         name="gather_pieces",
     )(*pieces)
     other = swap(mine, "blk", owners, 1)
+    other, feat_grad = lax.optimization_barrier((other, feat_grad))
     grad_self, grad_neigh = call(
         widen_kernel, [VMEM, VMEM], (whole, whole), (VMEM, VMEM), name="widen"
     )(mine, other)

time: 60.8 us -> 59.6 us (0.980)
  Pallas kernels: 11.2 us -> 9.88 us
    pallas_call x10, Pallas kernels: 11.2 us -> 9.88 us  [run(): pl.pallas_call(body, in_specs=in_specs, out_shape=out_shape, out_specs=ou...]
  transfers between devices with their start and end apart: 12 -> 12, of which waited for: 9 -> 10; matrix products, arithmetic and copies ran while one was open for 0% -> 0% of each run, Pallas kernels for 7% -> 7%
where the time goes in v3:
time: 59.6 us; the launch traced here: 59.2 us
  waiting for transfers between devices  24.2 us (41%)
  starting transfers between devices  18 us (30%)
  Pallas kernels  9.88 us (17%)
  local copies, waits for them, and re-layouts  6.35 us (11%)
  between operations  0.74 us (1%)
    ppermute x11, waiting for transfers between devices, swap(): return lax.ppermute(array, axis, [(i, i ^ distance) for i in range(size)])  17.2 us
    ppermute x11, starting transfers between devices, swap(): return lax.ppermute(array, axis, [(i, i ^ distance) for i in range(size)])  11.7 us
    pallas_call x10, Pallas kernels, run(): pl.pallas_call(body, in_specs=in_specs, out_shape=out_shape, out_specs=ou...  9.88 us
    all_to_all x1, waiting for transfers between devices, on_device(): lax.all_to_all(outgoing, 'blk', split_axis=0, concat_axis=0, tiled=True)  7 us
    unnamed x20, local copies, waits for them, and re-layouts  6.35 us
    all_to_all x1, starting transfers between devices, on_device(): lax.all_to_all(outgoing, 'blk', split_axis=0, concat_axis=0, tiled=True)  6.34 us
  transfers between devices with their start and end apart: 12, of which 10 were waited for; matrix products, arithmetic and copies ran while one was open for 0% of the time, Pallas kernels for 7%

profile of v3, /device:TPU:0, one launch (start us, length us, event | category | flops | bytes accessed | tf_op | source)
XLA Modules:
  0.0 59.2 jit_solution(1067012914317485600)
XLA Ops:
  0.6 2.1 %pick.1 = bf16[8,128,256]{2,1,0:T(8,128)(2,1)} custom-call(s32[1,8]{1,0:T(1,128)} %requests_in.3, bf16[16,128,256]{2,1,0:T(8,128)(2,1)} %refs_3_.1), custom_call_target="tpu_custom_call" | custom-call | bytes 1572896 | tf_op jit(solution)/shard_map/pick/pallas_call | solution.py:28
  2.8 6.3 %all-to-all-start = ((bf16[8,128,256]{2,1,0:T(8,128)(2,1)}), bf16[8,128,256]{2,1,0:T(8,128)(2,1)}, u32[]{:S(2)}, u32[]{:S(2)}) async-start(bf16[8,128,256]{2,1,0:T(8,128)(2,1)} %pick.1), calls=%async_computation | async-start | bytes 1048576 | tf_op jit(solution)/shard_map/all_to_all | solution.py:303
  9.1 1.2 %copy-done = bf16[16,128,256]{2,1,0:T(8,128)(2,1)S(1)} copy-done((bf16[16,128,256]{2,1,0:T(8,128)(2,1)S(1)}, bf16[16,128,256]{2,1,0:T(8,128)(2,1)}, u32[]{:S(2)}) %copy-start) | copy-done | bytes 1048600
  10.3 0.9 %copy-done.1 = bf16[256,256]{1,0:T(8,128)(2,1)S(1)} copy-done((bf16[256,256]{1,0:T(8,128)(2,1)S(1)}, bf16[256,256]{1,0:T(8,128)(2,1)}, u32[]{:S(2)}) %copy-start.1) | copy-done | bytes 131096
  11.2 1.0 %copy-done.3 = bf16[1,64,32,128]{3,2,1,0:T(8,128)(2,1)S(1)} copy-done((bf16[1,64,32,128]{3,2,1,0:T(8,128)(2,1)S(1)}, bf16[1,64,32,128]{3,2,1,0:T(8,128)(2,1)}, u32[]{:S(2)}) %copy-start.3) | copy-done | bytes 524312
  12.3 0.9 %copy-done.4 = bf16[16,32,256]{2,1,0:T(8,128)(2,1)S(1)} copy-done((bf16[16,32,256]{2,1,0:T(8,128)(2,1)S(1)}, bf16[16,32,256]{2,1,0:T(8,128)(2,1)}, u32[]{:S(2)}) %copy-start.4) | copy-done | bytes 262168
  13.2 0.9 %copy-done.5 = bf16[256,256]{1,0:T(8,128)(2,1)S(1)} copy-done((bf16[256,256]{1,0:T(8,128)(2,1)S(1)}, bf16[256,256]{1,0:T(8,128)(2,1)}, u32[]{:S(2)}) %copy-start.5) | copy-done | bytes 131096
  14.1 0.7 %copy-done.8 = s32[1,64]{1,0:T(1,128)S(1)} copy-done((s32[1,64]{1,0:T(1,128)S(1)}, s32[1,64]{1,0:T(1,128)}, u32[]{:S(2)}) %copy-start.8) | copy-done | bytes 280
  14.8 0.7 %copy-done.9 = s32[1,64]{1,0:T(1,128)S(1)} copy-done((s32[1,64]{1,0:T(1,128)S(1)}, s32[1,64]{1,0:T(1,128)}, u32[]{:S(2)}) %copy-start.9) | copy-done | bytes 280
  15.4 2.1 %prepare.1.refs_1_ = bf16[6,512,512]{2,1,0:T(8,128)(2,1)S(1)} custom-call(s32[1,64]{1,0:T(1,128)S(1)} %copy-done.8, s32[1,64]{1,0:T(1,128)S(1)} %copy-done.9, bf16[1,64,32,128]{3,2,1,0:T(8,128)(2,1)S(1)} %copy-done.3, bf16[16,128,256]{2,1,0:T(8,128)(2,1)S(1)} %copy-done, bf16[256,256]{1,0:T(8,128)(2,1)S(1)} %copy-done.1, bf16[256,256]{1,0:T(8,128)(2,1)S(1)} %copy-done.5, ...), custom_call_target="tpu_custom_call" | custom-call | bytes 5243392 | tf_op jit(solution)/shard_map/prepare/pallas_call | solution.py:28
  17.6 7.0 %all-to-all-done = bf16[8,128,256]{2,1,0:T(8,128)(2,1)} async-done(((bf16[8,128,256]{2,1,0:T(8,128)(2,1)}), bf16[8,128,256]{2,1,0:T(8,128)(2,1)}, u32[]{:S(2)}, u32[]{:S(2)}) %all-to-all-start) | async-done | bytes 524320 | tf_op jit(solution)/shard_map/all_to_all | solution.py:303
  24.6 2.3 %layer.1 = (f32[512,256]{1,0:T(8,128)S(1)}, bf16[512,256]{1,0:T(8,128)(2,1)S(1)}, bf16[400,256]{1,0:T(8,128)(2,1)S(1)}, bf16[400,256]{1,0:T(8,128)(2,1)S(1)}, bf...) custom-call(bf16[1024,256]{1,0:T(8,128)(2,1)} %bitcast.refs_0_, bf16[6,512,512]{2,1,0:T(8,128)(2,1)S(1)} %prepare.1.refs_1_, ...), custom_call_target="tpu_custom_call" | custom-call | flops 536870912 | bytes 5276672 | tf_op jit(solution)/shard_map/layer/pallas_call | solution.py:28
  26.9 2.5 %collective-permute-start.2 = (bf16[400,256]{1,0:T(8,128)(2,1)S(1)}, bf16[400,256]{1,0:T(8,128)(2,1)S(1)}, u32[]{:S(2)}, u32[]{:S(2)}) collective-permute-start(bf16[400,256]{1,0:T(8,128)(2,1)S(1)} %get-tuple-element.32), channel_id=1, source_target_pairs={{0,24},{8,16},{16,8},{24,0},{1,25},{9,17},{17,9},{25,1},{2,26},{10... | collective-permute-start | bytes 614408 | tf_op jit(solution)/shard_map/ppermute | solution.py:78
  29.4 0.5 collective-permute-start
  30.0 0.5 collective-permute-start.1
  30.5 1.0 %own.1 = (bf16[16,32,256]{2,1,0:T(8,128)(2,1)}, f32[512,256]{1,0:T(8,128)S(1)}) custom-call(f32[512,256]{1,0:T(8,128)S(1)} %get-tuple-element.33.preact, bf16[512,256]{1,0:T(8,128)(2,1)S(1)} %get-tuple-element.34.grad_pre, bf16[256,256]{1,0:T(8,128)(2,1)S(1)} %copy-done.2), custom_call_target="tpu_custom_call" | custom-call | flops 67108864 | bytes 1703936 | tf_op jit(solution)/shard_map/own/pallas_call | solution.py:28
  31.5 4.4 %collective-permute-done.2.refs_3_ = bf16[400,256]{1,0:T(8,128)(2,1)S(1)} collective-permute-done((bf16[400,256]{1,0:T(8,128)(2,1)S(1)}, bf16[400,256]{1,0:T(8,128)(2,1)S(1)}, u32[]{:S(2)}, u32[]{:S(2)}) %collective-permute-start.2) | collective-permute-done | bytes 204832 | tf_op jit(solution)/shard_map/ppermute | solution.py:78
  35.9 3.1 %collective-permute-done.refs_1_ = bf16[400,256]{1,0:T(8,128)(2,1)S(1)} collective-permute-done((bf16[400,256]{1,0:T(8,128)(2,1)S(1)}, bf16[400,256]{1,0:T(8,128)(2,1)S(1)}, u32[]{:S(2)}, u32[]{:S(2)}) %collective-permute-start) | collective-permute-done | bytes 204832 | tf_op jit(solution)/shard_map/ppermute | solution.py:78
  39.2 1.3 %collective-permute-done.3.refs_1_ = bf16[208,256]{1,0:T(8,128)(2,1)S(1)} collective-permute-done((bf16[208,256]{1,0:T(8,128)(2,1)S(1)}, bf16[208,256]{1,0:T(8,128)(2,1)S(1)}, u32[]{:S(2)}, u32[]{:S(2)}) %collective-permute-start.3) | collective-permute-done | bytes 106528 | tf_op jit(solution)/shard_map/ppermute | solution.py:78
  40.5 1.8 %collective-permute-start.4 = (bf16[144,256]{1,0:T(8,128)(2,1)S(1)}, bf16[144,256]{1,0:T(8,128)(2,1)S(1)}, u32[]{:S(2)}, u32[]{:S(2)}) collective-permute-start(bf16[144,256]{1,0:T(8,128)(2,1)S(1)} %get-tuple-element.39), channel_id=1, source_target_pairs={{0,6},{1,7},{2,4},{3,5},{4,2},{5,3},{6,0},{7,1},{8,14},{9,15},{10,... | collective-permute-start | bytes 221192 | tf_op jit(solution)/shard_map/ppermute | solution.py:78
  42.3 2.7 %collective-permute-start.6 = (bf16[144,256]{1,0:T(8,128)(2,1)S(1)}, bf16[144,256]{1,0:T(8,128)(2,1)S(1)}, u32[]{:S(2)}, u32[]{:S(2)}) collective-permute-start(bf16[144,256]{1,0:T(8,128)(2,1)S(1)} %get-tuple-element.44), channel_id=1, source_target_pairs={{0,4},{1,5},{2,6},{3,7},{4,0},{5,1},{6,2},{7,3},{8,12},{9,13},{10,... | collective-permute-start | bytes 221192 | tf_op jit(solution)/shard_map/ppermute | solution.py:78
  45.0 2.6 %collective-permute-done.4.refs_3_ = bf16[144,256]{1,0:T(8,128)(2,1)S(1)} collective-permute-done((bf16[144,256]{1,0:T(8,128)(2,1)S(1)}, bf16[144,256]{1,0:T(8,128)(2,1)S(1)}, u32[]{:S(2)}, u32[]{:S(2)}) %collective-permute-start.4) | collective-permute-done | bytes 73760 | tf_op jit(solution)/shard_map/ppermute | solution.py:78
  47.6 1.9 %collective-permute-done.5.refs_1_ = bf16[144,256]{1,0:T(8,128)(2,1)S(1)} collective-permute-done((bf16[144,256]{1,0:T(8,128)(2,1)S(1)}, bf16[144,256]{1,0:T(8,128)(2,1)S(1)}, u32[]{:S(2)}, u32[]{:S(2)}) %collective-permute-start.5) | collective-permute-done | bytes 73760 | tf_op jit(solution)/shard_map/ppermute | solution.py:78
  49.5 0.5 collective-permute-done.6.refs_2_
  50.0 2.4 %collective-permute-start.9 = (bf16[64,256]{1,0:T(8,128)(2,1)S(1)}, bf16[64,256]{1,0:T(8,128)(2,1)S(1)}, u32[]{:S(2)}, u32[]{:S(2)}) collective-permute-start(bf16[64,256]{1,0:T(8,128)(2,1)S(1)} %piece.1.refs_0_), channel_id=1, source_target_pairs={{0,24},{8,16},{16,8},{24,0},{1,25},{9,17},{17,9},{25,1},{2,26},{10... | collective-permute-start | bytes 98312 | tf_op jit(solution)/shard_map/ppermute | solution.py:78
  52.4 0.6 %collective-permute-start.8 = (bf16[64,256]{1,0:T(8,128)(2,1)S(1)}, bf16[64,256]{1,0:T(8,128)(2,1)S(1)}, u32[]{:S(2)}, u32[]{:S(2)}) collective-permute-start(bf16[64,256]{1,0:T(8,128)(2,1)S(1)} %piece.1.refs_0_), channel_id=1, source_target_pairs={{0,16},{8,24},{16,0},{24,8},{1,17},{9,25},{17,1},{25,9},{2,18},{10... | collective-permute-start | bytes 98312 | tf_op jit(solution)/shard_map/ppermute | solution.py:78
  53.0 0.5 collective-permute-start.7
  53.5 1.3 %collective-permute-done.9.refs_3_ = bf16[64,256]{1,0:T(8,128)(2,1)S(1)} collective-permute-done((bf16[64,256]{1,0:T(8,128)(2,1)S(1)}, bf16[64,256]{1,0:T(8,128)(2,1)S(1)}, u32[]{:S(2)}, u32[]{:S(2)}) %collective-permute-start.9) | collective-permute-done | bytes 32800 | tf_op jit(solution)/shard_map/ppermute | solution.py:78
  54.8 1.4 %collective-permute-done.8.refs_2_ = bf16[64,256]{1,0:T(8,128)(2,1)S(1)} collective-permute-done((bf16[64,256]{1,0:T(8,128)(2,1)S(1)}, bf16[64,256]{1,0:T(8,128)(2,1)S(1)}, u32[]{:S(2)}, u32[]{:S(2)}) %collective-permute-start.8) | collective-permute-done | bytes 32800 | tf_op jit(solution)/shard_map/ppermute | solution.py:78
  56.3 0.6 %collective-permute-done.7.refs_1_ = bf16[64,256]{1,0:T(8,128)(2,1)S(1)} collective-permute-done((bf16[64,256]{1,0:T(8,128)(2,1)S(1)}, bf16[64,256]{1,0:T(8,128)(2,1)S(1)}, u32[]{:S(2)}, u32[]{:S(2)}) %collective-permute-start.7) | collective-permute-done | bytes 32800 | tf_op jit(solution)/shard_map/ppermute | solution.py:78
  57.0 1.3 %finish.1 = (bf16[16,32,256]{2,1,0:T(8,128)(2,1)}, f32[1,256]{1,0:T(1,128)}) custom-call(s32[1,8]{1,0:T(1,128)S(1)} %copy-done.6, f32[512,256]{1,0:T(8,128)S(1)} %get-tuple-element.46.self_term, bf16[144,256]{1,0:T(8,128)(2,1)S(1)} %get-tuple-element.42.refs_0_, bf16[144,256]{1,0:T(8,128)(2,1)S(1)} %collective-permute-done.5.refs_1_, ...), custom_call_target="tpu_custom_call" | custom-call | bytes 1082400 | tf_op jit(solution)/shard_map/finish/pallas_call | solution.py:28
  58.3 0.8 %widen.1 = (f32[256,256]{1,0:T(8,128)}, f32[256,256]{1,0:T(8,128)}) custom-call(bf16[256,256]{1,0:T(8,128)(2,1)S(1)} %gather_pieces.1.mine, bf16[256,256]{1,0:T(8,128)(2,1)S(1)} %collective-permute-done.10.other), custom_call_target="tpu_custom_call" | custom-call | bytes 786432 | tf_op jit(solution)/shard_map/widen/pallas_call | solution.py:28
  (22 shorter events, 0.4 us)
Async XLA Ops:
  2.8 21.8 %copy-start.7 = (f32[256]{0:T(256)S(1)}, f32[256]{0:T(256)}, u32[]{:S(2)}) copy-start(f32[256]{0:T(256)} %param.16) | copy-start | bytes 3076
  2.8 21.8 %all-to-all-start = ((bf16[8,128,256]{2,1,0:T(8,128)(2,1)}), bf16[8,128,256]{2,1,0:T(8,128)(2,1)}, u32[]{:S(2)}, u32[]{:S(2)}) async-start(bf16[8,128,256]{2,1,0:T(8,128)(2,1)} %pick.1), calls=%async_computation | async-start | bytes 1048576 | tf_op jit(solution)/shard_map/all_to_all | solution.py:303
  9.1 1.2 %copy-start = (bf16[16,128,256]{2,1,0:T(8,128)(2,1)S(1)}, bf16[16,128,256]{2,1,0:T(8,128)(2,1)}, u32[]{:S(2)}) copy-start(bf16[16,128,256]{2,1,0:T(8,128)(2,1)} %refs_3_.1) | copy-start | bytes 3145732
  10.3 0.9 %copy-start.1 = (bf16[256,256]{1,0:T(8,128)(2,1)S(1)}, bf16[256,256]{1,0:T(8,128)(2,1)}, u32[]{:S(2)}) copy-start(bf16[256,256]{1,0:T(8,128)(2,1)} %w_self.1) | copy-start | bytes 393220
  11.2 1.0 %copy-start.3 = (bf16[1,64,32,128]{3,2,1,0:T(8,128)(2,1)S(1)}, bf16[1,64,32,128]{3,2,1,0:T(8,128)(2,1)}, u32[]{:S(2)}) copy-start(bf16[1,64,32,128]{3,2,1,0:T(8,128)(2,1)} %refs_2_.1) | copy-start | bytes 1572868
  12.3 0.9 %copy-start.4 = (bf16[16,32,256]{2,1,0:T(8,128)(2,1)S(1)}, bf16[16,32,256]{2,1,0:T(8,128)(2,1)}, u32[]{:S(2)}) copy-start(bf16[16,32,256]{2,1,0:T(8,128)(2,1)} %refs_6_.1) | copy-start | bytes 786436
  13.2 0.9 %copy-start.5 = (bf16[256,256]{1,0:T(8,128)(2,1)S(1)}, bf16[256,256]{1,0:T(8,128)(2,1)}, u32[]{:S(2)}) copy-start(bf16[256,256]{1,0:T(8,128)(2,1)} %refs_5_.1) | copy-start | bytes 393220
  14.1 0.7 %copy-start.8 = (s32[1,64]{1,0:T(1,128)S(1)}, s32[1,64]{1,0:T(1,128)}, u32[]{:S(2)}) copy-start(s32[1,64]{1,0:T(1,128)} %refs_0_.1) | copy-start | bytes 772
  14.8 0.7 %copy-start.9 = (s32[1,64]{1,0:T(1,128)S(1)}, s32[1,64]{1,0:T(1,128)}, u32[]{:S(2)}) copy-start(s32[1,64]{1,0:T(1,128)} %refs_1_.1) | copy-start | bytes 772
  17.6 12.9 %copy-start.2 = (bf16[256,256]{1,0:T(8,128)(2,1)S(1)}, bf16[256,256]{1,0:T(8,128)(2,1)}, u32[]{:S(2)}) copy-start(bf16[256,256]{1,0:T(8,128)(2,1)} %w_self.1) | copy-start | bytes 393220
  17.6 39.4 %copy-start.6 = (s32[1,8]{1,0:T(1,128)S(1)}, s32[1,8]{1,0:T(1,128)}, u32[]{:S(2)}) copy-start(s32[1,8]{1,0:T(1,128)} %requests_in.3) | copy-start | bytes 100
  26.9 9.0 %collective-permute-start.2 = (bf16[400,256]{1,0:T(8,128)(2,1)S(1)}, bf16[400,256]{1,0:T(8,128)(2,1)S(1)}, u32[]{:S(2)}, u32[]{:S(2)}) collective-permute-start(bf16[400,256]{1,0:T(8,128)(2,1)S(1)} %get-tuple-element.32), channel_id=1, source_target_pairs={{0,24},{8,16},{16,8},{24,0},{1,25},{9,17},{17,9},{25,1},{2,26},{10... | collective-permute-start | bytes 614408 | tf_op jit(solution)/shard_map/ppermute | solution.py:78
  29.4 9.6 %collective-permute-start = (bf16[400,256]{1,0:T(8,128)(2,1)S(1)}, bf16[400,256]{1,0:T(8,128)(2,1)S(1)}, u32[]{:S(2)}, u32[]{:S(2)}) collective-permute-start(bf16[400,256]{1,0:T(8,128)(2,1)S(1)} %get-tuple-element.30), channel_id=1, source_target_pairs={{0,8},{8,0},{16,24},{24,16},{1,9},{9,1},{17,25},{25,17},{2,10},{10... | collective-permute-start | bytes 614408 | tf_op jit(solution)/shard_map/ppermute | solution.py:78
  30.0 9.0 %collective-permute-start.1 = (bf16[400,256]{1,0:T(8,128)(2,1)S(1)}, bf16[400,256]{1,0:T(8,128)(2,1)S(1)}, u32[]{:S(2)}, u32[]{:S(2)}) collective-permute-start(bf16[400,256]{1,0:T(8,128)(2,1)S(1)} %get-tuple-element.31), channel_id=1, source_target_pairs={{0,16},{8,24},{16,0},{24,8},{1,17},{9,25},{17,1},{25,9},{2,18},{10... | collective-permute-start | bytes 614408 | tf_op jit(solution)/shard_map/ppermute | solution.py:78
  39.1 1.4 %collective-permute-start.3 = (bf16[208,256]{1,0:T(8,128)(2,1)S(1)}, bf16[208,256]{1,0:T(8,128)(2,1)S(1)}, u32[]{:S(2)}, u32[]{:S(2)}) collective-permute-start(bf16[208,256]{1,0:T(8,128)(2,1)S(1)} %get-tuple-element.38), channel_id=1, source_target_pairs={{0,1},{1,0},{2,3},{3,2},{4,5},{5,4},{6,7},{7,6},{8,9},{9,8},{10,11... | collective-permute-start | bytes 319496 | tf_op jit(solution)/shard_map/ppermute | solution.py:78
  40.5 7.0 %collective-permute-start.4 = (bf16[144,256]{1,0:T(8,128)(2,1)S(1)}, bf16[144,256]{1,0:T(8,128)(2,1)S(1)}, u32[]{:S(2)}, u32[]{:S(2)}) collective-permute-start(bf16[144,256]{1,0:T(8,128)(2,1)S(1)} %get-tuple-element.39), channel_id=1, source_target_pairs={{0,6},{1,7},{2,4},{3,5},{4,2},{5,3},{6,0},{7,1},{8,14},{9,15},{10,... | collective-permute-start | bytes 221192 | tf_op jit(solution)/shard_map/ppermute | solution.py:78
  42.3 7.2 %collective-permute-start.5 = (bf16[144,256]{1,0:T(8,128)(2,1)S(1)}, bf16[144,256]{1,0:T(8,128)(2,1)S(1)}, u32[]{:S(2)}, u32[]{:S(2)}) collective-permute-start(bf16[144,256]{1,0:T(8,128)(2,1)S(1)} %get-tuple-element.43), channel_id=1, source_target_pairs={{0,2},{1,3},{2,0},{3,1},{4,6},{5,7},{6,4},{7,5},{8,10},{9,11},{10,... | collective-permute-start | bytes 221192 | tf_op jit(solution)/shard_map/ppermute | solution.py:78
  42.3 7.6 %collective-permute-start.6 = (bf16[144,256]{1,0:T(8,128)(2,1)S(1)}, bf16[144,256]{1,0:T(8,128)(2,1)S(1)}, u32[]{:S(2)}, u32[]{:S(2)}) collective-permute-start(bf16[144,256]{1,0:T(8,128)(2,1)S(1)} %get-tuple-element.44), channel_id=1, source_target_pairs={{0,4},{1,5},{2,6},{3,7},{4,0},{5,1},{6,2},{7,3},{8,12},{9,13},{10,... | collective-permute-start | bytes 221192 | tf_op jit(solution)/shard_map/ppermute | solution.py:78
  50.0 4.9 %collective-permute-start.9 = (bf16[64,256]{1,0:T(8,128)(2,1)S(1)}, bf16[64,256]{1,0:T(8,128)(2,1)S(1)}, u32[]{:S(2)}, u32[]{:S(2)}) collective-permute-start(bf16[64,256]{1,0:T(8,128)(2,1)S(1)} %piece.1.refs_0_), channel_id=1, source_target_pairs={{0,24},{8,16},{16,8},{24,0},{1,25},{9,17},{17,9},{25,1},{2,26},{10... | collective-permute-start | bytes 98312 | tf_op jit(solution)/shard_map/ppermute | solution.py:78
  52.4 3.9 %collective-permute-start.8 = (bf16[64,256]{1,0:T(8,128)(2,1)S(1)}, bf16[64,256]{1,0:T(8,128)(2,1)S(1)}, u32[]{:S(2)}, u32[]{:S(2)}) collective-permute-start(bf16[64,256]{1,0:T(8,128)(2,1)S(1)} %piece.1.refs_0_), channel_id=1, source_target_pairs={{0,16},{8,24},{16,0},{24,8},{1,17},{9,25},{17,1},{25,9},{2,18},{10... | collective-permute-start | bytes 98312 | tf_op jit(solution)/shard_map/ppermute | solution.py:78
  53.0 3.9 %collective-permute-start.7 = (bf16[64,256]{1,0:T(8,128)(2,1)S(1)}, bf16[64,256]{1,0:T(8,128)(2,1)S(1)}, u32[]{:S(2)}, u32[]{:S(2)}) collective-permute-start(bf16[64,256]{1,0:T(8,128)(2,1)S(1)} %piece.1.refs_0_), channel_id=1, source_target_pairs={{0,8},{8,0},{16,24},{24,16},{1,9},{9,1},{17,25},{25,17},{2,10},{10... | collective-permute-start | bytes 98312 | tf_op jit(solution)/shard_map/ppermute | solution.py:78
  56.9 1.4 %collective-permute-start.10 = (bf16[256,256]{1,0:T(8,128)(2,1)S(1)}, bf16[256,256]{1,0:T(8,128)(2,1)S(1)}, u32[]{:S(2)}, u32[]{:S(2)}) collective-permute-start(bf16[256,256]{1,0:T(8,128)(2,1)S(1)} %gather_pieces.1.mine), channel_id=1, source_target_pairs={{0,1},{1,0},{2,3},{3,2},{4,5},{5,4},{6,7},{7,6},{8,9},{9,8},{10,11... | collective-permute-start | bytes 393224 | tf_op jit(solution)/shard_map/ppermute | solution.py:78

commit v4 on v3

--- a/solution.py
+++ b/solution.py
@@ -78,20 +78,21 @@
     return lax.ppermute(array, axis, [(i, i ^ distance) for i in range(size)])
 
 
-def pick_kernel(requests_in, feats, out, held, requests, sems):
-    count = out.shape[0]
-    into = pltpu.make_async_copy(feats, held, sems.at[0])
-    into.start()
+def pick_kernel(requests_in, feats, keep, send, held, requests, sem):
+    copy = pltpu.make_async_copy(feats, held, sem)
+    copy.start()
     pltpu.sync_copy(requests_in, requests)
-    into.wait()
-    away = [
-        pltpu.make_async_copy(held.at[requests[0, i]], out.at[i], sems.at[1 + i])
-        for i in range(count)
-    ]
-    for copy in away:
-        copy.start()
-    for copy in away:
-        copy.wait()
+    copy.wait()
+    blk = lax.axis_index("blk")
+    for k in range(keep.shape[0]):
+        keep[k] = held[requests[0, blk ^ (2 * k)]]
+        send[k] = held[requests[0, blk ^ (2 * k + 1)]]
+
+
+def join_kernel(keep, got, *messages):
+    for k, message in enumerate(messages):
+        message[0] = keep[k]
+        message[1] = got[k]
 
 
 def prepare_kernel(
@@ -102,13 +103,13 @@
     features = w_self.shape[0]
     per_slab = row_count // width
     slabs = owners // per_slab
-    rep = lax.axis_index("rep")
+    rep, blk = lax.axis_index("rep"), lax.axis_index("blk")
     copy = pltpu.make_async_copy(feats.at[:, aligned(rep, quarter), :], rows, sem)
     copy.start()
     packed[:slabs] = jnp.zeros((slabs, row_count, row_count), packed.dtype)
 
     def place(t, carry):
-        owner = slot[0, t]
+        owner = slot[0, t] ^ blk
         packed[
             owner // per_slab, aligned(dest[0, t], quarter), aligned(owner % per_slab, width)
         ] = tiles[0, t]
@@ -130,43 +131,30 @@
     packed[2 * slabs + 1, features:, features:] = w_neigh[...]
 
 
-def layer_kernel(grad_scale, owners, replicas, sources_in, packed, bias, *refs):
-    preact_out, grad_pre_out, messages = refs[0], refs[1], refs[2 : 2 + replicas]
-    contributions, gradients, sources, sems = refs[2 + replicas :]
+def layer_kernel(grad_scale, packed, bias, *refs):
+    arrived, (preact_out, grad_pre_out, keep, send) = refs[:-4], refs[-4:]
     row_count, features = preact_out.shape
-    width = contributions.shape[1]
-    quarter = width // replicas
-    share = features // replicas
-    per_slab = row_count // width
-    slabs = owners // per_slab
-    zs = owners // 2
-    rep = lax.axis_index("rep")
+    zs = len(arrived)
+    width = arrived[0].shape[1]
+    pair = 2 * width
+    per_slab = row_count // pair
+    slabs = zs // per_slab
     rows = packed[2 * slabs, :, :features]
     cotangent = packed[2 * slabs, :, features:]
     rows_t = packed[2 * slabs + 1, :features]
     w_self = packed[2 * slabs + 1, features:, :features]
     w_neigh = packed[2 * slabs + 1, features:, features:]
-
-    def fetch(slab):
-        place = aligned(slab, row_count)
-        return pltpu.make_async_copy(sources_in.at[place, :], sources.at[place, :], sems.at[slab])
-
-    for slab in range(slabs):
-        fetch(slab).start()
-    preact = dot(rows, w_self) + bias[...]
-    for slab in range(slabs):
-        fetch(slab).wait()
     half = row_count // 2
 
     def gather_rows(part):
-        def add(slab, total):
-            return total + dot(packed[slab, part], sources[aligned(slab, row_count), :])
-
-        total = dot(packed[0, part], sources[:row_count])
-        return lax.fori_loop(1, slabs, add, total, unroll=slabs <= 4).astype(BF16)
+        total = jnp.zeros((half, features), F32)
+        for k, message in enumerate(arrived):
+            lanes = slice(k % per_slab * pair, (k % per_slab + 1) * pair)
+            total += dot(packed[k // per_slab, part, lanes], message[...].reshape(pair, features))
+        return total.astype(BF16)
 
     agg = jnp.concatenate([gather_rows(slice(0, half)), gather_rows(slice(half, row_count))])
-    preact += dot(agg, w_neigh)
+    preact = dot(rows, w_self) + bias[...] + dot(agg, w_neigh)
     preact_out[...] = preact
     gating = jax.nn.sigmoid(preact)
     grad_pre = (
@@ -176,30 +164,30 @@
     back = lax.dot_general(grad_pre, w_neigh, NT, preferred_element_type=F32).astype(BF16)
 
     def contribute(slab, carry):
-        contributions[pl.ds(slab * per_slab, per_slab)] = (
-            dot(packed[slabs + slab], back).astype(BF16).reshape(per_slab, width, features)
-        )
+        block = dot(packed[slabs + slab], back).astype(BF16)
+        for i in range(per_slab):
+            place = aligned(slab * per_slab + i, width)
+            keep[place, :] = block[i * pair : i * pair + width]
+            send[place, :] = block[i * pair + width : (i + 1) * pair]
         return carry
 
     lax.fori_loop(0, slabs, contribute, 0, unroll=slabs <= 4)
-    gradients[0] = (dot(rows_t, grad_pre) * grad_scale).astype(BF16)
-    gradients[1] = (dot(agg.T, grad_pre) * grad_scale).astype(BF16)
+    base = zs * width
+    grad_self = (dot(rows_t, grad_pre) * grad_scale).astype(BF16)
+    grad_neigh = (dot(agg.T, grad_pre) * grad_scale).astype(BF16)
     bias_rows = split_rows(
         jnp.sum(grad_pre.astype(F32), axis=0, keepdims=True) * grad_scale
     )
-    base = owners * quarter
-    for k, message in enumerate(messages):
-        target = rep ^ k
-        for core in range(2):
-            for z in range(zs):
-                start = (core * zs + z) * quarter
-                message[start : start + quarter] = contributions[
-                    2 * z + core, aligned(target, quarter), :
-                ]
-        for half in range(2):
-            start = base + half * share
-            message[start : start + share] = gradients[half, aligned(target, share), :]
-        message[base + 2 * share :] = bias_rows
+    core = lax.axis_index("blk") % 2
+    for side, to_self, to_neigh in ((0, keep, send), (1, send, keep)):
+
+        @pl.when(core == side)
+        def _():
+            to_self[base : base + features] = grad_self
+            to_neigh[base : base + features] = grad_neigh
+
+    keep[base + features :] = bias_rows
+    send[base + features :] = bias_rows
 
 
 def own_kernel(preact, grad_pre, w_self, hidden, self_term):
@@ -208,35 +196,41 @@
     self_term[...] = lax.dot_general(grad_pre[...], w_self[...], NT, preferred_element_type=F32)
 
 
-def rep_sum_kernel(share, *refs):
-    arrived, keep, send = refs[:-2], refs[-2], refs[-1]
-    core = lax.axis_index("blk") % 2
-    rows = keep.shape[0] - PAD - share
-    base = 2 * rows
-    bias_rows = split_rows(butterfly_sum([join_rows(a[base + 2 * share :]) for a in arrived]))
-    for out, side in ((keep, core), (send, 1 - core)):
-        total = sum(a[aligned(side, rows), :].astype(F32) for a in arrived)
-        out[:rows] = total.astype(BF16)
-        place = pl.ds(pl.multiple_of(base + side * share, PAD), share)
-        total = sum(a[place, :].astype(F32) for a in arrived)
-        out[rows : rows + share] = total.astype(BF16)
-        out[rows + share :] = bias_rows
-
-
-def core_join_kernel(share, keep, got, *messages):
-    zs = len(messages)
-    z = lax.axis_index("blk") // 2
-    rows = keep.shape[0] - PAD - share
-    quarter = rows // zs
-    grads = keep[rows : rows + share].astype(F32) + got[rows : rows + share].astype(F32)
-    grads = grads.astype(BF16)
-    bias_rows = split_rows(join_rows(keep[rows + share :]) + join_rows(got[rows + share :]))
+def assemble_kernel(zs, keep, got, *refs):
+    messages, gradients = refs[:-1], refs[-1]
+    replicas = len(messages)
+    features = keep.shape[1]
+    base = keep.shape[0] - PAD - features
+    width = base // zs
+    quarter, share = width // replicas, features // replicas
+    end = 2 * zs * quarter
+    rep = lax.axis_index("rep")
+    grads = slice(base, base + features)
+    gradients[...] = (keep[grads].astype(F32) + got[grads].astype(F32)).astype(BF16)
+    bias_rows = split_rows(join_rows(keep[base + features :]) + join_rows(got[base + features :]))
     for k, message in enumerate(messages):
-        place = aligned(z ^ k, quarter)
-        message[:quarter] = keep[place, :]
-        message[quarter : 2 * quarter] = got[place, :]
-        message[2 * quarter : 2 * quarter + share] = grads
-        message[2 * quarter + share :] = bias_rows
+        target = rep ^ k
+        for z in range(zs):
+            place = pl.ds(pl.multiple_of(z * width + target * quarter, quarter), quarter)
+            start = 2 * z * quarter
+            message[start : start + quarter] = keep[place, :]
+            message[start + quarter : start + 2 * quarter] = got[place, :]
+        message[end : end + share] = gradients[aligned(target, share), :]
+        message[end + share :] = bias_rows
+
+
+def rep_sum_kernel(zs, *refs):
+    arrived, parcels = refs[:-zs], refs[-zs:]
+    rows = (arrived[0].shape[0] - parcels[0].shape[0]) // (zs - 1)
+    share = parcels[0].shape[0] - PAD - rows
+    end = zs * rows
+    grads = sum(a[end : end + share].astype(F32) for a in arrived).astype(BF16)
+    bias_rows = split_rows(butterfly_sum([join_rows(a[end + share :]) for a in arrived]))
+    for k, parcel in enumerate(parcels):
+        place = slice(k * rows, (k + 1) * rows)
+        parcel[:rows] = sum(a[place].astype(F32) for a in arrived).astype(BF16)
+        parcel[rows : rows + share] = grads
+        parcel[rows + share :] = bias_rows
 
 
 def piece_kernel(*refs):
@@ -287,20 +281,29 @@
     share = features // replicas
     grad_scale = 1.0 / math.sqrt(owners * blk_dev * width)
 
-    outgoing = call(
+    blocks = struct((zs, width, features), BF16)
+    keep, send = call(
         pick_kernel,
         [HBM, HBM],
-        struct((owners, width, features), BF16),
-        HBM,
+        (blocks, blocks),
+        (VMEM, VMEM),
         (
             pltpu.VMEM(feats.shape, BF16),
             pltpu.SMEM((1, owners), jnp.int32),
-            pltpu.SemaphoreType.DMA((1 + owners,)),
+            pltpu.SemaphoreType.DMA,
         ),
         name="pick",
-        limit=56 * MIB,
+        limit=53 * MIB,
     )(requests, feats)
-    sources = lax.all_to_all(outgoing, "blk", split_axis=0, concat_axis=0, tiled=True)
+    got = swap(send, "blk", owners, 1)
+    messages = call(
+        join_kernel,
+        [VMEM, VMEM],
+        (struct((2, width, features), BF16),) * zs,
+        (VMEM,) * zs,
+        name="join",
+    )(keep, got)
+    sources = [messages[0]] + [swap(messages[k], "blk", owners, 2 * k) for k in range(1, zs)]
     per_slab = row_count // width
     packed = call(
         lambda *refs: prepare_kernel(owners, *refs),
@@ -311,23 +314,24 @@
         name="prepare",
     )(tile_dest, tile_slot, tile_vals, feats, w_self, w_neigh, cotangent)
 
-    message_rows = owners * quarter + 2 * share + PAD
-    outs = call(
-        lambda *refs: layer_kernel(grad_scale, owners, replicas, *refs),
-        [HBM, VMEM, VMEM],
-        (struct((row_count, features), F32), struct((row_count, features), BF16))
-        + (struct((message_rows, features), BF16),) * replicas,
-        (VMEM,) * (2 + replicas),
-        (
-            pltpu.VMEM((owners, width, features), BF16),
-            pltpu.VMEM((2, features, features), BF16),
-            pltpu.VMEM((owners * width, features), BF16),
-            pltpu.SemaphoreType.DMA((owners // per_slab,)),
-        ),
+    half = struct((zs * width + features + PAD, features), BF16)
+    preact, grad_pre, keep, send = call(
+        lambda *refs: layer_kernel(grad_scale, *refs),
+        [VMEM] * (2 + zs),
+        (struct((row_count, features), F32), struct((row_count, features), BF16), half, half),
+        (VMEM,) * 4,
         name="layer",
         flops=4 * row_count * features * owners * width,
-    )(sources.reshape(owners * width, features), packed, bias.reshape(1, features))
-    messages = outs[2:]
+    )(packed, bias.reshape(1, features), *sources)
+    got = swap(send, "blk", owners, 1)
+    messages = call(
+        lambda *refs: assemble_kernel(zs, *refs),
+        [VMEM, VMEM],
+        (struct((2 * zs * quarter + share + PAD, features), BF16),) * replicas,
+        (VMEM,) * replicas,
+        (pltpu.VMEM((features, features), BF16),),
+        name="assemble",
+    )(keep, got)
     hidden, self_term = call(
         own_kernel,
         [VMEM] * 3,
@@ -335,27 +339,18 @@
         (VMEM, VMEM),
         name="own",
         flops=2 * row_count * features * features,
-    )(outs[0], outs[1], w_self)
+    )(preact, grad_pre, w_self)
     arrived = [messages[0]] + [
         swap(messages[k], "rep", replicas, k) for k in range(1, replicas)
     ]
     arrived[-1], self_term = lax.optimization_barrier((arrived[-1], self_term))
-    half = struct((zs * quarter + share + PAD, features), BF16)
-    keep, send = call(
-        lambda *refs: rep_sum_kernel(share, *refs),
+    parcels = call(
+        lambda *refs: rep_sum_kernel(zs, *refs),
         [VMEM] * replicas,
-        (half, half),
-        (VMEM, VMEM),
+        (struct((2 * quarter + share + PAD, features), BF16),) * zs,
+        (VMEM,) * zs,
         name="rep_sum",
     )(*arrived)
-    got = swap(send, "blk", owners, 1)
-    parcels = call(
-        lambda *refs: core_join_kernel(share, *refs),
-        [VMEM, VMEM],
-        (struct((2 * quarter + share + PAD, features), BF16),) * zs,
-        (VMEM,) * zs,
-        name="core_join",
-    )(keep, got)
     landed = [parcels[0]] + [swap(parcels[k], "blk", owners, 2 * k) for k in range(1, zs)]
     landed[-1], hidden = lax.optimization_barrier((landed[-1], hidden))
     piece = call(

time: 59.6 us -> 54.9 us (0.921)
  waiting for transfers between devices: 24.2 us -> 20.9 us
  Pallas kernels: 9.88 us -> 8.11 us
  local copies, waits for them, and re-layouts: 6.35 us -> 6.99 us
    all_to_all x1 -> x0, waiting for transfers between devices: 7 us -> none  [on_device(): lax.all_to_all(outgoing, 'blk', split_axis=0, concat_axis=0, tiled=True)]
    all_to_all x1 -> x0, starting transfers between devices: 6.34 us -> none  [on_device(): lax.all_to_all(outgoing, 'blk', split_axis=0, concat_axis=0, tiled=True)]
    ppermute x11 -> x15, starting transfers between devices: 11.7 us -> 17.8 us  [swap(): return lax.ppermute(array, axis, [(i, i ^ distance) for i in range(size)])]
    ppermute x11 -> x15, waiting for transfers between devices: 17.2 us -> 20.9 us  [swap(): return lax.ppermute(array, axis, [(i, i ^ distance) for i in range(size)])]
    pallas_call x10 -> x11, Pallas kernels: 9.88 us -> 8.11 us  [run(): pl.pallas_call(body, in_specs=in_specs, out_shape=out_shape, out_specs=ou...]
    unnamed x20 -> x18, local copies, waits for them, and re-layouts: 6.35 us -> 6.99 us
  transfers between devices with their start and end apart: 12 -> 15, of which waited for: 10 -> 11; matrix products, arithmetic and copies ran while one was open for 0% -> 0% of each run, Pallas kernels for 7% -> 8%
where the time goes in v4:
time: 54.9 us; the launch traced here: 54.6 us
  waiting for transfers between devices  20.9 us (38%)
  starting transfers between devices  17.8 us (32%)
  Pallas kernels  8.11 us (15%)
  local copies, waits for them, and re-layouts  6.99 us (13%)
  between operations  0.73 us (1%)
    ppermute x15, waiting for transfers between devices, swap(): return lax.ppermute(array, axis, [(i, i ^ distance) for i in range(size)])  20.9 us
    ppermute x15, starting transfers between devices, swap(): return lax.ppermute(array, axis, [(i, i ^ distance) for i in range(size)])  17.8 us
    pallas_call x11, Pallas kernels, run(): pl.pallas_call(body, in_specs=in_specs, out_shape=out_shape, out_specs=ou...  8.11 us
    unnamed x18, local copies, waits for them, and re-layouts  6.99 us
  transfers between devices with their start and end apart: 15, of which 11 were waited for; matrix products, arithmetic and copies ran while one was open for 0% of the time, Pallas kernels for 8%

profile of v4, /device:TPU:0, one launch (start us, length us, event | category | flops | bytes accessed | tf_op | source)
XLA Modules:
  0.0 54.6 jit_solution(3894514112351145196)
XLA Ops:
  0.6 0.6 %copy-done.5 = s32[1,8]{1,0:T(1,128)S(1)} copy-done((s32[1,8]{1,0:T(1,128)S(1)}, s32[1,8]{1,0:T(1,128)}, u32[]{:S(2)}) %copy-start.5) | copy-done | bytes 56
  1.3 1.3 %pick.1 = (bf16[4,128,256]{2,1,0:T(8,128)(2,1)S(1)}, bf16[4,128,256]{2,1,0:T(8,128)(2,1)S(1)}) custom-call(s32[1,8]{1,0:T(1,128)S(1)} %copy-done.5, bf16[16,128,256]{2,1,0:T(8,128)(2,1)} %feats.1), custom_call_target="tpu_custom_call" | custom-call | bytes 1572896 | tf_op jit(solution)/shard_map/pick/pallas_call | solution.py:28
  3.1 1.2 %collective-permute-done.got = bf16[4,128,256]{2,1,0:T(8,128)(2,1)S(1)} collective-permute-done((bf16[4,128,256]{2,1,0:T(8,128)(2,1)S(1)}, bf16[4,128,256]{2,1,0:T(8,128)(2,1)S(1)}, u32[]{:S(2)}, u32[]{:S(2)}) %collective-permute-start) | collective-permute-done | bytes 262176 | tf_op jit(solution)/shard_map/ppermute | solution.py:78
  4.3 3.0 %collective-permute-start.1 = (bf16[2,128,256]{2,1,0:T(8,128)(2,1)S(1)}, bf16[2,128,256]{2,1,0:T(8,128)(2,1)S(1)}, u32[]{:S(2)}, u32[]{:S(2)}) collective-permute-start(bf16[2,128,256]{2,1,0:T(8,128)(2,1)S(1)} %get-tuple-element.38), channel_id=1, source_target_pairs={{0,2},{1,3},{2,0},{3,1},{4,6},{5,7},{6,4},{7,5},{8,10},{9,11},{10,... | collective-permute-start | bytes 393224 | tf_op jit(solution)/shard_map/ppermute | solution.py:78
  7.3 2.6 %collective-permute-start.2 = (bf16[2,128,256]{2,1,0:T(8,128)(2,1)S(1)}, bf16[2,128,256]{2,1,0:T(8,128)(2,1)S(1)}, u32[]{:S(2)}, u32[]{:S(2)}) collective-permute-start(bf16[2,128,256]{2,1,0:T(8,128)(2,1)S(1)} %get-tuple-element.39), channel_id=1, source_target_pairs={{0,4},{1,5},{2,6},{3,7},{4,0},{5,1},{6,2},{7,3},{8,12},{9,13},{10,... | collective-permute-start | bytes 393224 | tf_op jit(solution)/shard_map/ppermute | solution.py:78
  9.9 1.2 %copy-done = bf16[16,128,256]{2,1,0:T(8,128)(2,1)S(1)} copy-done((bf16[16,128,256]{2,1,0:T(8,128)(2,1)S(1)}, bf16[16,128,256]{2,1,0:T(8,128)(2,1)}, u32[]{:S(2)}) %copy-start) | copy-done | bytes 1048600
  11.1 0.9 %copy-done.1 = bf16[256,256]{1,0:T(8,128)(2,1)S(1)} copy-done((bf16[256,256]{1,0:T(8,128)(2,1)S(1)}, bf16[256,256]{1,0:T(8,128)(2,1)}, u32[]{:S(2)}) %copy-start.1) | copy-done | bytes 131096
  12.0 1.0 %copy-done.2 = bf16[1,64,32,128]{3,2,1,0:T(8,128)(2,1)S(1)} copy-done((bf16[1,64,32,128]{3,2,1,0:T(8,128)(2,1)S(1)}, bf16[1,64,32,128]{3,2,1,0:T(8,128)(2,1)}, u32[]{:S(2)}) %copy-start.2) | copy-done | bytes 524312
  13.1 0.9 %copy-done.3 = bf16[16,32,256]{2,1,0:T(8,128)(2,1)S(1)} copy-done((bf16[16,32,256]{2,1,0:T(8,128)(2,1)S(1)}, bf16[16,32,256]{2,1,0:T(8,128)(2,1)}, u32[]{:S(2)}) %copy-start.3) | copy-done | bytes 262168
  14.0 0.9 %copy-done.4 = bf16[256,256]{1,0:T(8,128)(2,1)S(1)} copy-done((bf16[256,256]{1,0:T(8,128)(2,1)S(1)}, bf16[256,256]{1,0:T(8,128)(2,1)}, u32[]{:S(2)}) %copy-start.4) | copy-done | bytes 131096
  14.9 0.7 %copy-done.7 = s32[1,64]{1,0:T(1,128)S(1)} copy-done((s32[1,64]{1,0:T(1,128)S(1)}, s32[1,64]{1,0:T(1,128)}, u32[]{:S(2)}) %copy-start.7) | copy-done | bytes 280
  15.6 0.7 %copy-done.8 = s32[1,64]{1,0:T(1,128)S(1)} copy-done((s32[1,64]{1,0:T(1,128)S(1)}, s32[1,64]{1,0:T(1,128)}, u32[]{:S(2)}) %copy-start.8) | copy-done | bytes 280
  16.2 2.1 %prepare.1.refs_0_ = bf16[6,512,512]{2,1,0:T(8,128)(2,1)S(1)} custom-call(s32[1,64]{1,0:T(1,128)S(1)} %copy-done.7, s32[1,64]{1,0:T(1,128)S(1)} %copy-done.8, bf16[1,64,32,128]{3,2,1,0:T(8,128)(2,1)S(1)} %copy-done.2, bf16[16,128,256]{2,1,0:T(8,128)(2,1)S(1)} %copy-done, bf16[256,256]{1,0:T(8,128)(2,1)S(1)} %copy-done.1, bf16[256,256]{1,0:T(8,128)(2,1)S(1)} %copy-done.4, ...), custom_call_target="tpu_custom_call" | custom-call | bytes 5243392 | tf_op jit(solution)/shard_map/prepare/pallas_call | solution.py:28
  18.4 1.8 %collective-permute-done.2.refs_4_ = bf16[2,128,256]{2,1,0:T(8,128)(2,1)S(1)} collective-permute-done((bf16[2,128,256]{2,1,0:T(8,128)(2,1)S(1)}, bf16[2,128,256]{2,1,0:T(8,128)(2,1)S(1)}, u32[]{:S(2)}, u32[]{:S(2)}) %collective-permute-start.2) | collective-permute-done | bytes 131104 | tf_op jit(solution)/shard_map/ppermute | solution.py:78
  20.2 1.3 %layer.1 = (f32[512,256]{1,0:T(8,128)S(1)}, bf16[512,256]{1,0:T(8,128)(2,1)S(1)}, bf16[784,256]{1,0:T(8,128)(2,1)S(1)}, bf16[784,256]{1,0:T(8,128)(2,1)S(1)}) custom-call(bf16[6,512,512]{2,1,0:T(8,128)(2,1)S(1)} %prepare.1.refs_0_, f32[1,256]{1,0:T(1,128)S(1)} %bitcast.2, bf16[2,128,256]{2,1,0:T(8,128)(2,1)S(1)} %get-tuple-element.37.refs_2_, ...), custom_call_target="tpu_custom_call" | custom-call | flops 536870912 | bytes 5260288 | tf_op jit(solution)/shard_map/layer/pallas_call | solution.py:28
  21.6 1.7 %collective-permute-done.4.refs_1_ = bf16[784,256]{1,0:T(8,128)(2,1)S(1)} collective-permute-done((bf16[784,256]{1,0:T(8,128)(2,1)S(1)}, bf16[784,256]{1,0:T(8,128)(2,1)S(1)}, u32[]{:S(2)}, u32[]{:S(2)}) %collective-permute-start.4) | collective-permute-done | bytes 401440 | tf_op jit(solution)/shard_map/ppermute | solution.py:78
  23.4 2.5 %collective-permute-start.7 = (bf16[336,256]{1,0:T(8,128)(2,1)S(1)}, bf16[336,256]{1,0:T(8,128)(2,1)S(1)}, u32[]{:S(2)}, u32[]{:S(2)}) collective-permute-start(bf16[336,256]{1,0:T(8,128)(2,1)S(1)} %get-tuple-element.46), channel_id=1, source_target_pairs={{0,24},{8,16},{16,8},{24,0},{1,25},{9,17},{17,9},{25,1},{2,26},{10... | collective-permute-start | bytes 516104 | tf_op jit(solution)/shard_map/ppermute | solution.py:78
  25.9 0.5 collective-permute-start.5
  27.0 1.0 %own.1 = (bf16[16,32,256]{2,1,0:T(8,128)(2,1)}, f32[512,256]{1,0:T(8,128)S(1)}) custom-call(f32[512,256]{1,0:T(8,128)S(1)} %get-tuple-element.47.preact, bf16[512,256]{1,0:T(8,128)(2,1)S(1)} %get-tuple-element.48.grad_pre, bf16[256,256]{1,0:T(8,128)(2,1)S(1)} %copy-done.1), custom_call_target="tpu_custom_call" | custom-call | flops 67108864 | bytes 1703936 | tf_op jit(solution)/shard_map/own/pallas_call | solution.py:28
  27.9 3.7 %collective-permute-done.7.refs_3_ = bf16[336,256]{1,0:T(8,128)(2,1)S(1)} collective-permute-done((bf16[336,256]{1,0:T(8,128)(2,1)S(1)}, bf16[336,256]{1,0:T(8,128)(2,1)S(1)}, u32[]{:S(2)}, u32[]{:S(2)}) %collective-permute-start.7) | collective-permute-done | bytes 172064 | tf_op jit(solution)/shard_map/ppermute | solution.py:78
  31.6 3.0 %collective-permute-done.5.refs_1_ = bf16[336,256]{1,0:T(8,128)(2,1)S(1)} collective-permute-done((bf16[336,256]{1,0:T(8,128)(2,1)S(1)}, bf16[336,256]{1,0:T(8,128)(2,1)S(1)}, u32[]{:S(2)}, u32[]{:S(2)}) %collective-permute-start.5) | collective-permute-done | bytes 172064 | tf_op jit(solution)/shard_map/ppermute | solution.py:78
  34.7 2.5 %collective-permute-start.8 = (bf16[144,256]{1,0:T(8,128)(2,1)S(1)}, bf16[144,256]{1,0:T(8,128)(2,1)S(1)}, u32[]{:S(2)}, u32[]{:S(2)}) collective-permute-start(bf16[144,256]{1,0:T(8,128)(2,1)S(1)} %get-tuple-element.51), channel_id=1, source_target_pairs={{0,6},{1,7},{2,4},{3,5},{4,2},{5,3},{6,0},{7,1},{8,14},{9,15},{10,... | collective-permute-start | bytes 221192 | tf_op jit(solution)/shard_map/ppermute | solution.py:78
  37.2 1.4 %collective-permute-start.9 = (bf16[144,256]{1,0:T(8,128)(2,1)S(1)}, bf16[144,256]{1,0:T(8,128)(2,1)S(1)}, u32[]{:S(2)}, u32[]{:S(2)}) collective-permute-start(bf16[144,256]{1,0:T(8,128)(2,1)S(1)} %get-tuple-element.55), channel_id=1, source_target_pairs={{0,2},{1,3},{2,0},{3,1},{4,6},{5,7},{6,4},{7,5},{8,10},{9,11},{10,... | collective-permute-start | bytes 221192 | tf_op jit(solution)/shard_map/ppermute | solution.py:78
  39.1 2.5 %collective-permute-done.8.refs_3_ = bf16[144,256]{1,0:T(8,128)(2,1)S(1)} collective-permute-done((bf16[144,256]{1,0:T(8,128)(2,1)S(1)}, bf16[144,256]{1,0:T(8,128)(2,1)S(1)}, u32[]{:S(2)}, u32[]{:S(2)}) %collective-permute-start.8) | collective-permute-done | bytes 73760 | tf_op jit(solution)/shard_map/ppermute | solution.py:78
  41.6 0.8 %collective-permute-done.9.refs_1_ = bf16[144,256]{1,0:T(8,128)(2,1)S(1)} collective-permute-done((bf16[144,256]{1,0:T(8,128)(2,1)S(1)}, bf16[144,256]{1,0:T(8,128)(2,1)S(1)}, u32[]{:S(2)}, u32[]{:S(2)}) %collective-permute-start.9) | collective-permute-done | bytes 73760 | tf_op jit(solution)/shard_map/ppermute | solution.py:78
  42.4 2.9 %collective-permute-done.10.refs_2_ = bf16[144,256]{1,0:T(8,128)(2,1)S(1)} collective-permute-done((bf16[144,256]{1,0:T(8,128)(2,1)S(1)}, bf16[144,256]{1,0:T(8,128)(2,1)S(1)}, u32[]{:S(2)}, u32[]{:S(2)}) %collective-permute-start.10) | collective-permute-done | bytes 73760 | tf_op jit(solution)/shard_map/ppermute | solution.py:78
  45.3 2.5 %collective-permute-start.13 = (bf16[64,256]{1,0:T(8,128)(2,1)S(1)}, bf16[64,256]{1,0:T(8,128)(2,1)S(1)}, u32[]{:S(2)}, u32[]{:S(2)}) collective-permute-start(bf16[64,256]{1,0:T(8,128)(2,1)S(1)} %piece.1.refs_0_), channel_id=1, source_target_pairs={{0,24},{8,16},{16,8},{24,0},{1,25},{9,17},{17,9},{25,1},{2,26},{10... | collective-permute-start | bytes 98312 | tf_op jit(solution)/shard_map/ppermute | solution.py:78
  48.4 0.5 collective-permute-start.11
  48.9 1.3 %collective-permute-done.13.refs_3_ = bf16[64,256]{1,0:T(8,128)(2,1)S(1)} collective-permute-done((bf16[64,256]{1,0:T(8,128)(2,1)S(1)}, bf16[64,256]{1,0:T(8,128)(2,1)S(1)}, u32[]{:S(2)}, u32[]{:S(2)}) %collective-permute-start.13) | collective-permute-done | bytes 32800 | tf_op jit(solution)/shard_map/ppermute | solution.py:78
  50.2 1.5 %collective-permute-done.12.refs_2_ = bf16[64,256]{1,0:T(8,128)(2,1)S(1)} collective-permute-done((bf16[64,256]{1,0:T(8,128)(2,1)S(1)}, bf16[64,256]{1,0:T(8,128)(2,1)S(1)}, u32[]{:S(2)}, u32[]{:S(2)}) %collective-permute-start.12) | collective-permute-done | bytes 32800 | tf_op jit(solution)/shard_map/ppermute | solution.py:78
  52.4 1.3 %finish.1 = (bf16[16,32,256]{2,1,0:T(8,128)(2,1)}, f32[1,256]{1,0:T(1,128)}) custom-call(s32[1,8]{1,0:T(1,128)S(1)} %copy-done.5, f32[512,256]{1,0:T(8,128)S(1)} %get-tuple-element.58.self_term, bf16[144,256]{1,0:T(8,128)(2,1)S(1)} %get-tuple-element.54.refs_0_, bf16[144,256]{1,0:T(8,128)(2,1)S(1)} %collective-permute-done.9.refs_1_, ...), custom_call_target="tpu_custom_call" | custom-call | bytes 1082400 | tf_op jit(solution)/shard_map/finish/pallas_call | solution.py:28
  53.7 0.8 %widen.1 = (f32[256,256]{1,0:T(8,128)}, f32[256,256]{1,0:T(8,128)}) custom-call(bf16[256,256]{1,0:T(8,128)(2,1)S(1)} %gather_pieces.1.mine, bf16[256,256]{1,0:T(8,128)(2,1)S(1)} %collective-permute-done.14.other), custom_call_target="tpu_custom_call" | custom-call | bytes 786432 | tf_op jit(solution)/shard_map/widen/pallas_call | solution.py:28
  (27 shorter events, 3.0 us)
Async XLA Ops:
  0.6 0.7 %copy-start.5 = (s32[1,8]{1,0:T(1,128)S(1)}, s32[1,8]{1,0:T(1,128)}, u32[]{:S(2)}) copy-start(s32[1,8]{1,0:T(1,128)} %requests_in.3) | copy-start | bytes 100
  2.6 17.6 %copy-start.6 = (f32[256]{0:T(256)S(1)}, f32[256]{0:T(256)}, u32[]{:S(2)}) copy-start(f32[256]{0:T(256)} %param.16) | copy-start | bytes 3076
  2.6 1.7 %collective-permute-start = (bf16[4,128,256]{2,1,0:T(8,128)(2,1)S(1)}, bf16[4,128,256]{2,1,0:T(8,128)(2,1)S(1)}, u32[]{:S(2)}, u32[]{:S(2)}) collective-permute-start(bf16[4,128,256]{2,1,0:T(8,128)(2,1)S(1)} %get-tuple-element.36), channel_id=1, source_target_pairs={{0,1},{1,0},{2,3},{3,2},{4,5},{5,4},{6,7},{7,6},{8,9},{9,8},{10,11... | collective-permute-start | bytes 786440 | tf_op jit(solution)/shard_map/ppermute | solution.py:78
  4.3 14.1 %collective-permute-start.1 = (bf16[2,128,256]{2,1,0:T(8,128)(2,1)S(1)}, bf16[2,128,256]{2,1,0:T(8,128)(2,1)S(1)}, u32[]{:S(2)}, u32[]{:S(2)}) collective-permute-start(bf16[2,128,256]{2,1,0:T(8,128)(2,1)S(1)} %get-tuple-element.38), channel_id=1, source_target_pairs={{0,2},{1,3},{2,0},{3,1},{4,6},{5,7},{6,4},{7,5},{8,10},{9,11},{10,... | collective-permute-start | bytes 393224 | tf_op jit(solution)/shard_map/ppermute | solution.py:78
  7.3 12.9 %collective-permute-start.2 = (bf16[2,128,256]{2,1,0:T(8,128)(2,1)S(1)}, bf16[2,128,256]{2,1,0:T(8,128)(2,1)S(1)}, u32[]{:S(2)}, u32[]{:S(2)}) collective-permute-start(bf16[2,128,256]{2,1,0:T(8,128)(2,1)S(1)} %get-tuple-element.39), channel_id=1, source_target_pairs={{0,4},{1,5},{2,6},{3,7},{4,0},{5,1},{6,2},{7,3},{8,12},{9,13},{10,... | collective-permute-start | bytes 393224 | tf_op jit(solution)/shard_map/ppermute | solution.py:78
  9.9 10.3 %collective-permute-start.3 = (bf16[2,128,256]{2,1,0:T(8,128)(2,1)S(1)}, bf16[2,128,256]{2,1,0:T(8,128)(2,1)S(1)}, u32[]{:S(2)}, u32[]{:S(2)}) collective-permute-start(bf16[2,128,256]{2,1,0:T(8,128)(2,1)S(1)} %get-tuple-element.40), channel_id=1, source_target_pairs={{0,6},{1,7},{2,4},{3,5},{4,2},{5,3},{6,0},{7,1},{8,14},{9,15},{10,... | collective-permute-start | bytes 393224 | tf_op jit(solution)/shard_map/ppermute | solution.py:78
  9.9 1.2 %copy-start = (bf16[16,128,256]{2,1,0:T(8,128)(2,1)S(1)}, bf16[16,128,256]{2,1,0:T(8,128)(2,1)}, u32[]{:S(2)}) copy-start(bf16[16,128,256]{2,1,0:T(8,128)(2,1)} %feats.1) | copy-start | bytes 3145732
  11.1 0.9 %copy-start.1 = (bf16[256,256]{1,0:T(8,128)(2,1)S(1)}, bf16[256,256]{1,0:T(8,128)(2,1)}, u32[]{:S(2)}) copy-start(bf16[256,256]{1,0:T(8,128)(2,1)} %w_self.1) | copy-start | bytes 393220
  12.0 1.0 %copy-start.2 = (bf16[1,64,32,128]{3,2,1,0:T(8,128)(2,1)S(1)}, bf16[1,64,32,128]{3,2,1,0:T(8,128)(2,1)}, u32[]{:S(2)}) copy-start(bf16[1,64,32,128]{3,2,1,0:T(8,128)(2,1)} %refs_2_.1) | copy-start | bytes 1572868
  13.1 0.9 %copy-start.3 = (bf16[16,32,256]{2,1,0:T(8,128)(2,1)S(1)}, bf16[16,32,256]{2,1,0:T(8,128)(2,1)}, u32[]{:S(2)}) copy-start(bf16[16,32,256]{2,1,0:T(8,128)(2,1)} %refs_6_.1) | copy-start | bytes 786436
  14.0 0.9 %copy-start.4 = (bf16[256,256]{1,0:T(8,128)(2,1)S(1)}, bf16[256,256]{1,0:T(8,128)(2,1)}, u32[]{:S(2)}) copy-start(bf16[256,256]{1,0:T(8,128)(2,1)} %refs_5_.1) | copy-start | bytes 393220
  14.9 0.7 %copy-start.7 = (s32[1,64]{1,0:T(1,128)S(1)}, s32[1,64]{1,0:T(1,128)}, u32[]{:S(2)}) copy-start(s32[1,64]{1,0:T(1,128)} %refs_0_.1) | copy-start | bytes 772
  15.6 0.7 %copy-start.8 = (s32[1,64]{1,0:T(1,128)S(1)}, s32[1,64]{1,0:T(1,128)}, u32[]{:S(2)}) copy-start(s32[1,64]{1,0:T(1,128)} %refs_1_.1) | copy-start | bytes 772
  21.5 1.8 %collective-permute-start.4 = (bf16[784,256]{1,0:T(8,128)(2,1)S(1)}, bf16[784,256]{1,0:T(8,128)(2,1)S(1)}, u32[]{:S(2)}, u32[]{:S(2)}) collective-permute-start(bf16[784,256]{1,0:T(8,128)(2,1)S(1)} %get-tuple-element.42), channel_id=1, source_target_pairs={{0,1},{1,0},{2,3},{3,2},{4,5},{5,4},{6,7},{7,6},{8,9},{9,8},{10,11... | collective-permute-start | bytes 1204232 | tf_op jit(solution)/shard_map/ppermute | solution.py:78
  23.4 8.2 %collective-permute-start.7 = (bf16[336,256]{1,0:T(8,128)(2,1)S(1)}, bf16[336,256]{1,0:T(8,128)(2,1)S(1)}, u32[]{:S(2)}, u32[]{:S(2)}) collective-permute-start(bf16[336,256]{1,0:T(8,128)(2,1)S(1)} %get-tuple-element.46), channel_id=1, source_target_pairs={{0,24},{8,16},{16,8},{24,0},{1,25},{9,17},{17,9},{25,1},{2,26},{10... | collective-permute-start | bytes 516104 | tf_op jit(solution)/shard_map/ppermute | solution.py:78
  25.9 8.7 %collective-permute-start.5 = (bf16[336,256]{1,0:T(8,128)(2,1)S(1)}, bf16[336,256]{1,0:T(8,128)(2,1)S(1)}, u32[]{:S(2)}, u32[]{:S(2)}) collective-permute-start(bf16[336,256]{1,0:T(8,128)(2,1)S(1)} %get-tuple-element.44), channel_id=1, source_target_pairs={{0,8},{8,0},{16,24},{24,16},{1,9},{9,1},{17,25},{25,17},{2,10},{10... | collective-permute-start | bytes 516104 | tf_op jit(solution)/shard_map/ppermute | solution.py:78
  26.5 8.1 %collective-permute-start.6 = (bf16[336,256]{1,0:T(8,128)(2,1)S(1)}, bf16[336,256]{1,0:T(8,128)(2,1)S(1)}, u32[]{:S(2)}, u32[]{:S(2)}) collective-permute-start(bf16[336,256]{1,0:T(8,128)(2,1)S(1)} %get-tuple-element.45), channel_id=1, source_target_pairs={{0,16},{8,24},{16,0},{24,8},{1,17},{9,25},{17,1},{25,9},{2,18},{10... | collective-permute-start | bytes 516104 | tf_op jit(solution)/shard_map/ppermute | solution.py:78
  34.7 7.0 %collective-permute-start.8 = (bf16[144,256]{1,0:T(8,128)(2,1)S(1)}, bf16[144,256]{1,0:T(8,128)(2,1)S(1)}, u32[]{:S(2)}, u32[]{:S(2)}) collective-permute-start(bf16[144,256]{1,0:T(8,128)(2,1)S(1)} %get-tuple-element.51), channel_id=1, source_target_pairs={{0,6},{1,7},{2,4},{3,5},{4,2},{5,3},{6,0},{7,1},{8,14},{9,15},{10,... | collective-permute-start | bytes 221192 | tf_op jit(solution)/shard_map/ppermute | solution.py:78
  37.2 5.2 %collective-permute-start.9 = (bf16[144,256]{1,0:T(8,128)(2,1)S(1)}, bf16[144,256]{1,0:T(8,128)(2,1)S(1)}, u32[]{:S(2)}, u32[]{:S(2)}) collective-permute-start(bf16[144,256]{1,0:T(8,128)(2,1)S(1)} %get-tuple-element.55), channel_id=1, source_target_pairs={{0,2},{1,3},{2,0},{3,1},{4,6},{5,7},{6,4},{7,5},{8,10},{9,11},{10,... | collective-permute-start | bytes 221192 | tf_op jit(solution)/shard_map/ppermute | solution.py:78
  38.6 6.7 %collective-permute-start.10 = (bf16[144,256]{1,0:T(8,128)(2,1)S(1)}, bf16[144,256]{1,0:T(8,128)(2,1)S(1)}, u32[]{:S(2)}, u32[]{:S(2)}) collective-permute-start(bf16[144,256]{1,0:T(8,128)(2,1)S(1)} %get-tuple-element.56), channel_id=1, source_target_pairs={{0,4},{1,5},{2,6},{3,7},{4,0},{5,1},{6,2},{7,3},{8,12},{9,13},{10,... | collective-permute-start | bytes 221192 | tf_op jit(solution)/shard_map/ppermute | solution.py:78
  45.3 4.9 %collective-permute-start.13 = (bf16[64,256]{1,0:T(8,128)(2,1)S(1)}, bf16[64,256]{1,0:T(8,128)(2,1)S(1)}, u32[]{:S(2)}, u32[]{:S(2)}) collective-permute-start(bf16[64,256]{1,0:T(8,128)(2,1)S(1)} %piece.1.refs_0_), channel_id=1, source_target_pairs={{0,24},{8,16},{16,8},{24,0},{1,25},{9,17},{17,9},{25,1},{2,26},{10... | collective-permute-start | bytes 98312 | tf_op jit(solution)/shard_map/ppermute | solution.py:78
  47.9 3.9 %collective-permute-start.12 = (bf16[64,256]{1,0:T(8,128)(2,1)S(1)}, bf16[64,256]{1,0:T(8,128)(2,1)S(1)}, u32[]{:S(2)}, u32[]{:S(2)}) collective-permute-start(bf16[64,256]{1,0:T(8,128)(2,1)S(1)} %piece.1.refs_0_), channel_id=1, source_target_pairs={{0,16},{8,24},{16,0},{24,8},{1,17},{9,25},{17,1},{25,9},{2,18},{10... | collective-permute-start | bytes 98312 | tf_op jit(solution)/shard_map/ppermute | solution.py:78
  48.4 3.9 %collective-permute-start.11 = (bf16[64,256]{1,0:T(8,128)(2,1)S(1)}, bf16[64,256]{1,0:T(8,128)(2,1)S(1)}, u32[]{:S(2)}, u32[]{:S(2)}) collective-permute-start(bf16[64,256]{1,0:T(8,128)(2,1)S(1)} %piece.1.refs_0_), channel_id=1, source_target_pairs={{0,8},{8,0},{16,24},{24,16},{1,9},{9,1},{17,25},{25,17},{2,10},{10... | collective-permute-start | bytes 98312 | tf_op jit(solution)/shard_map/ppermute | solution.py:78
  52.3 1.4 %collective-permute-start.14 = (bf16[256,256]{1,0:T(8,128)(2,1)S(1)}, bf16[256,256]{1,0:T(8,128)(2,1)S(1)}, u32[]{:S(2)}, u32[]{:S(2)}) collective-permute-start(bf16[256,256]{1,0:T(8,128)(2,1)S(1)} %gather_pieces.1.mine), channel_id=1, source_target_pairs={{0,1},{1,0},{2,3},{3,2},{4,5},{5,4},{6,7},{7,6},{8,9},{9,8},{10,11... | collective-permute-start | bytes 393224 | tf_op jit(solution)/shard_map/ppermute | solution.py:78

commit v5 on v4

--- a/solution.py
+++ b/solution.py
@@ -314,6 +314,7 @@
         name="prepare",
     )(tile_dest, tile_slot, tile_vals, feats, w_self, w_neigh, cotangent)
 
+    sources[-1], packed = lax.optimization_barrier((sources[-1], packed))
     half = struct((zs * width + features + PAD, features), BF16)
     preact, grad_pre, keep, send = call(
         lambda *refs: layer_kernel(grad_scale, *refs),
@@ -343,7 +344,7 @@
     arrived = [messages[0]] + [
         swap(messages[k], "rep", replicas, k) for k in range(1, replicas)
     ]
-    arrived[-1], self_term = lax.optimization_barrier((arrived[-1], self_term))
+    *arrived, self_term = lax.optimization_barrier((*arrived, self_term))
     parcels = call(
         lambda *refs: rep_sum_kernel(zs, *refs),
         [VMEM] * replicas,

time: 54.9 us -> 53.3 us (0.971)
  waiting for transfers between devices: 20.9 us -> 19.2 us
    ppermute x15, waiting for transfers between devices: 20.9 us -> 19.2 us  [swap(): return lax.ppermute(array, axis, [(i, i ^ distance) for i in range(size)])]
  transfers between devices with their start and end apart: 15 -> 15, of which waited for: 11 -> 10; matrix products, arithmetic and copies ran while one was open for 0% -> 0% of each run, Pallas kernels for 8% -> 8%
where the time goes in v5:
time: 53.3 us; the launch traced here: 52.9 us
  waiting for transfers between devices  19.2 us (36%)
  starting transfers between devices  17.9 us (34%)
  Pallas kernels  8.11 us (15%)
  local copies, waits for them, and re-layouts  6.99 us (13%)
  between operations  0.74 us (1%)
    ppermute x15, waiting for transfers between devices, swap(): return lax.ppermute(array, axis, [(i, i ^ distance) for i in range(size)])  19.2 us
    ppermute x15, starting transfers between devices, swap(): return lax.ppermute(array, axis, [(i, i ^ distance) for i in range(size)])  17.9 us
    pallas_call x11, Pallas kernels, run(): pl.pallas_call(body, in_specs=in_specs, out_shape=out_shape, out_specs=ou...  8.11 us
    unnamed x18, local copies, waits for them, and re-layouts  6.99 us
  transfers between devices with their start and end apart: 15, of which 10 were waited for; matrix products, arithmetic and copies ran while one was open for 0% of the time, Pallas kernels for 8%

profile of v5, /device:TPU:0, one launch (start us, length us, event | category | flops | bytes accessed | tf_op | source)
XLA Modules:
  0.0 52.9 jit_solution(3771626639932169862)
XLA Ops:
  0.6 0.6 %copy-done.5 = s32[1,8]{1,0:T(1,128)S(1)} copy-done((s32[1,8]{1,0:T(1,128)S(1)}, s32[1,8]{1,0:T(1,128)}, u32[]{:S(2)}) %copy-start.5) | copy-done | bytes 56
  1.3 1.3 %pick.1 = (bf16[4,128,256]{2,1,0:T(8,128)(2,1)S(1)}, bf16[4,128,256]{2,1,0:T(8,128)(2,1)S(1)}) custom-call(s32[1,8]{1,0:T(1,128)S(1)} %copy-done.5, bf16[16,128,256]{2,1,0:T(8,128)(2,1)} %refs_3_.1), custom_call_target="tpu_custom_call" | custom-call | bytes 1572896 | tf_op jit(solution)/shard_map/pick/pallas_call | solution.py:28
  3.1 1.2 %collective-permute-done.got = bf16[4,128,256]{2,1,0:T(8,128)(2,1)S(1)} collective-permute-done((bf16[4,128,256]{2,1,0:T(8,128)(2,1)S(1)}, bf16[4,128,256]{2,1,0:T(8,128)(2,1)S(1)}, u32[]{:S(2)}, u32[]{:S(2)}) %collective-permute-start) | collective-permute-done | bytes 262176 | tf_op jit(solution)/shard_map/ppermute | solution.py:78
  4.3 5.0 %collective-permute-start.1 = (bf16[2,128,256]{2,1,0:T(8,128)(2,1)S(1)}, bf16[2,128,256]{2,1,0:T(8,128)(2,1)S(1)}, u32[]{:S(2)}, u32[]{:S(2)}) collective-permute-start(bf16[2,128,256]{2,1,0:T(8,128)(2,1)S(1)} %get-tuple-element.42), channel_id=1, source_target_pairs={{0,6},{1,7},{2,4},{3,5},{4,2},{5,3},{6,0},{7,1},{8,14},{9,15},{10,... | collective-permute-start | bytes 393224 | tf_op jit(solution)/shard_map/ppermute | solution.py:78
  9.3 0.6 %collective-permute-start.3 = (bf16[2,128,256]{2,1,0:T(8,128)(2,1)S(1)}, bf16[2,128,256]{2,1,0:T(8,128)(2,1)S(1)}, u32[]{:S(2)}, u32[]{:S(2)}) collective-permute-start(bf16[2,128,256]{2,1,0:T(8,128)(2,1)S(1)} %get-tuple-element.46), channel_id=1, source_target_pairs={{0,4},{1,5},{2,6},{3,7},{4,0},{5,1},{6,2},{7,3},{8,12},{9,13},{10,... | collective-permute-start | bytes 393224 | tf_op jit(solution)/shard_map/ppermute | solution.py:78
  10.0 1.2 %copy-done = bf16[16,128,256]{2,1,0:T(8,128)(2,1)S(1)} copy-done((bf16[16,128,256]{2,1,0:T(8,128)(2,1)S(1)}, bf16[16,128,256]{2,1,0:T(8,128)(2,1)}, u32[]{:S(2)}) %copy-start) | copy-done | bytes 1048600
  11.2 0.9 %copy-done.1 = bf16[256,256]{1,0:T(8,128)(2,1)S(1)} copy-done((bf16[256,256]{1,0:T(8,128)(2,1)S(1)}, bf16[256,256]{1,0:T(8,128)(2,1)}, u32[]{:S(2)}) %copy-start.1) | copy-done | bytes 131096
  12.1 1.0 %copy-done.2 = bf16[1,64,32,128]{3,2,1,0:T(8,128)(2,1)S(1)} copy-done((bf16[1,64,32,128]{3,2,1,0:T(8,128)(2,1)S(1)}, bf16[1,64,32,128]{3,2,1,0:T(8,128)(2,1)}, u32[]{:S(2)}) %copy-start.2) | copy-done | bytes 524312
  13.1 0.9 %copy-done.3 = bf16[16,32,256]{2,1,0:T(8,128)(2,1)S(1)} copy-done((bf16[16,32,256]{2,1,0:T(8,128)(2,1)S(1)}, bf16[16,32,256]{2,1,0:T(8,128)(2,1)}, u32[]{:S(2)}) %copy-start.3) | copy-done | bytes 262168
  14.1 0.9 %copy-done.4 = bf16[256,256]{1,0:T(8,128)(2,1)S(1)} copy-done((bf16[256,256]{1,0:T(8,128)(2,1)S(1)}, bf16[256,256]{1,0:T(8,128)(2,1)}, u32[]{:S(2)}) %copy-start.4) | copy-done | bytes 131096
  15.0 0.7 %copy-done.7 = s32[1,64]{1,0:T(1,128)S(1)} copy-done((s32[1,64]{1,0:T(1,128)S(1)}, s32[1,64]{1,0:T(1,128)}, u32[]{:S(2)}) %copy-start.7) | copy-done | bytes 280
  15.7 0.7 %copy-done.8 = s32[1,64]{1,0:T(1,128)S(1)} copy-done((s32[1,64]{1,0:T(1,128)S(1)}, s32[1,64]{1,0:T(1,128)}, u32[]{:S(2)}) %copy-start.8) | copy-done | bytes 280
  16.3 2.1 %prepare.1.refs_0_ = bf16[6,512,512]{2,1,0:T(8,128)(2,1)S(1)} custom-call(s32[1,64]{1,0:T(1,128)S(1)} %copy-done.7, s32[1,64]{1,0:T(1,128)S(1)} %copy-done.8, bf16[1,64,32,128]{3,2,1,0:T(8,128)(2,1)S(1)} %copy-done.2, bf16[16,128,256]{2,1,0:T(8,128)(2,1)S(1)} %copy-done, bf16[256,256]{1,0:T(8,128)(2,1)S(1)} %copy-done.1, bf16[256,256]{1,0:T(8,128)(2,1)S(1)} %copy-done.4, ...), custom_call_target="tpu_custom_call" | custom-call | bytes 5243392 | tf_op jit(solution)/shard_map/prepare/pallas_call | solution.py:28
  18.5 2.2 %collective-permute-done.3.refs_4_ = bf16[2,128,256]{2,1,0:T(8,128)(2,1)S(1)} collective-permute-done((bf16[2,128,256]{2,1,0:T(8,128)(2,1)S(1)}, bf16[2,128,256]{2,1,0:T(8,128)(2,1)S(1)}, u32[]{:S(2)}, u32[]{:S(2)}) %collective-permute-start.3) | collective-permute-done | bytes 131104 | tf_op jit(solution)/shard_map/ppermute | solution.py:78
  20.7 1.3 %layer.1 = (f32[512,256]{1,0:T(8,128)S(1)}, bf16[512,256]{1,0:T(8,128)(2,1)S(1)}, bf16[784,256]{1,0:T(8,128)(2,1)S(1)}, bf16[784,256]{1,0:T(8,128)(2,1)S(1)}) custom-call(bf16[6,512,512]{2,1,0:T(8,128)(2,1)S(1)} %prepare.1.refs_0_, f32[1,256]{1,0:T(1,128)S(1)} %bitcast.2, bf16[2,128,256]{2,1,0:T(8,128)(2,1)S(1)} %get-tuple-element.44.refs_2_, ...), custom_call_target="tpu_custom_call" | custom-call | flops 536870912 | bytes 5260288 | tf_op jit(solution)/shard_map/layer/pallas_call | solution.py:28
  22.1 1.7 %collective-permute-done.4.refs_1_ = bf16[784,256]{1,0:T(8,128)(2,1)S(1)} collective-permute-done((bf16[784,256]{1,0:T(8,128)(2,1)S(1)}, bf16[784,256]{1,0:T(8,128)(2,1)S(1)}, u32[]{:S(2)}, u32[]{:S(2)}) %collective-permute-start.4) | collective-permute-done | bytes 401440 | tf_op jit(solution)/shard_map/ppermute | solution.py:78
  23.9 1.6 %collective-permute-start.5 = (bf16[336,256]{1,0:T(8,128)(2,1)S(1)}, bf16[336,256]{1,0:T(8,128)(2,1)S(1)}, u32[]{:S(2)}, u32[]{:S(2)}) collective-permute-start(bf16[336,256]{1,0:T(8,128)(2,1)S(1)} %get-tuple-element.51), channel_id=1, source_target_pairs={{0,8},{8,0},{16,24},{24,16},{1,9},{9,1},{17,25},{25,17},{2,10},{10... | collective-permute-start | bytes 516104 | tf_op jit(solution)/shard_map/ppermute | solution.py:78
  25.5 1.5 %collective-permute-start.6 = (bf16[336,256]{1,0:T(8,128)(2,1)S(1)}, bf16[336,256]{1,0:T(8,128)(2,1)S(1)}, u32[]{:S(2)}, u32[]{:S(2)}) collective-permute-start(bf16[336,256]{1,0:T(8,128)(2,1)S(1)} %get-tuple-element.52), channel_id=1, source_target_pairs={{0,16},{8,24},{16,0},{24,8},{1,17},{9,25},{17,1},{25,9},{2,18},{10... | collective-permute-start | bytes 516104 | tf_op jit(solution)/shard_map/ppermute | solution.py:78
  27.5 1.0 %own.1 = (bf16[16,32,256]{2,1,0:T(8,128)(2,1)}, f32[512,256]{1,0:T(8,128)S(1)}) custom-call(f32[512,256]{1,0:T(8,128)S(1)} %get-tuple-element.54.preact, bf16[512,256]{1,0:T(8,128)(2,1)S(1)} %get-tuple-element.55.grad_pre, bf16[256,256]{1,0:T(8,128)(2,1)S(1)} %copy-done.1), custom_call_target="tpu_custom_call" | custom-call | flops 67108864 | bytes 1703936 | tf_op jit(solution)/shard_map/own/pallas_call | solution.py:28
  28.4 2.8 %collective-permute-done.5.refs_1_ = bf16[336,256]{1,0:T(8,128)(2,1)S(1)} collective-permute-done((bf16[336,256]{1,0:T(8,128)(2,1)S(1)}, bf16[336,256]{1,0:T(8,128)(2,1)S(1)}, u32[]{:S(2)}, u32[]{:S(2)}) %collective-permute-start.5) | collective-permute-done | bytes 172064 | tf_op jit(solution)/shard_map/ppermute | solution.py:78
  31.2 4.1 %collective-permute-done.6.refs_2_ = bf16[336,256]{1,0:T(8,128)(2,1)S(1)} collective-permute-done((bf16[336,256]{1,0:T(8,128)(2,1)S(1)}, bf16[336,256]{1,0:T(8,128)(2,1)S(1)}, u32[]{:S(2)}, u32[]{:S(2)}) %collective-permute-start.6) | collective-permute-done | bytes 172064 | tf_op jit(solution)/shard_map/ppermute | solution.py:78
  35.4 2.5 %collective-permute-start.8 = (bf16[144,256]{1,0:T(8,128)(2,1)S(1)}, bf16[144,256]{1,0:T(8,128)(2,1)S(1)}, u32[]{:S(2)}, u32[]{:S(2)}) collective-permute-start(bf16[144,256]{1,0:T(8,128)(2,1)S(1)} %get-tuple-element.61), channel_id=1, source_target_pairs={{0,6},{1,7},{2,4},{3,5},{4,2},{5,3},{6,0},{7,1},{8,14},{9,15},{10,... | collective-permute-start | bytes 221192 | tf_op jit(solution)/shard_map/ppermute | solution.py:78
  38.0 1.9 %collective-permute-start.10 = (bf16[144,256]{1,0:T(8,128)(2,1)S(1)}, bf16[144,256]{1,0:T(8,128)(2,1)S(1)}, u32[]{:S(2)}, u32[]{:S(2)}) collective-permute-start(bf16[144,256]{1,0:T(8,128)(2,1)S(1)} %get-tuple-element.66), channel_id=1, source_target_pairs={{0,4},{1,5},{2,6},{3,7},{4,0},{5,1},{6,2},{7,3},{8,12},{9,13},{10,... | collective-permute-start | bytes 221192 | tf_op jit(solution)/shard_map/ppermute | solution.py:78
  39.9 2.1 %collective-permute-done.8.refs_3_ = bf16[144,256]{1,0:T(8,128)(2,1)S(1)} collective-permute-done((bf16[144,256]{1,0:T(8,128)(2,1)S(1)}, bf16[144,256]{1,0:T(8,128)(2,1)S(1)}, u32[]{:S(2)}, u32[]{:S(2)}) %collective-permute-start.8) | collective-permute-done | bytes 73760 | tf_op jit(solution)/shard_map/ppermute | solution.py:78
  42.0 1.7 %collective-permute-done.9.refs_1_ = bf16[144,256]{1,0:T(8,128)(2,1)S(1)} collective-permute-done((bf16[144,256]{1,0:T(8,128)(2,1)S(1)}, bf16[144,256]{1,0:T(8,128)(2,1)S(1)}, u32[]{:S(2)}, u32[]{:S(2)}) %collective-permute-start.9) | collective-permute-done | bytes 73760 | tf_op jit(solution)/shard_map/ppermute | solution.py:78
  43.7 1.5 %collective-permute-start.13 = (bf16[64,256]{1,0:T(8,128)(2,1)S(1)}, bf16[64,256]{1,0:T(8,128)(2,1)S(1)}, u32[]{:S(2)}, u32[]{:S(2)}) collective-permute-start(bf16[64,256]{1,0:T(8,128)(2,1)S(1)} %piece.1.refs_0_), channel_id=1, source_target_pairs={{0,24},{8,16},{16,8},{24,0},{1,25},{9,17},{17,9},{25,1},{2,26},{10... | collective-permute-start | bytes 98312 | tf_op jit(solution)/shard_map/ppermute | solution.py:78
  45.2 1.5 %collective-permute-start.12 = (bf16[64,256]{1,0:T(8,128)(2,1)S(1)}, bf16[64,256]{1,0:T(8,128)(2,1)S(1)}, u32[]{:S(2)}, u32[]{:S(2)}) collective-permute-start(bf16[64,256]{1,0:T(8,128)(2,1)S(1)} %piece.1.refs_0_), channel_id=1, source_target_pairs={{0,16},{8,24},{16,0},{24,8},{1,17},{9,25},{17,1},{25,9},{2,18},{10... | collective-permute-start | bytes 98312 | tf_op jit(solution)/shard_map/ppermute | solution.py:78
  46.7 0.6 %collective-permute-start.11 = (bf16[64,256]{1,0:T(8,128)(2,1)S(1)}, bf16[64,256]{1,0:T(8,128)(2,1)S(1)}, u32[]{:S(2)}, u32[]{:S(2)}) collective-permute-start(bf16[64,256]{1,0:T(8,128)(2,1)S(1)} %piece.1.refs_0_), channel_id=1, source_target_pairs={{0,8},{8,0},{16,24},{24,16},{1,9},{9,1},{17,25},{25,17},{2,10},{10... | collective-permute-start | bytes 98312 | tf_op jit(solution)/shard_map/ppermute | solution.py:78
  47.3 1.3 %collective-permute-done.13.refs_3_ = bf16[64,256]{1,0:T(8,128)(2,1)S(1)} collective-permute-done((bf16[64,256]{1,0:T(8,128)(2,1)S(1)}, bf16[64,256]{1,0:T(8,128)(2,1)S(1)}, u32[]{:S(2)}, u32[]{:S(2)}) %collective-permute-start.13) | collective-permute-done | bytes 32800 | tf_op jit(solution)/shard_map/ppermute | solution.py:78
  49.2 1.5 %collective-permute-done.11.refs_1_ = bf16[64,256]{1,0:T(8,128)(2,1)S(1)} collective-permute-done((bf16[64,256]{1,0:T(8,128)(2,1)S(1)}, bf16[64,256]{1,0:T(8,128)(2,1)S(1)}, u32[]{:S(2)}, u32[]{:S(2)}) %collective-permute-start.11) | collective-permute-done | bytes 32800 | tf_op jit(solution)/shard_map/ppermute | solution.py:78
  50.7 1.3 %finish.1 = (bf16[16,32,256]{2,1,0:T(8,128)(2,1)}, f32[1,256]{1,0:T(1,128)}) custom-call(s32[1,8]{1,0:T(1,128)S(1)} %copy-done.5, f32[512,256]{1,0:T(8,128)S(1)} %get-tuple-element.68.self_term, bf16[144,256]{1,0:T(8,128)(2,1)S(1)} %get-tuple-element.64.refs_0_, bf16[144,256]{1,0:T(8,128)(2,1)S(1)} %collective-permute-done.9.refs_1_, ...), custom_call_target="tpu_custom_call" | custom-call | bytes 1082400 | tf_op jit(solution)/shard_map/finish/pallas_call | solution.py:28
  52.1 0.8 %widen.1 = (f32[256,256]{1,0:T(8,128)}, f32[256,256]{1,0:T(8,128)}) custom-call(bf16[256,256]{1,0:T(8,128)(2,1)S(1)} %gather_pieces.1.mine, bf16[256,256]{1,0:T(8,128)(2,1)S(1)} %collective-permute-done.14.other), custom_call_target="tpu_custom_call" | custom-call | bytes 786432 | tf_op jit(solution)/shard_map/widen/pallas_call | solution.py:28
  (27 shorter events, 2.0 us)
Async XLA Ops:
  0.6 0.7 %copy-start.5 = (s32[1,8]{1,0:T(1,128)S(1)}, s32[1,8]{1,0:T(1,128)}, u32[]{:S(2)}) copy-start(s32[1,8]{1,0:T(1,128)} %requests_in.3) | copy-start | bytes 100
  2.6 18.1 %copy-start.6 = (f32[256]{0:T(256)S(1)}, f32[256]{0:T(256)}, u32[]{:S(2)}) copy-start(f32[256]{0:T(256)} %param.16) | copy-start | bytes 3076
  2.6 1.7 %collective-permute-start = (bf16[4,128,256]{2,1,0:T(8,128)(2,1)S(1)}, bf16[4,128,256]{2,1,0:T(8,128)(2,1)S(1)}, u32[]{:S(2)}, u32[]{:S(2)}) collective-permute-start(bf16[4,128,256]{2,1,0:T(8,128)(2,1)S(1)} %get-tuple-element.41), channel_id=1, source_target_pairs={{0,1},{1,0},{2,3},{3,2},{4,5},{5,4},{6,7},{7,6},{8,9},{9,8},{10,11... | collective-permute-start | bytes 786440 | tf_op jit(solution)/shard_map/ppermute | solution.py:78
  4.3 14.2 %collective-permute-start.1 = (bf16[2,128,256]{2,1,0:T(8,128)(2,1)S(1)}, bf16[2,128,256]{2,1,0:T(8,128)(2,1)S(1)}, u32[]{:S(2)}, u32[]{:S(2)}) collective-permute-start(bf16[2,128,256]{2,1,0:T(8,128)(2,1)S(1)} %get-tuple-element.42), channel_id=1, source_target_pairs={{0,6},{1,7},{2,4},{3,5},{4,2},{5,3},{6,0},{7,1},{8,14},{9,15},{10,... | collective-permute-start | bytes 393224 | tf_op jit(solution)/shard_map/ppermute | solution.py:78
  9.3 9.1 %collective-permute-start.2 = (bf16[2,128,256]{2,1,0:T(8,128)(2,1)S(1)}, bf16[2,128,256]{2,1,0:T(8,128)(2,1)S(1)}, u32[]{:S(2)}, u32[]{:S(2)}) collective-permute-start(bf16[2,128,256]{2,1,0:T(8,128)(2,1)S(1)} %get-tuple-element.45), channel_id=1, source_target_pairs={{0,2},{1,3},{2,0},{3,1},{4,6},{5,7},{6,4},{7,5},{8,10},{9,11},{10,... | collective-permute-start | bytes 393224 | tf_op jit(solution)/shard_map/ppermute | solution.py:78
  9.3 11.4 %collective-permute-start.3 = (bf16[2,128,256]{2,1,0:T(8,128)(2,1)S(1)}, bf16[2,128,256]{2,1,0:T(8,128)(2,1)S(1)}, u32[]{:S(2)}, u32[]{:S(2)}) collective-permute-start(bf16[2,128,256]{2,1,0:T(8,128)(2,1)S(1)} %get-tuple-element.46), channel_id=1, source_target_pairs={{0,4},{1,5},{2,6},{3,7},{4,0},{5,1},{6,2},{7,3},{8,12},{9,13},{10,... | collective-permute-start | bytes 393224 | tf_op jit(solution)/shard_map/ppermute | solution.py:78
  10.0 1.2 %copy-start = (bf16[16,128,256]{2,1,0:T(8,128)(2,1)S(1)}, bf16[16,128,256]{2,1,0:T(8,128)(2,1)}, u32[]{:S(2)}) copy-start(bf16[16,128,256]{2,1,0:T(8,128)(2,1)} %refs_3_.1) | copy-start | bytes 3145732
  11.2 0.9 %copy-start.1 = (bf16[256,256]{1,0:T(8,128)(2,1)S(1)}, bf16[256,256]{1,0:T(8,128)(2,1)}, u32[]{:S(2)}) copy-start(bf16[256,256]{1,0:T(8,128)(2,1)} %w_self.1) | copy-start | bytes 393220
  12.1 1.0 %copy-start.2 = (bf16[1,64,32,128]{3,2,1,0:T(8,128)(2,1)S(1)}, bf16[1,64,32,128]{3,2,1,0:T(8,128)(2,1)}, u32[]{:S(2)}) copy-start(bf16[1,64,32,128]{3,2,1,0:T(8,128)(2,1)} %refs_2_.1) | copy-start | bytes 1572868
  13.1 0.9 %copy-start.3 = (bf16[16,32,256]{2,1,0:T(8,128)(2,1)S(1)}, bf16[16,32,256]{2,1,0:T(8,128)(2,1)}, u32[]{:S(2)}) copy-start(bf16[16,32,256]{2,1,0:T(8,128)(2,1)} %refs_6_.1) | copy-start | bytes 786436
  14.1 0.9 %copy-start.4 = (bf16[256,256]{1,0:T(8,128)(2,1)S(1)}, bf16[256,256]{1,0:T(8,128)(2,1)}, u32[]{:S(2)}) copy-start(bf16[256,256]{1,0:T(8,128)(2,1)} %refs_5_.1) | copy-start | bytes 393220
  15.0 0.7 %copy-start.7 = (s32[1,64]{1,0:T(1,128)S(1)}, s32[1,64]{1,0:T(1,128)}, u32[]{:S(2)}) copy-start(s32[1,64]{1,0:T(1,128)} %refs_0_.1) | copy-start | bytes 772
  15.7 0.7 %copy-start.8 = (s32[1,64]{1,0:T(1,128)S(1)}, s32[1,64]{1,0:T(1,128)}, u32[]{:S(2)}) copy-start(s32[1,64]{1,0:T(1,128)} %refs_1_.1) | copy-start | bytes 772
  22.0 1.8 %collective-permute-start.4 = (bf16[784,256]{1,0:T(8,128)(2,1)S(1)}, bf16[784,256]{1,0:T(8,128)(2,1)S(1)}, u32[]{:S(2)}, u32[]{:S(2)}) collective-permute-start(bf16[784,256]{1,0:T(8,128)(2,1)S(1)} %get-tuple-element.49), channel_id=1, source_target_pairs={{0,1},{1,0},{2,3},{3,2},{4,5},{5,4},{6,7},{7,6},{8,9},{9,8},{10,11... | collective-permute-start | bytes 1204232 | tf_op jit(solution)/shard_map/ppermute | solution.py:78
  23.9 7.3 %collective-permute-start.5 = (bf16[336,256]{1,0:T(8,128)(2,1)S(1)}, bf16[336,256]{1,0:T(8,128)(2,1)S(1)}, u32[]{:S(2)}, u32[]{:S(2)}) collective-permute-start(bf16[336,256]{1,0:T(8,128)(2,1)S(1)} %get-tuple-element.51), channel_id=1, source_target_pairs={{0,8},{8,0},{16,24},{24,16},{1,9},{9,1},{17,25},{25,17},{2,10},{10... | collective-permute-start | bytes 516104 | tf_op jit(solution)/shard_map/ppermute | solution.py:78
  25.5 9.8 %collective-permute-start.6 = (bf16[336,256]{1,0:T(8,128)(2,1)S(1)}, bf16[336,256]{1,0:T(8,128)(2,1)S(1)}, u32[]{:S(2)}, u32[]{:S(2)}) collective-permute-start(bf16[336,256]{1,0:T(8,128)(2,1)S(1)} %get-tuple-element.52), channel_id=1, source_target_pairs={{0,16},{8,24},{16,0},{24,8},{1,17},{9,25},{17,1},{25,9},{2,18},{10... | collective-permute-start | bytes 516104 | tf_op jit(solution)/shard_map/ppermute | solution.py:78
  27.0 8.3 %collective-permute-start.7 = (bf16[336,256]{1,0:T(8,128)(2,1)S(1)}, bf16[336,256]{1,0:T(8,128)(2,1)S(1)}, u32[]{:S(2)}, u32[]{:S(2)}) collective-permute-start(bf16[336,256]{1,0:T(8,128)(2,1)S(1)} %get-tuple-element.53), channel_id=1, source_target_pairs={{0,24},{8,16},{16,8},{24,0},{1,25},{9,17},{17,9},{25,1},{2,26},{10... | collective-permute-start | bytes 516104 | tf_op jit(solution)/shard_map/ppermute | solution.py:78
  35.4 6.6 %collective-permute-start.8 = (bf16[144,256]{1,0:T(8,128)(2,1)S(1)}, bf16[144,256]{1,0:T(8,128)(2,1)S(1)}, u32[]{:S(2)}, u32[]{:S(2)}) collective-permute-start(bf16[144,256]{1,0:T(8,128)(2,1)S(1)} %get-tuple-element.61), channel_id=1, source_target_pairs={{0,6},{1,7},{2,4},{3,5},{4,2},{5,3},{6,0},{7,1},{8,14},{9,15},{10,... | collective-permute-start | bytes 221192 | tf_op jit(solution)/shard_map/ppermute | solution.py:78
  38.0 5.8 %collective-permute-start.9 = (bf16[144,256]{1,0:T(8,128)(2,1)S(1)}, bf16[144,256]{1,0:T(8,128)(2,1)S(1)}, u32[]{:S(2)}, u32[]{:S(2)}) collective-permute-start(bf16[144,256]{1,0:T(8,128)(2,1)S(1)} %get-tuple-element.65), channel_id=1, source_target_pairs={{0,2},{1,3},{2,0},{3,1},{4,6},{5,7},{6,4},{7,5},{8,10},{9,11},{10,... | collective-permute-start | bytes 221192 | tf_op jit(solution)/shard_map/ppermute | solution.py:78
  38.0 5.8 %collective-permute-start.10 = (bf16[144,256]{1,0:T(8,128)(2,1)S(1)}, bf16[144,256]{1,0:T(8,128)(2,1)S(1)}, u32[]{:S(2)}, u32[]{:S(2)}) collective-permute-start(bf16[144,256]{1,0:T(8,128)(2,1)S(1)} %get-tuple-element.66), channel_id=1, source_target_pairs={{0,4},{1,5},{2,6},{3,7},{4,0},{5,1},{6,2},{7,3},{8,12},{9,13},{10,... | collective-permute-start | bytes 221192 | tf_op jit(solution)/shard_map/ppermute | solution.py:78
  43.7 4.9 %collective-permute-start.13 = (bf16[64,256]{1,0:T(8,128)(2,1)S(1)}, bf16[64,256]{1,0:T(8,128)(2,1)S(1)}, u32[]{:S(2)}, u32[]{:S(2)}) collective-permute-start(bf16[64,256]{1,0:T(8,128)(2,1)S(1)} %piece.1.refs_0_), channel_id=1, source_target_pairs={{0,24},{8,16},{16,8},{24,0},{1,25},{9,17},{17,9},{25,1},{2,26},{10... | collective-permute-start | bytes 98312 | tf_op jit(solution)/shard_map/ppermute | solution.py:78
  45.2 3.9 %collective-permute-start.12 = (bf16[64,256]{1,0:T(8,128)(2,1)S(1)}, bf16[64,256]{1,0:T(8,128)(2,1)S(1)}, u32[]{:S(2)}, u32[]{:S(2)}) collective-permute-start(bf16[64,256]{1,0:T(8,128)(2,1)S(1)} %piece.1.refs_0_), channel_id=1, source_target_pairs={{0,16},{8,24},{16,0},{24,8},{1,17},{9,25},{17,1},{25,9},{2,18},{10... | collective-permute-start | bytes 98312 | tf_op jit(solution)/shard_map/ppermute | solution.py:78
  46.7 3.9 %collective-permute-start.11 = (bf16[64,256]{1,0:T(8,128)(2,1)S(1)}, bf16[64,256]{1,0:T(8,128)(2,1)S(1)}, u32[]{:S(2)}, u32[]{:S(2)}) collective-permute-start(bf16[64,256]{1,0:T(8,128)(2,1)S(1)} %piece.1.refs_0_), channel_id=1, source_target_pairs={{0,8},{8,0},{16,24},{24,16},{1,9},{9,1},{17,25},{25,17},{2,10},{10... | collective-permute-start | bytes 98312 | tf_op jit(solution)/shard_map/ppermute | solution.py:78
  50.6 1.4 %collective-permute-start.14 = (bf16[256,256]{1,0:T(8,128)(2,1)S(1)}, bf16[256,256]{1,0:T(8,128)(2,1)S(1)}, u32[]{:S(2)}, u32[]{:S(2)}) collective-permute-start(bf16[256,256]{1,0:T(8,128)(2,1)S(1)} %gather_pieces.1.mine), channel_id=1, source_target_pairs={{0,1},{1,0},{2,3},{3,2},{4,5},{5,4},{6,7},{7,6},{8,9},{9,8},{10,11... | collective-permute-start | bytes 393224 | tf_op jit(solution)/shard_map/ppermute | solution.py:78

commit v6 on v5

--- a/solution.py
+++ b/solution.py
@@ -74,6 +74,32 @@
     return jnp.sum(rows.astype(F32), axis=0, keepdims=True)
 
 
+def split_halves(row):
+    lanes = row.shape[1] // 2
+    high = row.astype(BF16).astype(F32)
+    low = row - high
+    place = lax.broadcasted_iota(jnp.int32, (PAD, lanes), 0)
+    spread = jnp.zeros((PAD, lanes), F32)
+    for i, part in enumerate((high[:, :lanes], high[:, lanes:], low[:, :lanes], low[:, lanes:])):
+        spread = jnp.where(place == i, part, spread)
+    return spread.astype(BF16)
+
+
+def join_halves(rows):
+    rows = rows.astype(F32)
+    place = lax.broadcasted_iota(jnp.int32, rows.shape, 0)
+    left = jnp.sum(jnp.where(place % 2 == 0, rows, 0.0), axis=0, keepdims=True)
+    right = jnp.sum(jnp.where(place % 2 == 1, rows, 0.0), axis=0, keepdims=True)
+    return jnp.concatenate([left, right], axis=1)
+
+
+def put(message, start, block):
+    rows = (message.shape[0] - PAD) // 2
+    count, lanes = block.shape[0], message.shape[1]
+    message[start : start + count] = block[:, :lanes]
+    message[rows + start : rows + start + count] = block[:, lanes:]
+
+
 def swap(array, axis, size, distance):
     return lax.ppermute(array, axis, [(i, i ^ distance) for i in range(size)])
 
@@ -207,50 +233,62 @@
     rep = lax.axis_index("rep")
     grads = slice(base, base + features)
     gradients[...] = (keep[grads].astype(F32) + got[grads].astype(F32)).astype(BF16)
-    bias_rows = split_rows(join_rows(keep[base + features :]) + join_rows(got[base + features :]))
+    bias_rows = split_halves(
+        join_rows(keep[base + features :]) + join_rows(got[base + features :])
+    )
     for k, message in enumerate(messages):
         target = rep ^ k
         for z in range(zs):
             place = pl.ds(pl.multiple_of(z * width + target * quarter, quarter), quarter)
             start = 2 * z * quarter
-            message[start : start + quarter] = keep[place, :]
-            message[start + quarter : start + 2 * quarter] = got[place, :]
-        message[end : end + share] = gradients[aligned(target, share), :]
-        message[end + share :] = bias_rows
+            put(message, start, keep[place, :])
+            put(message, start + quarter, got[place, :])
+        put(message, end, gradients[aligned(target, share), :])
+        message[2 * (end + share) :] = bias_rows
 
 
 def rep_sum_kernel(zs, *refs):
     arrived, parcels = refs[:-zs], refs[-zs:]
-    rows = (arrived[0].shape[0] - parcels[0].shape[0]) // (zs - 1)
-    share = parcels[0].shape[0] - PAD - rows
-    end = zs * rows
-    grads = sum(a[end : end + share].astype(F32) for a in arrived).astype(BF16)
-    bias_rows = split_rows(butterfly_sum([join_rows(a[end + share :]) for a in arrived]))
-    for k, parcel in enumerate(parcels):
-        place = slice(k * rows, (k + 1) * rows)
-        parcel[:rows] = sum(a[place].astype(F32) for a in arrived).astype(BF16)
-        parcel[rows : rows + share] = grads
-        parcel[rows + share :] = bias_rows
+    taken, given = (arrived[0].shape[0] - PAD) // 2, (parcels[0].shape[0] - PAD) // 2
+    rows = (taken - given) // (zs - 1)
+    bias_rows = split_halves(butterfly_sum([join_halves(a[2 * taken :]) for a in arrived]))
+    for side in range(2):
+        grads = slice(side * taken + zs * rows, (side + 1) * taken)
+        grads = sum(a[grads].astype(F32) for a in arrived).astype(BF16)
+        for k, parcel in enumerate(parcels):
+            place = slice(side * taken + k * rows, side * taken + (k + 1) * rows)
+            start = side * given
+            parcel[start : start + rows] = sum(a[place].astype(F32) for a in arrived).astype(BF16)
+            parcel[start + rows : start + given] = grads
+    for parcel in parcels:
+        parcel[2 * given :] = bias_rows
 
 
 def piece_kernel(*refs):
     arrived, piece = refs[:-1], refs[-1]
-    share = piece.shape[0]
-    base = arrived[0].shape[0] - PAD - share
-    piece[...] = butterfly_sum([a[base : base + share].astype(F32) for a in arrived]).astype(BF16)
+    share, lanes = piece.shape[0], arrived[0].shape[1]
+    given = (arrived[0].shape[0] - PAD) // 2
+    for side in range(2):
+        place = slice((side + 1) * given - share, (side + 1) * given)
+        total = butterfly_sum([a[place].astype(F32) for a in arrived])
+        piece[:, side * lanes : (side + 1) * lanes] = total.astype(BF16)
 
 
 def finish_kernel(requests_in, self_term, *refs):
     arrived, (feat_grad, grad_bias, total, requests) = refs[:-4], refs[-4:]
     pltpu.sync_copy(requests_in, requests)
-    grad_bias[...] = butterfly_sum([join_rows(a[a.shape[0] - PAD :]) for a in arrived])
-    quarter = total.shape[1]
+    grad_bias[...] = butterfly_sum([join_halves(a[a.shape[0] - PAD :]) for a in arrived])
+    quarter, lanes = total.shape[1], arrived[0].shape[1]
+    given = (arrived[0].shape[0] - PAD) // 2
     blk = lax.axis_index("blk")
     total[...] = self_term[...].reshape(total.shape)
     for k, message in enumerate(arrived):
         for other in range(2):
             block = requests[0, blk ^ (2 * k + other)]
-            total[block] += message[other * quarter : (other + 1) * quarter].astype(F32)
+            for side in range(2):
+                start = side * given + other * quarter
+                part = message[start : start + quarter].astype(F32)
+                total[block, :, side * lanes : (side + 1) * lanes] += part
     feat_grad[...] = total[...].astype(BF16)
 
 
@@ -328,7 +366,7 @@
     messages = call(
         lambda *refs: assemble_kernel(zs, *refs),
         [VMEM, VMEM],
-        (struct((2 * zs * quarter + share + PAD, features), BF16),) * replicas,
+        (struct((2 * (2 * zs * quarter + share) + PAD, features // 2), BF16),) * replicas,
         (VMEM,) * replicas,
         (pltpu.VMEM((features, features), BF16),),
         name="assemble",
@@ -348,7 +386,7 @@
     parcels = call(
         lambda *refs: rep_sum_kernel(zs, *refs),
         [VMEM] * replicas,
-        (struct((2 * quarter + share + PAD, features), BF16),) * zs,
+        (struct((2 * (2 * quarter + share) + PAD, features // 2), BF16),) * zs,
         (VMEM,) * zs,
         name="rep_sum",
     )(*arrived)

time: 53.3 us -> 52.9 us (level)
  transfers between devices with their start and end apart: 15 -> 15, of which waited for: 10 -> 11; matrix products, arithmetic and copies ran while one was open for 0% -> 0% of each run, Pallas kernels for 8% -> 8%
where the time goes in v6:
time: 52.9 us; the launch traced here: 52.5 us
  waiting for transfers between devices  18.7 us (35%)
  starting transfers between devices  17.9 us (34%)
  Pallas kernels  8.2 us (16%)
  local copies, waits for them, and re-layouts  6.99 us (13%)
  between operations  0.74 us (1%)
    ppermute x15, waiting for transfers between devices, swap(): return lax.ppermute(array, axis, [(i, i ^ distance) for i in range(size)])  18.7 us
    ppermute x15, starting transfers between devices, swap(): return lax.ppermute(array, axis, [(i, i ^ distance) for i in range(size)])  17.9 us
    pallas_call x11, Pallas kernels, run(): pl.pallas_call(body, in_specs=in_specs, out_shape=out_shape, out_specs=ou...  8.2 us
    unnamed x18, local copies, waits for them, and re-layouts  6.99 us
  transfers between devices with their start and end apart: 15, of which 11 were waited for; matrix products, arithmetic and copies ran while one was open for 0% of the time, Pallas kernels for 8%

profile of v6, /device:TPU:0, one launch (start us, length us, event | category | flops | bytes accessed | tf_op | source)
XLA Modules:
  0.0 52.5 jit_solution(16909526201758221054)
XLA Ops:
  0.6 0.6 %copy-done.5 = s32[1,8]{1,0:T(1,128)S(1)} copy-done((s32[1,8]{1,0:T(1,128)S(1)}, s32[1,8]{1,0:T(1,128)}, u32[]{:S(2)}) %copy-start.5) | copy-done | bytes 56
  1.3 1.3 %pick.1 = (bf16[4,128,256]{2,1,0:T(8,128)(2,1)S(1)}, bf16[4,128,256]{2,1,0:T(8,128)(2,1)S(1)}) custom-call(s32[1,8]{1,0:T(1,128)S(1)} %copy-done.5, bf16[16,128,256]{2,1,0:T(8,128)(2,1)} %refs_3_.1), custom_call_target="tpu_custom_call" | custom-call | bytes 1572896 | tf_op jit(solution)/shard_map/pick/pallas_call | solution.py:28
  3.1 1.2 %collective-permute-done.got = bf16[4,128,256]{2,1,0:T(8,128)(2,1)S(1)} collective-permute-done((bf16[4,128,256]{2,1,0:T(8,128)(2,1)S(1)}, bf16[4,128,256]{2,1,0:T(8,128)(2,1)S(1)}, u32[]{:S(2)}, u32[]{:S(2)}) %collective-permute-start) | collective-permute-done | bytes 262176 | tf_op jit(solution)/shard_map/ppermute | solution.py:104
  4.3 5.0 %collective-permute-start.1 = (bf16[2,128,256]{2,1,0:T(8,128)(2,1)S(1)}, bf16[2,128,256]{2,1,0:T(8,128)(2,1)S(1)}, u32[]{:S(2)}, u32[]{:S(2)}) collective-permute-start(bf16[2,128,256]{2,1,0:T(8,128)(2,1)S(1)} %get-tuple-element.42), channel_id=1, source_target_pairs={{0,6},{1,7},{2,4},{3,5},{4,2},{5,3},{6,0},{7,1},{8,14},{9,15},{10,... | collective-permute-start | bytes 393224 | tf_op jit(solution)/shard_map/ppermute | solution.py:104
  9.3 0.6 %collective-permute-start.3 = (bf16[2,128,256]{2,1,0:T(8,128)(2,1)S(1)}, bf16[2,128,256]{2,1,0:T(8,128)(2,1)S(1)}, u32[]{:S(2)}, u32[]{:S(2)}) collective-permute-start(bf16[2,128,256]{2,1,0:T(8,128)(2,1)S(1)} %get-tuple-element.46), channel_id=1, source_target_pairs={{0,4},{1,5},{2,6},{3,7},{4,0},{5,1},{6,2},{7,3},{8,12},{9,13},{10,... | collective-permute-start | bytes 393224 | tf_op jit(solution)/shard_map/ppermute | solution.py:104
  10.0 1.2 %copy-done = bf16[16,128,256]{2,1,0:T(8,128)(2,1)S(1)} copy-done((bf16[16,128,256]{2,1,0:T(8,128)(2,1)S(1)}, bf16[16,128,256]{2,1,0:T(8,128)(2,1)}, u32[]{:S(2)}) %copy-start) | copy-done | bytes 1048600
  11.2 0.9 %copy-done.1 = bf16[256,256]{1,0:T(8,128)(2,1)S(1)} copy-done((bf16[256,256]{1,0:T(8,128)(2,1)S(1)}, bf16[256,256]{1,0:T(8,128)(2,1)}, u32[]{:S(2)}) %copy-start.1) | copy-done | bytes 131096
  12.1 1.0 %copy-done.2 = bf16[1,64,32,128]{3,2,1,0:T(8,128)(2,1)S(1)} copy-done((bf16[1,64,32,128]{3,2,1,0:T(8,128)(2,1)S(1)}, bf16[1,64,32,128]{3,2,1,0:T(8,128)(2,1)}, u32[]{:S(2)}) %copy-start.2) | copy-done | bytes 524312
  13.1 0.9 %copy-done.3 = bf16[16,32,256]{2,1,0:T(8,128)(2,1)S(1)} copy-done((bf16[16,32,256]{2,1,0:T(8,128)(2,1)S(1)}, bf16[16,32,256]{2,1,0:T(8,128)(2,1)}, u32[]{:S(2)}) %copy-start.3) | copy-done | bytes 262168
  14.1 0.9 %copy-done.4 = bf16[256,256]{1,0:T(8,128)(2,1)S(1)} copy-done((bf16[256,256]{1,0:T(8,128)(2,1)S(1)}, bf16[256,256]{1,0:T(8,128)(2,1)}, u32[]{:S(2)}) %copy-start.4) | copy-done | bytes 131096
  15.0 0.7 %copy-done.7 = s32[1,64]{1,0:T(1,128)S(1)} copy-done((s32[1,64]{1,0:T(1,128)S(1)}, s32[1,64]{1,0:T(1,128)}, u32[]{:S(2)}) %copy-start.7) | copy-done | bytes 280
  15.7 0.7 %copy-done.8 = s32[1,64]{1,0:T(1,128)S(1)} copy-done((s32[1,64]{1,0:T(1,128)S(1)}, s32[1,64]{1,0:T(1,128)}, u32[]{:S(2)}) %copy-start.8) | copy-done | bytes 280
  16.3 2.1 %prepare.1.refs_0_ = bf16[6,512,512]{2,1,0:T(8,128)(2,1)S(1)} custom-call(s32[1,64]{1,0:T(1,128)S(1)} %copy-done.7, s32[1,64]{1,0:T(1,128)S(1)} %copy-done.8, bf16[1,64,32,128]{3,2,1,0:T(8,128)(2,1)S(1)} %copy-done.2, bf16[16,128,256]{2,1,0:T(8,128)(2,1)S(1)} %copy-done, bf16[256,256]{1,0:T(8,128)(2,1)S(1)} %copy-done.1, bf16[256,256]{1,0:T(8,128)(2,1)S(1)} %copy-done.4, ...), custom_call_target="tpu_custom_call" | custom-call | bytes 5243392 | tf_op jit(solution)/shard_map/prepare/pallas_call | solution.py:28
  18.5 2.2 %collective-permute-done.3.refs_4_ = bf16[2,128,256]{2,1,0:T(8,128)(2,1)S(1)} collective-permute-done((bf16[2,128,256]{2,1,0:T(8,128)(2,1)S(1)}, bf16[2,128,256]{2,1,0:T(8,128)(2,1)S(1)}, u32[]{:S(2)}, u32[]{:S(2)}) %collective-permute-start.3) | collective-permute-done | bytes 131104 | tf_op jit(solution)/shard_map/ppermute | solution.py:104
  20.7 1.3 %layer.1 = (f32[512,256]{1,0:T(8,128)S(1)}, bf16[512,256]{1,0:T(8,128)(2,1)S(1)}, bf16[784,256]{1,0:T(8,128)(2,1)S(1)}, bf16[784,256]{1,0:T(8,128)(2,1)S(1)}) custom-call(bf16[6,512,512]{2,1,0:T(8,128)(2,1)S(1)} %prepare.1.refs_0_, f32[1,256]{1,0:T(1,128)S(1)} %bitcast.2, bf16[2,128,256]{2,1,0:T(8,128)(2,1)S(1)} %get-tuple-element.44.refs_2_, ...), custom_call_target="tpu_custom_call" | custom-call | flops 536870912 | bytes 5260288 | tf_op jit(solution)/shard_map/layer/pallas_call | solution.py:28
  22.1 1.7 %collective-permute-done.4.refs_1_ = bf16[784,256]{1,0:T(8,128)(2,1)S(1)} collective-permute-done((bf16[784,256]{1,0:T(8,128)(2,1)S(1)}, bf16[784,256]{1,0:T(8,128)(2,1)S(1)}, u32[]{:S(2)}, u32[]{:S(2)}) %collective-permute-start.4) | collective-permute-done | bytes 401440 | tf_op jit(solution)/shard_map/ppermute | solution.py:104
  24.0 1.6 %collective-permute-start.5 = (bf16[656,128]{1,0:T(8,128)(2,1)S(1)}, bf16[656,128]{1,0:T(8,128)(2,1)S(1)}, u32[]{:S(2)}, u32[]{:S(2)}) collective-permute-start(bf16[656,128]{1,0:T(8,128)(2,1)S(1)} %get-tuple-element.51), channel_id=1, source_target_pairs={{0,8},{8,0},{16,24},{24,16},{1,9},{9,1},{17,25},{25,17},{2,10},{10... | collective-permute-start | bytes 503816 | tf_op jit(solution)/shard_map/ppermute | solution.py:104
  25.6 1.5 %collective-permute-start.6 = (bf16[656,128]{1,0:T(8,128)(2,1)S(1)}, bf16[656,128]{1,0:T(8,128)(2,1)S(1)}, u32[]{:S(2)}, u32[]{:S(2)}) collective-permute-start(bf16[656,128]{1,0:T(8,128)(2,1)S(1)} %get-tuple-element.52), channel_id=1, source_target_pairs={{0,16},{8,24},{16,0},{24,8},{1,17},{9,25},{17,1},{25,9},{2,18},{10... | collective-permute-start | bytes 503816 | tf_op jit(solution)/shard_map/ppermute | solution.py:104
  27.6 1.0 %own.1 = (bf16[16,32,256]{2,1,0:T(8,128)(2,1)}, f32[512,256]{1,0:T(8,128)S(1)}) custom-call(f32[512,256]{1,0:T(8,128)S(1)} %get-tuple-element.54.preact, bf16[512,256]{1,0:T(8,128)(2,1)S(1)} %get-tuple-element.55.grad_pre, bf16[256,256]{1,0:T(8,128)(2,1)S(1)} %copy-done.1), custom_call_target="tpu_custom_call" | custom-call | flops 67108864 | bytes 1703936 | tf_op jit(solution)/shard_map/own/pallas_call | solution.py:28
  28.5 2.7 %collective-permute-done.5.refs_1_ = bf16[656,128]{1,0:T(8,128)(2,1)S(1)} collective-permute-done((bf16[656,128]{1,0:T(8,128)(2,1)S(1)}, bf16[656,128]{1,0:T(8,128)(2,1)S(1)}, u32[]{:S(2)}, u32[]{:S(2)}) %collective-permute-start.5) | collective-permute-done | bytes 167968 | tf_op jit(solution)/shard_map/ppermute | solution.py:104
  31.2 4.0 %collective-permute-done.6.refs_2_ = bf16[656,128]{1,0:T(8,128)(2,1)S(1)} collective-permute-done((bf16[656,128]{1,0:T(8,128)(2,1)S(1)}, bf16[656,128]{1,0:T(8,128)(2,1)S(1)}, u32[]{:S(2)}, u32[]{:S(2)}) %collective-permute-start.6) | collective-permute-done | bytes 167968 | tf_op jit(solution)/shard_map/ppermute | solution.py:104
  35.3 2.5 %collective-permute-start.8 = (bf16[272,128]{1,0:T(8,128)(2,1)S(1)}, bf16[272,128]{1,0:T(8,128)(2,1)S(1)}, u32[]{:S(2)}, u32[]{:S(2)}) collective-permute-start(bf16[272,128]{1,0:T(8,128)(2,1)S(1)} %get-tuple-element.61), channel_id=1, source_target_pairs={{0,6},{1,7},{2,4},{3,5},{4,2},{5,3},{6,0},{7,1},{8,14},{9,15},{10,... | collective-permute-start | bytes 208904 | tf_op jit(solution)/shard_map/ppermute | solution.py:104
  37.9 1.9 %collective-permute-start.10 = (bf16[272,128]{1,0:T(8,128)(2,1)S(1)}, bf16[272,128]{1,0:T(8,128)(2,1)S(1)}, u32[]{:S(2)}, u32[]{:S(2)}) collective-permute-start(bf16[272,128]{1,0:T(8,128)(2,1)S(1)} %get-tuple-element.66), channel_id=1, source_target_pairs={{0,4},{1,5},{2,6},{3,7},{4,0},{5,1},{6,2},{7,3},{8,12},{9,13},{10,... | collective-permute-start | bytes 208904 | tf_op jit(solution)/shard_map/ppermute | solution.py:104
  39.8 2.1 %collective-permute-done.8.refs_3_ = bf16[272,128]{1,0:T(8,128)(2,1)S(1)} collective-permute-done((bf16[272,128]{1,0:T(8,128)(2,1)S(1)}, bf16[272,128]{1,0:T(8,128)(2,1)S(1)}, u32[]{:S(2)}, u32[]{:S(2)}) %collective-permute-start.8) | collective-permute-done | bytes 69664 | tf_op jit(solution)/shard_map/ppermute | solution.py:104
  41.8 1.3 %collective-permute-done.9.refs_1_ = bf16[272,128]{1,0:T(8,128)(2,1)S(1)} collective-permute-done((bf16[272,128]{1,0:T(8,128)(2,1)S(1)}, bf16[272,128]{1,0:T(8,128)(2,1)S(1)}, u32[]{:S(2)}, u32[]{:S(2)}) %collective-permute-start.9) | collective-permute-done | bytes 69664 | tf_op jit(solution)/shard_map/ppermute | solution.py:104
  43.4 1.5 %collective-permute-start.13 = (bf16[64,256]{1,0:T(8,128)(2,1)S(1)}, bf16[64,256]{1,0:T(8,128)(2,1)S(1)}, u32[]{:S(2)}, u32[]{:S(2)}) collective-permute-start(bf16[64,256]{1,0:T(8,128)(2,1)S(1)} %piece.1.refs_0_), channel_id=1, source_target_pairs={{0,24},{8,16},{16,8},{24,0},{1,25},{9,17},{17,9},{25,1},{2,26},{10... | collective-permute-start | bytes 98312 | tf_op jit(solution)/shard_map/ppermute | solution.py:104
  44.9 1.5 %collective-permute-start.12 = (bf16[64,256]{1,0:T(8,128)(2,1)S(1)}, bf16[64,256]{1,0:T(8,128)(2,1)S(1)}, u32[]{:S(2)}, u32[]{:S(2)}) collective-permute-start(bf16[64,256]{1,0:T(8,128)(2,1)S(1)} %piece.1.refs_0_), channel_id=1, source_target_pairs={{0,16},{8,24},{16,0},{24,8},{1,17},{9,25},{17,1},{25,9},{2,18},{10... | collective-permute-start | bytes 98312 | tf_op jit(solution)/shard_map/ppermute | solution.py:104
  46.3 0.6 %collective-permute-start.11 = (bf16[64,256]{1,0:T(8,128)(2,1)S(1)}, bf16[64,256]{1,0:T(8,128)(2,1)S(1)}, u32[]{:S(2)}, u32[]{:S(2)}) collective-permute-start(bf16[64,256]{1,0:T(8,128)(2,1)S(1)} %piece.1.refs_0_), channel_id=1, source_target_pairs={{0,8},{8,0},{16,24},{24,16},{1,9},{9,1},{17,25},{25,17},{2,10},{10... | collective-permute-start | bytes 98312 | tf_op jit(solution)/shard_map/ppermute | solution.py:104
  46.9 1.3 %collective-permute-done.13.refs_3_ = bf16[64,256]{1,0:T(8,128)(2,1)S(1)} collective-permute-done((bf16[64,256]{1,0:T(8,128)(2,1)S(1)}, bf16[64,256]{1,0:T(8,128)(2,1)S(1)}, u32[]{:S(2)}, u32[]{:S(2)}) %collective-permute-start.13) | collective-permute-done | bytes 32800 | tf_op jit(solution)/shard_map/ppermute | solution.py:104
  48.8 1.5 %collective-permute-done.11.refs_1_ = bf16[64,256]{1,0:T(8,128)(2,1)S(1)} collective-permute-done((bf16[64,256]{1,0:T(8,128)(2,1)S(1)}, bf16[64,256]{1,0:T(8,128)(2,1)S(1)}, u32[]{:S(2)}, u32[]{:S(2)}) %collective-permute-start.11) | collective-permute-done | bytes 32800 | tf_op jit(solution)/shard_map/ppermute | solution.py:104
  50.4 1.3 %finish.1 = (bf16[16,32,256]{2,1,0:T(8,128)(2,1)}, f32[1,256]{1,0:T(1,128)}) custom-call(s32[1,8]{1,0:T(1,128)S(1)} %copy-done.5, f32[512,256]{1,0:T(8,128)S(1)} %get-tuple-element.68.self_term, bf16[272,128]{1,0:T(8,128)(2,1)S(1)} %get-tuple-element.64.refs_0_, bf16[272,128]{1,0:T(8,128)(2,1)S(1)} %collective-permute-done.9.refs_1_, ...), custom_call_target="tpu_custom_call" | custom-call | bytes 1066016 | tf_op jit(solution)/shard_map/finish/pallas_call | solution.py:28
  51.7 0.8 %widen.1 = (f32[256,256]{1,0:T(8,128)}, f32[256,256]{1,0:T(8,128)}) custom-call(bf16[256,256]{1,0:T(8,128)(2,1)S(1)} %gather_pieces.1.mine, bf16[256,256]{1,0:T(8,128)(2,1)S(1)} %collective-permute-done.14.other), custom_call_target="tpu_custom_call" | custom-call | bytes 786432 | tf_op jit(solution)/shard_map/widen/pallas_call | solution.py:28
  (27 shorter events, 2.2 us)
Async XLA Ops:
  0.6 0.7 %copy-start.5 = (s32[1,8]{1,0:T(1,128)S(1)}, s32[1,8]{1,0:T(1,128)}, u32[]{:S(2)}) copy-start(s32[1,8]{1,0:T(1,128)} %requests_in.3) | copy-start | bytes 100
  2.6 18.1 %copy-start.6 = (f32[256]{0:T(256)S(1)}, f32[256]{0:T(256)}, u32[]{:S(2)}) copy-start(f32[256]{0:T(256)} %param.16) | copy-start | bytes 3076
  2.6 1.7 %collective-permute-start = (bf16[4,128,256]{2,1,0:T(8,128)(2,1)S(1)}, bf16[4,128,256]{2,1,0:T(8,128)(2,1)S(1)}, u32[]{:S(2)}, u32[]{:S(2)}) collective-permute-start(bf16[4,128,256]{2,1,0:T(8,128)(2,1)S(1)} %get-tuple-element.41), channel_id=1, source_target_pairs={{0,1},{1,0},{2,3},{3,2},{4,5},{5,4},{6,7},{7,6},{8,9},{9,8},{10,11... | collective-permute-start | bytes 786440 | tf_op jit(solution)/shard_map/ppermute | solution.py:104
  4.3 14.2 %collective-permute-start.1 = (bf16[2,128,256]{2,1,0:T(8,128)(2,1)S(1)}, bf16[2,128,256]{2,1,0:T(8,128)(2,1)S(1)}, u32[]{:S(2)}, u32[]{:S(2)}) collective-permute-start(bf16[2,128,256]{2,1,0:T(8,128)(2,1)S(1)} %get-tuple-element.42), channel_id=1, source_target_pairs={{0,6},{1,7},{2,4},{3,5},{4,2},{5,3},{6,0},{7,1},{8,14},{9,15},{10,... | collective-permute-start | bytes 393224 | tf_op jit(solution)/shard_map/ppermute | solution.py:104
  9.3 9.1 %collective-permute-start.2 = (bf16[2,128,256]{2,1,0:T(8,128)(2,1)S(1)}, bf16[2,128,256]{2,1,0:T(8,128)(2,1)S(1)}, u32[]{:S(2)}, u32[]{:S(2)}) collective-permute-start(bf16[2,128,256]{2,1,0:T(8,128)(2,1)S(1)} %get-tuple-element.45), channel_id=1, source_target_pairs={{0,2},{1,3},{2,0},{3,1},{4,6},{5,7},{6,4},{7,5},{8,10},{9,11},{10,... | collective-permute-start | bytes 393224 | tf_op jit(solution)/shard_map/ppermute | solution.py:104
  9.3 11.4 %collective-permute-start.3 = (bf16[2,128,256]{2,1,0:T(8,128)(2,1)S(1)}, bf16[2,128,256]{2,1,0:T(8,128)(2,1)S(1)}, u32[]{:S(2)}, u32[]{:S(2)}) collective-permute-start(bf16[2,128,256]{2,1,0:T(8,128)(2,1)S(1)} %get-tuple-element.46), channel_id=1, source_target_pairs={{0,4},{1,5},{2,6},{3,7},{4,0},{5,1},{6,2},{7,3},{8,12},{9,13},{10,... | collective-permute-start | bytes 393224 | tf_op jit(solution)/shard_map/ppermute | solution.py:104
  10.0 1.2 %copy-start = (bf16[16,128,256]{2,1,0:T(8,128)(2,1)S(1)}, bf16[16,128,256]{2,1,0:T(8,128)(2,1)}, u32[]{:S(2)}) copy-start(bf16[16,128,256]{2,1,0:T(8,128)(2,1)} %refs_3_.1) | copy-start | bytes 3145732
  11.2 0.9 %copy-start.1 = (bf16[256,256]{1,0:T(8,128)(2,1)S(1)}, bf16[256,256]{1,0:T(8,128)(2,1)}, u32[]{:S(2)}) copy-start(bf16[256,256]{1,0:T(8,128)(2,1)} %w_self.1) | copy-start | bytes 393220
  12.1 1.0 %copy-start.2 = (bf16[1,64,32,128]{3,2,1,0:T(8,128)(2,1)S(1)}, bf16[1,64,32,128]{3,2,1,0:T(8,128)(2,1)}, u32[]{:S(2)}) copy-start(bf16[1,64,32,128]{3,2,1,0:T(8,128)(2,1)} %refs_2_.1) | copy-start | bytes 1572868
  13.1 0.9 %copy-start.3 = (bf16[16,32,256]{2,1,0:T(8,128)(2,1)S(1)}, bf16[16,32,256]{2,1,0:T(8,128)(2,1)}, u32[]{:S(2)}) copy-start(bf16[16,32,256]{2,1,0:T(8,128)(2,1)} %refs_6_.1) | copy-start | bytes 786436
  14.1 0.9 %copy-start.4 = (bf16[256,256]{1,0:T(8,128)(2,1)S(1)}, bf16[256,256]{1,0:T(8,128)(2,1)}, u32[]{:S(2)}) copy-start(bf16[256,256]{1,0:T(8,128)(2,1)} %refs_5_.1) | copy-start | bytes 393220
  15.0 0.7 %copy-start.7 = (s32[1,64]{1,0:T(1,128)S(1)}, s32[1,64]{1,0:T(1,128)}, u32[]{:S(2)}) copy-start(s32[1,64]{1,0:T(1,128)} %refs_0_.1) | copy-start | bytes 772
  15.7 0.7 %copy-start.8 = (s32[1,64]{1,0:T(1,128)S(1)}, s32[1,64]{1,0:T(1,128)}, u32[]{:S(2)}) copy-start(s32[1,64]{1,0:T(1,128)} %refs_1_.1) | copy-start | bytes 772
  22.0 1.8 %collective-permute-start.4 = (bf16[784,256]{1,0:T(8,128)(2,1)S(1)}, bf16[784,256]{1,0:T(8,128)(2,1)S(1)}, u32[]{:S(2)}, u32[]{:S(2)}) collective-permute-start(bf16[784,256]{1,0:T(8,128)(2,1)S(1)} %get-tuple-element.49), channel_id=1, source_target_pairs={{0,1},{1,0},{2,3},{3,2},{4,5},{5,4},{6,7},{7,6},{8,9},{9,8},{10,11... | collective-permute-start | bytes 1204232 | tf_op jit(solution)/shard_map/ppermute | solution.py:104
  24.0 7.2 %collective-permute-start.5 = (bf16[656,128]{1,0:T(8,128)(2,1)S(1)}, bf16[656,128]{1,0:T(8,128)(2,1)S(1)}, u32[]{:S(2)}, u32[]{:S(2)}) collective-permute-start(bf16[656,128]{1,0:T(8,128)(2,1)S(1)} %get-tuple-element.51), channel_id=1, source_target_pairs={{0,8},{8,0},{16,24},{24,16},{1,9},{9,1},{17,25},{25,17},{2,10},{10... | collective-permute-start | bytes 503816 | tf_op jit(solution)/shard_map/ppermute | solution.py:104
  25.6 9.6 %collective-permute-start.6 = (bf16[656,128]{1,0:T(8,128)(2,1)S(1)}, bf16[656,128]{1,0:T(8,128)(2,1)S(1)}, u32[]{:S(2)}, u32[]{:S(2)}) collective-permute-start(bf16[656,128]{1,0:T(8,128)(2,1)S(1)} %get-tuple-element.52), channel_id=1, source_target_pairs={{0,16},{8,24},{16,0},{24,8},{1,17},{9,25},{17,1},{25,9},{2,18},{10... | collective-permute-start | bytes 503816 | tf_op jit(solution)/shard_map/ppermute | solution.py:104
  27.1 8.1 %collective-permute-start.7 = (bf16[656,128]{1,0:T(8,128)(2,1)S(1)}, bf16[656,128]{1,0:T(8,128)(2,1)S(1)}, u32[]{:S(2)}, u32[]{:S(2)}) collective-permute-start(bf16[656,128]{1,0:T(8,128)(2,1)S(1)} %get-tuple-element.53), channel_id=1, source_target_pairs={{0,24},{8,16},{16,8},{24,0},{1,25},{9,17},{17,9},{25,1},{2,26},{10... | collective-permute-start | bytes 503816 | tf_op jit(solution)/shard_map/ppermute | solution.py:104
  35.3 6.5 %collective-permute-start.8 = (bf16[272,128]{1,0:T(8,128)(2,1)S(1)}, bf16[272,128]{1,0:T(8,128)(2,1)S(1)}, u32[]{:S(2)}, u32[]{:S(2)}) collective-permute-start(bf16[272,128]{1,0:T(8,128)(2,1)S(1)} %get-tuple-element.61), channel_id=1, source_target_pairs={{0,6},{1,7},{2,4},{3,5},{4,2},{5,3},{6,0},{7,1},{8,14},{9,15},{10,... | collective-permute-start | bytes 208904 | tf_op jit(solution)/shard_map/ppermute | solution.py:104
  37.9 5.3 %collective-permute-start.9 = (bf16[272,128]{1,0:T(8,128)(2,1)S(1)}, bf16[272,128]{1,0:T(8,128)(2,1)S(1)}, u32[]{:S(2)}, u32[]{:S(2)}) collective-permute-start(bf16[272,128]{1,0:T(8,128)(2,1)S(1)} %get-tuple-element.65), channel_id=1, source_target_pairs={{0,2},{1,3},{2,0},{3,1},{4,6},{5,7},{6,4},{7,5},{8,10},{9,11},{10,... | collective-permute-start | bytes 208904 | tf_op jit(solution)/shard_map/ppermute | solution.py:104
  37.9 5.5 %collective-permute-start.10 = (bf16[272,128]{1,0:T(8,128)(2,1)S(1)}, bf16[272,128]{1,0:T(8,128)(2,1)S(1)}, u32[]{:S(2)}, u32[]{:S(2)}) collective-permute-start(bf16[272,128]{1,0:T(8,128)(2,1)S(1)} %get-tuple-element.66), channel_id=1, source_target_pairs={{0,4},{1,5},{2,6},{3,7},{4,0},{5,1},{6,2},{7,3},{8,12},{9,13},{10,... | collective-permute-start | bytes 208904 | tf_op jit(solution)/shard_map/ppermute | solution.py:104
  43.4 4.9 %collective-permute-start.13 = (bf16[64,256]{1,0:T(8,128)(2,1)S(1)}, bf16[64,256]{1,0:T(8,128)(2,1)S(1)}, u32[]{:S(2)}, u32[]{:S(2)}) collective-permute-start(bf16[64,256]{1,0:T(8,128)(2,1)S(1)} %piece.1.refs_0_), channel_id=1, source_target_pairs={{0,24},{8,16},{16,8},{24,0},{1,25},{9,17},{17,9},{25,1},{2,26},{10... | collective-permute-start | bytes 98312 | tf_op jit(solution)/shard_map/ppermute | solution.py:104
  44.9 3.9 %collective-permute-start.12 = (bf16[64,256]{1,0:T(8,128)(2,1)S(1)}, bf16[64,256]{1,0:T(8,128)(2,1)S(1)}, u32[]{:S(2)}, u32[]{:S(2)}) collective-permute-start(bf16[64,256]{1,0:T(8,128)(2,1)S(1)} %piece.1.refs_0_), channel_id=1, source_target_pairs={{0,16},{8,24},{16,0},{24,8},{1,17},{9,25},{17,1},{25,9},{2,18},{10... | collective-permute-start | bytes 98312 | tf_op jit(solution)/shard_map/ppermute | solution.py:104
  46.3 3.9 %collective-permute-start.11 = (bf16[64,256]{1,0:T(8,128)(2,1)S(1)}, bf16[64,256]{1,0:T(8,128)(2,1)S(1)}, u32[]{:S(2)}, u32[]{:S(2)}) collective-permute-start(bf16[64,256]{1,0:T(8,128)(2,1)S(1)} %piece.1.refs_0_), channel_id=1, source_target_pairs={{0,8},{8,0},{16,24},{24,16},{1,9},{9,1},{17,25},{25,17},{2,10},{10... | collective-permute-start | bytes 98312 | tf_op jit(solution)/shard_map/ppermute | solution.py:104
  50.3 1.4 %collective-permute-start.14 = (bf16[256,256]{1,0:T(8,128)(2,1)S(1)}, bf16[256,256]{1,0:T(8,128)(2,1)S(1)}, u32[]{:S(2)}, u32[]{:S(2)}) collective-permute-start(bf16[256,256]{1,0:T(8,128)(2,1)S(1)} %gather_pieces.1.mine), channel_id=1, source_target_pairs={{0,1},{1,0},{2,3},{3,2},{4,5},{5,4},{6,7},{7,6},{8,9},{9,8},{10,11... | collective-permute-start | bytes 393224 | tf_op jit(solution)/shard_map/ppermute | solution.py:104

commit v7 on v6

--- a/solution.py
+++ b/solution.py
@@ -100,6 +100,10 @@
     message[rows + start : rows + start + count] = block[:, lanes:]
 
 
+def flipped(k, zs):
+    return k // (zs // 2)
+
+
 def swap(array, axis, size, distance):
     return lax.ppermute(array, axis, [(i, i ^ distance) for i in range(size)])
 
@@ -111,14 +115,16 @@
     copy.wait()
     blk = lax.axis_index("blk")
     for k in range(keep.shape[0]):
-        keep[k] = held[requests[0, blk ^ (2 * k)]]
-        send[k] = held[requests[0, blk ^ (2 * k + 1)]]
+        flip = flipped(k, keep.shape[0])
+        keep[k] = held[requests[0, blk ^ (2 * k + flip)]]
+        send[k] = held[requests[0, blk ^ (2 * k + 1 - flip)]]
 
 
 def join_kernel(keep, got, *messages):
     for k, message in enumerate(messages):
-        message[0] = keep[k]
-        message[1] = got[k]
+        flip = flipped(k, len(messages))
+        message[flip] = keep[k]
+        message[1 - flip] = got[k]
 
 
 def prepare_kernel(
@@ -341,7 +347,9 @@
         (VMEM,) * zs,
         name="join",
     )(keep, got)
-    sources = [messages[0]] + [swap(messages[k], "blk", owners, 2 * k) for k in range(1, zs)]
+    sources = [messages[0]] + [
+        swap(messages[k], "blk", owners, 2 * k + flipped(k, zs)) for k in range(1, zs)
+    ]
     per_slab = row_count // width
     packed = call(
         lambda *refs: prepare_kernel(owners, *refs),
@@ -407,6 +415,7 @@
         name="finish",
     )(requests, self_term, *landed)
     pieces = [piece] + [swap(piece, "rep", replicas, k) for k in range(1, replicas)]
+    *pieces, feat_grad = lax.optimization_barrier((*pieces, feat_grad))
     whole = struct((features, features), F32)
     mine = call(
         gather_kernel,

time: 52.9 us -> 52.8 us (level)
  transfers between devices with their start and end apart: 15 -> 15, of which waited for: 11 -> 10; matrix products, arithmetic and copies ran while one was open for 0% -> 0% of each run, Pallas kernels for 8% -> 8%
where the time goes in v7:
time: 52.8 us; the launch traced here: 52.5 us
  waiting for transfers between devices  19.1 us (36%)
  starting transfers between devices  17.5 us (33%)
  Pallas kernels  8.2 us (16%)
  local copies, waits for them, and re-layouts  6.99 us (13%)
  between operations  0.73 us (1%)
    ppermute x15, waiting for transfers between devices, swap(): return lax.ppermute(array, axis, [(i, i ^ distance) for i in range(size)])  19.1 us
    ppermute x15, starting transfers between devices, swap(): return lax.ppermute(array, axis, [(i, i ^ distance) for i in range(size)])  17.5 us
    pallas_call x11, Pallas kernels, run(): pl.pallas_call(body, in_specs=in_specs, out_shape=out_shape, out_specs=ou...  8.2 us
    unnamed x18, local copies, waits for them, and re-layouts  6.99 us
  transfers between devices with their start and end apart: 15, of which 10 were waited for; matrix products, arithmetic and copies ran while one was open for 0% of the time, Pallas kernels for 8%

profile of v7, /device:TPU:0, one launch (start us, length us, event | category | flops | bytes accessed | tf_op | source)
XLA Modules:
  0.0 52.5 jit_solution(78974408907121088)
XLA Ops:
  0.6 0.6 %copy-done.5 = s32[1,8]{1,0:T(1,128)S(1)} copy-done((s32[1,8]{1,0:T(1,128)S(1)}, s32[1,8]{1,0:T(1,128)}, u32[]{:S(2)}) %copy-start.5) | copy-done | bytes 56
  1.3 1.3 %pick.1 = (bf16[4,128,256]{2,1,0:T(8,128)(2,1)S(1)}, bf16[4,128,256]{2,1,0:T(8,128)(2,1)S(1)}) custom-call(s32[1,8]{1,0:T(1,128)S(1)} %copy-done.5, bf16[16,128,256]{2,1,0:T(8,128)(2,1)} %refs_3_.1), custom_call_target="tpu_custom_call" | custom-call | bytes 1572896 | tf_op jit(solution)/shard_map/pick/pallas_call | solution.py:28
  2.6 0.5 collective-permute-start
  3.1 1.2 %collective-permute-done.got = bf16[4,128,256]{2,1,0:T(8,128)(2,1)S(1)} collective-permute-done((bf16[4,128,256]{2,1,0:T(8,128)(2,1)S(1)}, bf16[4,128,256]{2,1,0:T(8,128)(2,1)S(1)}, u32[]{:S(2)}, u32[]{:S(2)}) %collective-permute-start) | collective-permute-done | bytes 262176 | tf_op jit(solution)/shard_map/ppermute | solution.py:108
  4.3 4.8 %collective-permute-start.1 = (bf16[2,128,256]{2,1,0:T(8,128)(2,1)S(1)}, bf16[2,128,256]{2,1,0:T(8,128)(2,1)S(1)}, u32[]{:S(2)}, u32[]{:S(2)}) collective-permute-start(bf16[2,128,256]{2,1,0:T(8,128)(2,1)S(1)} %get-tuple-element.47), channel_id=1, source_target_pairs={{0,7},{1,6},{2,5},{3,4},{4,3},{5,2},{6,1},{7,0},{8,15},{9,14},{10,... | collective-permute-start | bytes 393224 | tf_op jit(solution)/shard_map/ppermute | solution.py:108
  9.4 1.2 %copy-done = bf16[16,128,256]{2,1,0:T(8,128)(2,1)S(1)} copy-done((bf16[16,128,256]{2,1,0:T(8,128)(2,1)S(1)}, bf16[16,128,256]{2,1,0:T(8,128)(2,1)}, u32[]{:S(2)}) %copy-start) | copy-done | bytes 1048600
  10.7 0.9 %copy-done.1 = bf16[256,256]{1,0:T(8,128)(2,1)S(1)} copy-done((bf16[256,256]{1,0:T(8,128)(2,1)S(1)}, bf16[256,256]{1,0:T(8,128)(2,1)}, u32[]{:S(2)}) %copy-start.1) | copy-done | bytes 131096
  11.6 1.0 %copy-done.2 = bf16[1,64,32,128]{3,2,1,0:T(8,128)(2,1)S(1)} copy-done((bf16[1,64,32,128]{3,2,1,0:T(8,128)(2,1)S(1)}, bf16[1,64,32,128]{3,2,1,0:T(8,128)(2,1)}, u32[]{:S(2)}) %copy-start.2) | copy-done | bytes 524312
  12.6 0.9 %copy-done.3 = bf16[16,32,256]{2,1,0:T(8,128)(2,1)S(1)} copy-done((bf16[16,32,256]{2,1,0:T(8,128)(2,1)S(1)}, bf16[16,32,256]{2,1,0:T(8,128)(2,1)}, u32[]{:S(2)}) %copy-start.3) | copy-done | bytes 262168
  13.6 0.9 %copy-done.4 = bf16[256,256]{1,0:T(8,128)(2,1)S(1)} copy-done((bf16[256,256]{1,0:T(8,128)(2,1)S(1)}, bf16[256,256]{1,0:T(8,128)(2,1)}, u32[]{:S(2)}) %copy-start.4) | copy-done | bytes 131096
  14.5 0.7 %copy-done.7 = s32[1,64]{1,0:T(1,128)S(1)} copy-done((s32[1,64]{1,0:T(1,128)S(1)}, s32[1,64]{1,0:T(1,128)}, u32[]{:S(2)}) %copy-start.7) | copy-done | bytes 280
  15.1 0.7 %copy-done.8 = s32[1,64]{1,0:T(1,128)S(1)} copy-done((s32[1,64]{1,0:T(1,128)S(1)}, s32[1,64]{1,0:T(1,128)}, u32[]{:S(2)}) %copy-start.8) | copy-done | bytes 280
  15.8 2.1 %prepare.1.refs_0_ = bf16[6,512,512]{2,1,0:T(8,128)(2,1)S(1)} custom-call(s32[1,64]{1,0:T(1,128)S(1)} %copy-done.7, s32[1,64]{1,0:T(1,128)S(1)} %copy-done.8, bf16[1,64,32,128]{3,2,1,0:T(8,128)(2,1)S(1)} %copy-done.2, bf16[16,128,256]{2,1,0:T(8,128)(2,1)S(1)} %copy-done, bf16[256,256]{1,0:T(8,128)(2,1)S(1)} %copy-done.1, bf16[256,256]{1,0:T(8,128)(2,1)S(1)} %copy-done.4, ...), custom_call_target="tpu_custom_call" | custom-call | bytes 5243392 | tf_op jit(solution)/shard_map/prepare/pallas_call | solution.py:28
  17.9 2.7 %collective-permute-done.3.refs_4_ = bf16[2,128,256]{2,1,0:T(8,128)(2,1)S(1)} collective-permute-done((bf16[2,128,256]{2,1,0:T(8,128)(2,1)S(1)}, bf16[2,128,256]{2,1,0:T(8,128)(2,1)S(1)}, u32[]{:S(2)}, u32[]{:S(2)}) %collective-permute-start.3) | collective-permute-done | bytes 131104 | tf_op jit(solution)/shard_map/ppermute | solution.py:108
  20.6 1.3 %layer.1 = (f32[512,256]{1,0:T(8,128)S(1)}, bf16[512,256]{1,0:T(8,128)(2,1)S(1)}, bf16[784,256]{1,0:T(8,128)(2,1)S(1)}, bf16[784,256]{1,0:T(8,128)(2,1)S(1)}) custom-call(bf16[6,512,512]{2,1,0:T(8,128)(2,1)S(1)} %prepare.1.refs_0_, f32[1,256]{1,0:T(1,128)S(1)} %bitcast.2, bf16[2,128,256]{2,1,0:T(8,128)(2,1)S(1)} %get-tuple-element.49.refs_2_, ...), custom_call_target="tpu_custom_call" | custom-call | flops 536870912 | bytes 5260288 | tf_op jit(solution)/shard_map/layer/pallas_call | solution.py:28
  22.2 1.6 %collective-permute-done.4.refs_1_ = bf16[784,256]{1,0:T(8,128)(2,1)S(1)} collective-permute-done((bf16[784,256]{1,0:T(8,128)(2,1)S(1)}, bf16[784,256]{1,0:T(8,128)(2,1)S(1)}, u32[]{:S(2)}, u32[]{:S(2)}) %collective-permute-start.4) | collective-permute-done | bytes 401440 | tf_op jit(solution)/shard_map/ppermute | solution.py:108
  23.9 1.6 %collective-permute-start.5 = (bf16[656,128]{1,0:T(8,128)(2,1)S(1)}, bf16[656,128]{1,0:T(8,128)(2,1)S(1)}, u32[]{:S(2)}, u32[]{:S(2)}) collective-permute-start(bf16[656,128]{1,0:T(8,128)(2,1)S(1)} %get-tuple-element.56), channel_id=1, source_target_pairs={{0,8},{8,0},{16,24},{24,16},{1,9},{9,1},{17,25},{25,17},{2,10},{10... | collective-permute-start | bytes 503816 | tf_op jit(solution)/shard_map/ppermute | solution.py:108
  25.5 1.5 %collective-permute-start.6 = (bf16[656,128]{1,0:T(8,128)(2,1)S(1)}, bf16[656,128]{1,0:T(8,128)(2,1)S(1)}, u32[]{:S(2)}, u32[]{:S(2)}) collective-permute-start(bf16[656,128]{1,0:T(8,128)(2,1)S(1)} %get-tuple-element.57), channel_id=1, source_target_pairs={{0,16},{8,24},{16,0},{24,8},{1,17},{9,25},{17,1},{25,9},{2,18},{10... | collective-permute-start | bytes 503816 | tf_op jit(solution)/shard_map/ppermute | solution.py:108
  27.5 1.0 %own.1 = (bf16[16,32,256]{2,1,0:T(8,128)(2,1)}, f32[512,256]{1,0:T(8,128)S(1)}) custom-call(f32[512,256]{1,0:T(8,128)S(1)} %get-tuple-element.59.preact, bf16[512,256]{1,0:T(8,128)(2,1)S(1)} %get-tuple-element.60.grad_pre, bf16[256,256]{1,0:T(8,128)(2,1)S(1)} %copy-done.1), custom_call_target="tpu_custom_call" | custom-call | flops 67108864 | bytes 1703936 | tf_op jit(solution)/shard_map/own/pallas_call | solution.py:28
  28.5 2.7 %collective-permute-done.5.refs_1_ = bf16[656,128]{1,0:T(8,128)(2,1)S(1)} collective-permute-done((bf16[656,128]{1,0:T(8,128)(2,1)S(1)}, bf16[656,128]{1,0:T(8,128)(2,1)S(1)}, u32[]{:S(2)}, u32[]{:S(2)}) %collective-permute-start.5) | collective-permute-done | bytes 167968 | tf_op jit(solution)/shard_map/ppermute | solution.py:108
  31.1 4.0 %collective-permute-done.6.refs_2_ = bf16[656,128]{1,0:T(8,128)(2,1)S(1)} collective-permute-done((bf16[656,128]{1,0:T(8,128)(2,1)S(1)}, bf16[656,128]{1,0:T(8,128)(2,1)S(1)}, u32[]{:S(2)}, u32[]{:S(2)}) %collective-permute-start.6) | collective-permute-done | bytes 167968 | tf_op jit(solution)/shard_map/ppermute | solution.py:108
  35.3 2.5 %collective-permute-start.8 = (bf16[272,128]{1,0:T(8,128)(2,1)S(1)}, bf16[272,128]{1,0:T(8,128)(2,1)S(1)}, u32[]{:S(2)}, u32[]{:S(2)}) collective-permute-start(bf16[272,128]{1,0:T(8,128)(2,1)S(1)} %get-tuple-element.66), channel_id=1, source_target_pairs={{0,6},{1,7},{2,4},{3,5},{4,2},{5,3},{6,0},{7,1},{8,14},{9,15},{10,... | collective-permute-start | bytes 208904 | tf_op jit(solution)/shard_map/ppermute | solution.py:108
  37.8 1.9 %collective-permute-start.10 = (bf16[272,128]{1,0:T(8,128)(2,1)S(1)}, bf16[272,128]{1,0:T(8,128)(2,1)S(1)}, u32[]{:S(2)}, u32[]{:S(2)}) collective-permute-start(bf16[272,128]{1,0:T(8,128)(2,1)S(1)} %get-tuple-element.71), channel_id=1, source_target_pairs={{0,4},{1,5},{2,6},{3,7},{4,0},{5,1},{6,2},{7,3},{8,12},{9,13},{10,... | collective-permute-start | bytes 208904 | tf_op jit(solution)/shard_map/ppermute | solution.py:108
  39.7 2.0 %collective-permute-done.8.refs_3_ = bf16[272,128]{1,0:T(8,128)(2,1)S(1)} collective-permute-done((bf16[272,128]{1,0:T(8,128)(2,1)S(1)}, bf16[272,128]{1,0:T(8,128)(2,1)S(1)}, u32[]{:S(2)}, u32[]{:S(2)}) %collective-permute-start.8) | collective-permute-done | bytes 69664 | tf_op jit(solution)/shard_map/ppermute | solution.py:108
  41.7 1.7 %collective-permute-done.9.refs_1_ = bf16[272,128]{1,0:T(8,128)(2,1)S(1)} collective-permute-done((bf16[272,128]{1,0:T(8,128)(2,1)S(1)}, bf16[272,128]{1,0:T(8,128)(2,1)S(1)}, u32[]{:S(2)}, u32[]{:S(2)}) %collective-permute-start.9) | collective-permute-done | bytes 69664 | tf_op jit(solution)/shard_map/ppermute | solution.py:108
  43.4 1.5 %collective-permute-start.13 = (bf16[64,256]{1,0:T(8,128)(2,1)S(1)}, bf16[64,256]{1,0:T(8,128)(2,1)S(1)}, u32[]{:S(2)}, u32[]{:S(2)}) collective-permute-start(bf16[64,256]{1,0:T(8,128)(2,1)S(1)} %piece.1.refs_0_), channel_id=1, source_target_pairs={{0,24},{8,16},{16,8},{24,0},{1,25},{9,17},{17,9},{25,1},{2,26},{10... | collective-permute-start | bytes 98312 | tf_op jit(solution)/shard_map/ppermute | solution.py:108
  44.9 1.4 %collective-permute-start.12 = (bf16[64,256]{1,0:T(8,128)(2,1)S(1)}, bf16[64,256]{1,0:T(8,128)(2,1)S(1)}, u32[]{:S(2)}, u32[]{:S(2)}) collective-permute-start(bf16[64,256]{1,0:T(8,128)(2,1)S(1)} %piece.1.refs_0_), channel_id=1, source_target_pairs={{0,16},{8,24},{16,0},{24,8},{1,17},{9,25},{17,1},{25,9},{2,18},{10... | collective-permute-start | bytes 98312 | tf_op jit(solution)/shard_map/ppermute | solution.py:108
  46.3 0.7 %collective-permute-start.11 = (bf16[64,256]{1,0:T(8,128)(2,1)S(1)}, bf16[64,256]{1,0:T(8,128)(2,1)S(1)}, u32[]{:S(2)}, u32[]{:S(2)}) collective-permute-start(bf16[64,256]{1,0:T(8,128)(2,1)S(1)} %piece.1.refs_0_), channel_id=1, source_target_pairs={{0,8},{8,0},{16,24},{24,16},{1,9},{9,1},{17,25},{25,17},{2,10},{10... | collective-permute-start | bytes 98312 | tf_op jit(solution)/shard_map/ppermute | solution.py:108
  47.0 1.3 %finish.1 = (bf16[16,32,256]{2,1,0:T(8,128)(2,1)}, f32[1,256]{1,0:T(1,128)}) custom-call(s32[1,8]{1,0:T(1,128)S(1)} %copy-done.5, f32[512,256]{1,0:T(8,128)S(1)} %get-tuple-element.73.self_term, bf16[272,128]{1,0:T(8,128)(2,1)S(1)} %get-tuple-element.69.refs_0_, bf16[272,128]{1,0:T(8,128)(2,1)S(1)} %collective-permute-done.9.refs_1_, ...), custom_call_target="tpu_custom_call" | custom-call | bytes 1066016 | tf_op jit(solution)/shard_map/finish/pallas_call | solution.py:28
  48.8 1.4 %collective-permute-done.11.refs_1_ = bf16[64,256]{1,0:T(8,128)(2,1)S(1)} collective-permute-done((bf16[64,256]{1,0:T(8,128)(2,1)S(1)}, bf16[64,256]{1,0:T(8,128)(2,1)S(1)}, u32[]{:S(2)}, u32[]{:S(2)}) %collective-permute-start.11) | collective-permute-done | bytes 32800 | tf_op jit(solution)/shard_map/ppermute | solution.py:108
  50.3 1.3 %collective-permute-done.14.other = bf16[256,256]{1,0:T(8,128)(2,1)S(1)} collective-permute-done((bf16[256,256]{1,0:T(8,128)(2,1)S(1)}, bf16[256,256]{1,0:T(8,128)(2,1)S(1)}, u32[]{:S(2)}, u32[]{:S(2)}) %collective-permute-start.14) | collective-permute-done | bytes 131104 | tf_op jit(solution)/shard_map/ppermute | solution.py:108
  51.7 0.8 %widen.1 = (f32[256,256]{1,0:T(8,128)}, f32[256,256]{1,0:T(8,128)}) custom-call(bf16[256,256]{1,0:T(8,128)(2,1)S(1)} %gather_pieces.1.mine, bf16[256,256]{1,0:T(8,128)(2,1)S(1)} %collective-permute-done.14.other), custom_call_target="tpu_custom_call" | custom-call | bytes 786432 | tf_op jit(solution)/shard_map/widen/pallas_call | solution.py:28
  (27 shorter events, 2.0 us)
Async XLA Ops:
  0.6 0.7 %copy-start.5 = (s32[1,8]{1,0:T(1,128)S(1)}, s32[1,8]{1,0:T(1,128)}, u32[]{:S(2)}) copy-start(s32[1,8]{1,0:T(1,128)} %requests_in.3) | copy-start | bytes 100
  2.6 18.1 %copy-start.6 = (f32[256]{0:T(256)S(1)}, f32[256]{0:T(256)}, u32[]{:S(2)}) copy-start(f32[256]{0:T(256)} %param.16) | copy-start | bytes 3076
  2.6 1.7 %collective-permute-start = (bf16[4,128,256]{2,1,0:T(8,128)(2,1)S(1)}, bf16[4,128,256]{2,1,0:T(8,128)(2,1)S(1)}, u32[]{:S(2)}, u32[]{:S(2)}) collective-permute-start(bf16[4,128,256]{2,1,0:T(8,128)(2,1)S(1)} %get-tuple-element.46), channel_id=1, source_target_pairs={{0,1},{1,0},{2,3},{3,2},{4,5},{5,4},{6,7},{7,6},{8,9},{9,8},{10,11... | collective-permute-start | bytes 786440 | tf_op jit(solution)/shard_map/ppermute | solution.py:108
  4.3 13.6 %collective-permute-start.1 = (bf16[2,128,256]{2,1,0:T(8,128)(2,1)S(1)}, bf16[2,128,256]{2,1,0:T(8,128)(2,1)S(1)}, u32[]{:S(2)}, u32[]{:S(2)}) collective-permute-start(bf16[2,128,256]{2,1,0:T(8,128)(2,1)S(1)} %get-tuple-element.47), channel_id=1, source_target_pairs={{0,7},{1,6},{2,5},{3,4},{4,3},{5,2},{6,1},{7,0},{8,15},{9,14},{10,... | collective-permute-start | bytes 393224 | tf_op jit(solution)/shard_map/ppermute | solution.py:108
  9.1 8.9 %collective-permute-start.2 = (bf16[2,128,256]{2,1,0:T(8,128)(2,1)S(1)}, bf16[2,128,256]{2,1,0:T(8,128)(2,1)S(1)}, u32[]{:S(2)}, u32[]{:S(2)}) collective-permute-start(bf16[2,128,256]{2,1,0:T(8,128)(2,1)S(1)} %get-tuple-element.50), channel_id=1, source_target_pairs={{0,2},{1,3},{2,0},{3,1},{4,6},{5,7},{6,4},{7,5},{8,10},{9,11},{10,... | collective-permute-start | bytes 393224 | tf_op jit(solution)/shard_map/ppermute | solution.py:108
  9.1 11.6 %collective-permute-start.3 = (bf16[2,128,256]{2,1,0:T(8,128)(2,1)S(1)}, bf16[2,128,256]{2,1,0:T(8,128)(2,1)S(1)}, u32[]{:S(2)}, u32[]{:S(2)}) collective-permute-start(bf16[2,128,256]{2,1,0:T(8,128)(2,1)S(1)} %get-tuple-element.51), channel_id=1, source_target_pairs={{0,5},{1,4},{2,7},{3,6},{4,1},{5,0},{6,3},{7,2},{8,13},{9,12},{10,... | collective-permute-start | bytes 393224 | tf_op jit(solution)/shard_map/ppermute | solution.py:108
  9.4 1.2 %copy-start = (bf16[16,128,256]{2,1,0:T(8,128)(2,1)S(1)}, bf16[16,128,256]{2,1,0:T(8,128)(2,1)}, u32[]{:S(2)}) copy-start(bf16[16,128,256]{2,1,0:T(8,128)(2,1)} %refs_3_.1) | copy-start | bytes 3145732
  10.7 0.9 %copy-start.1 = (bf16[256,256]{1,0:T(8,128)(2,1)S(1)}, bf16[256,256]{1,0:T(8,128)(2,1)}, u32[]{:S(2)}) copy-start(bf16[256,256]{1,0:T(8,128)(2,1)} %w_self.1) | copy-start | bytes 393220
  11.6 1.0 %copy-start.2 = (bf16[1,64,32,128]{3,2,1,0:T(8,128)(2,1)S(1)}, bf16[1,64,32,128]{3,2,1,0:T(8,128)(2,1)}, u32[]{:S(2)}) copy-start(bf16[1,64,32,128]{3,2,1,0:T(8,128)(2,1)} %refs_2_.1) | copy-start | bytes 1572868
  12.6 0.9 %copy-start.3 = (bf16[16,32,256]{2,1,0:T(8,128)(2,1)S(1)}, bf16[16,32,256]{2,1,0:T(8,128)(2,1)}, u32[]{:S(2)}) copy-start(bf16[16,32,256]{2,1,0:T(8,128)(2,1)} %refs_6_.1) | copy-start | bytes 786436
  13.6 0.9 %copy-start.4 = (bf16[256,256]{1,0:T(8,128)(2,1)S(1)}, bf16[256,256]{1,0:T(8,128)(2,1)}, u32[]{:S(2)}) copy-start(bf16[256,256]{1,0:T(8,128)(2,1)} %refs_5_.1) | copy-start | bytes 393220
  14.5 0.7 %copy-start.7 = (s32[1,64]{1,0:T(1,128)S(1)}, s32[1,64]{1,0:T(1,128)}, u32[]{:S(2)}) copy-start(s32[1,64]{1,0:T(1,128)} %refs_0_.1) | copy-start | bytes 772
  15.1 0.7 %copy-start.8 = (s32[1,64]{1,0:T(1,128)S(1)}, s32[1,64]{1,0:T(1,128)}, u32[]{:S(2)}) copy-start(s32[1,64]{1,0:T(1,128)} %refs_1_.1) | copy-start | bytes 772
  22.0 1.8 %collective-permute-start.4 = (bf16[784,256]{1,0:T(8,128)(2,1)S(1)}, bf16[784,256]{1,0:T(8,128)(2,1)S(1)}, u32[]{:S(2)}, u32[]{:S(2)}) collective-permute-start(bf16[784,256]{1,0:T(8,128)(2,1)S(1)} %get-tuple-element.54), channel_id=1, source_target_pairs={{0,1},{1,0},{2,3},{3,2},{4,5},{5,4},{6,7},{7,6},{8,9},{9,8},{10,11... | collective-permute-start | bytes 1204232 | tf_op jit(solution)/shard_map/ppermute | solution.py:108
  23.9 7.2 %collective-permute-start.5 = (bf16[656,128]{1,0:T(8,128)(2,1)S(1)}, bf16[656,128]{1,0:T(8,128)(2,1)S(1)}, u32[]{:S(2)}, u32[]{:S(2)}) collective-permute-start(bf16[656,128]{1,0:T(8,128)(2,1)S(1)} %get-tuple-element.56), channel_id=1, source_target_pairs={{0,8},{8,0},{16,24},{24,16},{1,9},{9,1},{17,25},{25,17},{2,10},{10... | collective-permute-start | bytes 503816 | tf_op jit(solution)/shard_map/ppermute | solution.py:108
  25.5 9.6 %collective-permute-start.6 = (bf16[656,128]{1,0:T(8,128)(2,1)S(1)}, bf16[656,128]{1,0:T(8,128)(2,1)S(1)}, u32[]{:S(2)}, u32[]{:S(2)}) collective-permute-start(bf16[656,128]{1,0:T(8,128)(2,1)S(1)} %get-tuple-element.57), channel_id=1, source_target_pairs={{0,16},{8,24},{16,0},{24,8},{1,17},{9,25},{17,1},{25,9},{2,18},{10... | collective-permute-start | bytes 503816 | tf_op jit(solution)/shard_map/ppermute | solution.py:108
  27.0 8.1 %collective-permute-start.7 = (bf16[656,128]{1,0:T(8,128)(2,1)S(1)}, bf16[656,128]{1,0:T(8,128)(2,1)S(1)}, u32[]{:S(2)}, u32[]{:S(2)}) collective-permute-start(bf16[656,128]{1,0:T(8,128)(2,1)S(1)} %get-tuple-element.58), channel_id=1, source_target_pairs={{0,24},{8,16},{16,8},{24,0},{1,25},{9,17},{17,9},{25,1},{2,26},{10... | collective-permute-start | bytes 503816 | tf_op jit(solution)/shard_map/ppermute | solution.py:108
  35.3 6.5 %collective-permute-start.8 = (bf16[272,128]{1,0:T(8,128)(2,1)S(1)}, bf16[272,128]{1,0:T(8,128)(2,1)S(1)}, u32[]{:S(2)}, u32[]{:S(2)}) collective-permute-start(bf16[272,128]{1,0:T(8,128)(2,1)S(1)} %get-tuple-element.66), channel_id=1, source_target_pairs={{0,6},{1,7},{2,4},{3,5},{4,2},{5,3},{6,0},{7,1},{8,14},{9,15},{10,... | collective-permute-start | bytes 208904 | tf_op jit(solution)/shard_map/ppermute | solution.py:108
  37.8 5.6 %collective-permute-start.9 = (bf16[272,128]{1,0:T(8,128)(2,1)S(1)}, bf16[272,128]{1,0:T(8,128)(2,1)S(1)}, u32[]{:S(2)}, u32[]{:S(2)}) collective-permute-start(bf16[272,128]{1,0:T(8,128)(2,1)S(1)} %get-tuple-element.70), channel_id=1, source_target_pairs={{0,2},{1,3},{2,0},{3,1},{4,6},{5,7},{6,4},{7,5},{8,10},{9,11},{10,... | collective-permute-start | bytes 208904 | tf_op jit(solution)/shard_map/ppermute | solution.py:108
  37.8 5.6 %collective-permute-start.10 = (bf16[272,128]{1,0:T(8,128)(2,1)S(1)}, bf16[272,128]{1,0:T(8,128)(2,1)S(1)}, u32[]{:S(2)}, u32[]{:S(2)}) collective-permute-start(bf16[272,128]{1,0:T(8,128)(2,1)S(1)} %get-tuple-element.71), channel_id=1, source_target_pairs={{0,4},{1,5},{2,6},{3,7},{4,0},{5,1},{6,2},{7,3},{8,12},{9,13},{10,... | collective-permute-start | bytes 208904 | tf_op jit(solution)/shard_map/ppermute | solution.py:108
  43.4 4.9 %collective-permute-start.13 = (bf16[64,256]{1,0:T(8,128)(2,1)S(1)}, bf16[64,256]{1,0:T(8,128)(2,1)S(1)}, u32[]{:S(2)}, u32[]{:S(2)}) collective-permute-start(bf16[64,256]{1,0:T(8,128)(2,1)S(1)} %piece.1.refs_0_), channel_id=1, source_target_pairs={{0,24},{8,16},{16,8},{24,0},{1,25},{9,17},{17,9},{25,1},{2,26},{10... | collective-permute-start | bytes 98312 | tf_op jit(solution)/shard_map/ppermute | solution.py:108
  44.9 3.9 %collective-permute-start.12 = (bf16[64,256]{1,0:T(8,128)(2,1)S(1)}, bf16[64,256]{1,0:T(8,128)(2,1)S(1)}, u32[]{:S(2)}, u32[]{:S(2)}) collective-permute-start(bf16[64,256]{1,0:T(8,128)(2,1)S(1)} %piece.1.refs_0_), channel_id=1, source_target_pairs={{0,16},{8,24},{16,0},{24,8},{1,17},{9,25},{17,1},{25,9},{2,18},{10... | collective-permute-start | bytes 98312 | tf_op jit(solution)/shard_map/ppermute | solution.py:108
  46.3 3.9 %collective-permute-start.11 = (bf16[64,256]{1,0:T(8,128)(2,1)S(1)}, bf16[64,256]{1,0:T(8,128)(2,1)S(1)}, u32[]{:S(2)}, u32[]{:S(2)}) collective-permute-start(bf16[64,256]{1,0:T(8,128)(2,1)S(1)} %piece.1.refs_0_), channel_id=1, source_target_pairs={{0,8},{8,0},{16,24},{24,16},{1,9},{9,1},{17,25},{25,17},{2,10},{10... | collective-permute-start | bytes 98312 | tf_op jit(solution)/shard_map/ppermute | solution.py:108
  50.2 1.4 %collective-permute-start.14 = (bf16[256,256]{1,0:T(8,128)(2,1)S(1)}, bf16[256,256]{1,0:T(8,128)(2,1)S(1)}, u32[]{:S(2)}, u32[]{:S(2)}) collective-permute-start(bf16[256,256]{1,0:T(8,128)(2,1)S(1)} %gather_pieces.1.mine), channel_id=1, source_target_pairs={{0,1},{1,0},{2,3},{3,2},{4,5},{5,4},{6,7},{7,6},{8,9},{9,8},{10,11... | collective-permute-start | bytes 393224 | tf_op jit(solution)/shard_map/ppermute | solution.py:108

commit v8 on v7

--- a/solution.py
+++ b/solution.py
@@ -306,13 +306,16 @@
         out[aligned(rep ^ k, share), :] = piece[...]
 
 
-def widen_kernel(mine, other, grad_self, grad_neigh):
-    core = lax.axis_index("blk") % 2
-    first = core == 0
-    a = mine[...].astype(F32)
-    b = other[...].astype(F32)
-    grad_self[...] = jnp.where(first, a, b)
-    grad_neigh[...] = jnp.where(first, b, a)
+def widen_kernel(mine, other, grad_self, grad_neigh, held, sems):
+    first = lax.axis_index("blk") % 2 == 0
+    a, b = mine[...], other[...]
+    copies = []
+    for i, (out, like, unlike) in enumerate(((grad_self, a, b), (grad_neigh, b, a))):
+        held[i] = jnp.where(first, like, unlike).astype(F32)
+        copies.append(pltpu.make_async_copy(held.at[i], out, sems.at[i]))
+        copies[i].start()
+    for copy in copies:
+        copy.wait()
 
 
 def on_device(feats, requests, tile_dest, tile_slot, tile_vals, w_self, w_neigh, bias, cotangent):
@@ -427,7 +430,12 @@
     other = swap(mine, "blk", owners, 1)
     other, feat_grad = lax.optimization_barrier((other, feat_grad))
     grad_self, grad_neigh = call(
-        widen_kernel, [VMEM, VMEM], (whole, whole), (VMEM, VMEM), name="widen"
+        widen_kernel,
+        [VMEM, VMEM],
+        (whole, whole),
+        (HBM, HBM),
+        (pltpu.VMEM((2, features, features), F32), pltpu.SemaphoreType.DMA((2,))),
+        name="widen",
     )(mine, other)
     return (hidden, grad_self, grad_neigh, grad_bias.reshape(features), feat_grad)
 

time: 52.8 us -> 52.8 us (level)
  no operation moved by 1% of the time
where the time goes in v8:
time: 52.8 us; the launch traced here: 52.5 us
  waiting for transfers between devices  19.1 us (36%)
  starting transfers between devices  17.5 us (33%)
  Pallas kernels  8.2 us (16%)
  local copies, waits for them, and re-layouts  6.99 us (13%)
  between operations  0.73 us (1%)
    ppermute x15, waiting for transfers between devices, swap(): return lax.ppermute(array, axis, [(i, i ^ distance) for i in range(size)])  19.1 us
    ppermute x15, starting transfers between devices, swap(): return lax.ppermute(array, axis, [(i, i ^ distance) for i in range(size)])  17.5 us
    pallas_call x11, Pallas kernels, run(): pl.pallas_call(body, in_specs=in_specs, out_shape=out_shape, out_specs=ou...  8.2 us
    unnamed x18, local copies, waits for them, and re-layouts  6.99 us
  transfers between devices with their start and end apart: 15, of which 10 were waited for; matrix products, arithmetic and copies ran while one was open for 0% of the time, Pallas kernels for 8%

profile of v8, /device:TPU:0, one launch (start us, length us, event | category | flops | bytes accessed | tf_op | source)
XLA Modules:
  0.0 52.5 jit_solution(6943678090608383463)
XLA Ops:
  0.6 0.6 %copy-done.5 = s32[1,8]{1,0:T(1,128)S(1)} copy-done((s32[1,8]{1,0:T(1,128)S(1)}, s32[1,8]{1,0:T(1,128)}, u32[]{:S(2)}) %copy-start.5) | copy-done | bytes 56
  1.3 1.3 %pick.1 = (bf16[4,128,256]{2,1,0:T(8,128)(2,1)S(1)}, bf16[4,128,256]{2,1,0:T(8,128)(2,1)S(1)}) custom-call(s32[1,8]{1,0:T(1,128)S(1)} %copy-done.5, bf16[16,128,256]{2,1,0:T(8,128)(2,1)} %refs_3_.1), custom_call_target="tpu_custom_call" | custom-call | bytes 1572896 | tf_op jit(solution)/shard_map/pick/pallas_call | solution.py:28
  2.6 0.5 collective-permute-start
  3.1 1.2 %collective-permute-done.got = bf16[4,128,256]{2,1,0:T(8,128)(2,1)S(1)} collective-permute-done((bf16[4,128,256]{2,1,0:T(8,128)(2,1)S(1)}, bf16[4,128,256]{2,1,0:T(8,128)(2,1)S(1)}, u32[]{:S(2)}, u32[]{:S(2)}) %collective-permute-start) | collective-permute-done | bytes 262176 | tf_op jit(solution)/shard_map/ppermute | solution.py:108
  4.3 4.8 %collective-permute-start.1 = (bf16[2,128,256]{2,1,0:T(8,128)(2,1)S(1)}, bf16[2,128,256]{2,1,0:T(8,128)(2,1)S(1)}, u32[]{:S(2)}, u32[]{:S(2)}) collective-permute-start(bf16[2,128,256]{2,1,0:T(8,128)(2,1)S(1)} %get-tuple-element.47), channel_id=1, source_target_pairs={{0,7},{1,6},{2,5},{3,4},{4,3},{5,2},{6,1},{7,0},{8,15},{9,14},{10,... | collective-permute-start | bytes 393224 | tf_op jit(solution)/shard_map/ppermute | solution.py:108
  9.4 1.2 %copy-done = bf16[16,128,256]{2,1,0:T(8,128)(2,1)S(1)} copy-done((bf16[16,128,256]{2,1,0:T(8,128)(2,1)S(1)}, bf16[16,128,256]{2,1,0:T(8,128)(2,1)}, u32[]{:S(2)}) %copy-start) | copy-done | bytes 1048600
  10.7 0.9 %copy-done.1 = bf16[256,256]{1,0:T(8,128)(2,1)S(1)} copy-done((bf16[256,256]{1,0:T(8,128)(2,1)S(1)}, bf16[256,256]{1,0:T(8,128)(2,1)}, u32[]{:S(2)}) %copy-start.1) | copy-done | bytes 131096
  11.6 1.0 %copy-done.2 = bf16[1,64,32,128]{3,2,1,0:T(8,128)(2,1)S(1)} copy-done((bf16[1,64,32,128]{3,2,1,0:T(8,128)(2,1)S(1)}, bf16[1,64,32,128]{3,2,1,0:T(8,128)(2,1)}, u32[]{:S(2)}) %copy-start.2) | copy-done | bytes 524312
  12.6 0.9 %copy-done.3 = bf16[16,32,256]{2,1,0:T(8,128)(2,1)S(1)} copy-done((bf16[16,32,256]{2,1,0:T(8,128)(2,1)S(1)}, bf16[16,32,256]{2,1,0:T(8,128)(2,1)}, u32[]{:S(2)}) %copy-start.3) | copy-done | bytes 262168
  13.6 0.9 %copy-done.4 = bf16[256,256]{1,0:T(8,128)(2,1)S(1)} copy-done((bf16[256,256]{1,0:T(8,128)(2,1)S(1)}, bf16[256,256]{1,0:T(8,128)(2,1)}, u32[]{:S(2)}) %copy-start.4) | copy-done | bytes 131096
  14.5 0.7 %copy-done.7 = s32[1,64]{1,0:T(1,128)S(1)} copy-done((s32[1,64]{1,0:T(1,128)S(1)}, s32[1,64]{1,0:T(1,128)}, u32[]{:S(2)}) %copy-start.7) | copy-done | bytes 280
  15.1 0.7 %copy-done.8 = s32[1,64]{1,0:T(1,128)S(1)} copy-done((s32[1,64]{1,0:T(1,128)S(1)}, s32[1,64]{1,0:T(1,128)}, u32[]{:S(2)}) %copy-start.8) | copy-done | bytes 280
  15.8 2.1 %prepare.1.refs_0_ = bf16[6,512,512]{2,1,0:T(8,128)(2,1)S(1)} custom-call(s32[1,64]{1,0:T(1,128)S(1)} %copy-done.7, s32[1,64]{1,0:T(1,128)S(1)} %copy-done.8, bf16[1,64,32,128]{3,2,1,0:T(8,128)(2,1)S(1)} %copy-done.2, bf16[16,128,256]{2,1,0:T(8,128)(2,1)S(1)} %copy-done, bf16[256,256]{1,0:T(8,128)(2,1)S(1)} %copy-done.1, bf16[256,256]{1,0:T(8,128)(2,1)S(1)} %copy-done.4, ...), custom_call_target="tpu_custom_call" | custom-call | bytes 5243392 | tf_op jit(solution)/shard_map/prepare/pallas_call | solution.py:28
  17.9 2.7 %collective-permute-done.3.refs_4_ = bf16[2,128,256]{2,1,0:T(8,128)(2,1)S(1)} collective-permute-done((bf16[2,128,256]{2,1,0:T(8,128)(2,1)S(1)}, bf16[2,128,256]{2,1,0:T(8,128)(2,1)S(1)}, u32[]{:S(2)}, u32[]{:S(2)}) %collective-permute-start.3) | collective-permute-done | bytes 131104 | tf_op jit(solution)/shard_map/ppermute | solution.py:108
  20.6 1.3 %layer.1 = (f32[512,256]{1,0:T(8,128)S(1)}, bf16[512,256]{1,0:T(8,128)(2,1)S(1)}, bf16[784,256]{1,0:T(8,128)(2,1)S(1)}, bf16[784,256]{1,0:T(8,128)(2,1)S(1)}) custom-call(bf16[6,512,512]{2,1,0:T(8,128)(2,1)S(1)} %prepare.1.refs_0_, f32[1,256]{1,0:T(1,128)S(1)} %bitcast.2, bf16[2,128,256]{2,1,0:T(8,128)(2,1)S(1)} %get-tuple-element.49.refs_2_, ...), custom_call_target="tpu_custom_call" | custom-call | flops 536870912 | bytes 5260288 | tf_op jit(solution)/shard_map/layer/pallas_call | solution.py:28
  22.2 1.6 %collective-permute-done.4.refs_1_ = bf16[784,256]{1,0:T(8,128)(2,1)S(1)} collective-permute-done((bf16[784,256]{1,0:T(8,128)(2,1)S(1)}, bf16[784,256]{1,0:T(8,128)(2,1)S(1)}, u32[]{:S(2)}, u32[]{:S(2)}) %collective-permute-start.4) | collective-permute-done | bytes 401440 | tf_op jit(solution)/shard_map/ppermute | solution.py:108
  23.9 1.6 %collective-permute-start.5 = (bf16[656,128]{1,0:T(8,128)(2,1)S(1)}, bf16[656,128]{1,0:T(8,128)(2,1)S(1)}, u32[]{:S(2)}, u32[]{:S(2)}) collective-permute-start(bf16[656,128]{1,0:T(8,128)(2,1)S(1)} %get-tuple-element.56), channel_id=1, source_target_pairs={{0,8},{8,0},{16,24},{24,16},{1,9},{9,1},{17,25},{25,17},{2,10},{10... | collective-permute-start | bytes 503816 | tf_op jit(solution)/shard_map/ppermute | solution.py:108
  25.5 1.5 %collective-permute-start.6 = (bf16[656,128]{1,0:T(8,128)(2,1)S(1)}, bf16[656,128]{1,0:T(8,128)(2,1)S(1)}, u32[]{:S(2)}, u32[]{:S(2)}) collective-permute-start(bf16[656,128]{1,0:T(8,128)(2,1)S(1)} %get-tuple-element.57), channel_id=1, source_target_pairs={{0,16},{8,24},{16,0},{24,8},{1,17},{9,25},{17,1},{25,9},{2,18},{10... | collective-permute-start | bytes 503816 | tf_op jit(solution)/shard_map/ppermute | solution.py:108
  27.5 1.0 %own.1 = (bf16[16,32,256]{2,1,0:T(8,128)(2,1)}, f32[512,256]{1,0:T(8,128)S(1)}) custom-call(f32[512,256]{1,0:T(8,128)S(1)} %get-tuple-element.59.preact, bf16[512,256]{1,0:T(8,128)(2,1)S(1)} %get-tuple-element.60.grad_pre, bf16[256,256]{1,0:T(8,128)(2,1)S(1)} %copy-done.1), custom_call_target="tpu_custom_call" | custom-call | flops 67108864 | bytes 1703936 | tf_op jit(solution)/shard_map/own/pallas_call | solution.py:28
  28.5 2.7 %collective-permute-done.5.refs_1_ = bf16[656,128]{1,0:T(8,128)(2,1)S(1)} collective-permute-done((bf16[656,128]{1,0:T(8,128)(2,1)S(1)}, bf16[656,128]{1,0:T(8,128)(2,1)S(1)}, u32[]{:S(2)}, u32[]{:S(2)}) %collective-permute-start.5) | collective-permute-done | bytes 167968 | tf_op jit(solution)/shard_map/ppermute | solution.py:108
  31.1 4.0 %collective-permute-done.6.refs_2_ = bf16[656,128]{1,0:T(8,128)(2,1)S(1)} collective-permute-done((bf16[656,128]{1,0:T(8,128)(2,1)S(1)}, bf16[656,128]{1,0:T(8,128)(2,1)S(1)}, u32[]{:S(2)}, u32[]{:S(2)}) %collective-permute-start.6) | collective-permute-done | bytes 167968 | tf_op jit(solution)/shard_map/ppermute | solution.py:108
  35.3 2.5 %collective-permute-start.8 = (bf16[272,128]{1,0:T(8,128)(2,1)S(1)}, bf16[272,128]{1,0:T(8,128)(2,1)S(1)}, u32[]{:S(2)}, u32[]{:S(2)}) collective-permute-start(bf16[272,128]{1,0:T(8,128)(2,1)S(1)} %get-tuple-element.66), channel_id=1, source_target_pairs={{0,6},{1,7},{2,4},{3,5},{4,2},{5,3},{6,0},{7,1},{8,14},{9,15},{10,... | collective-permute-start | bytes 208904 | tf_op jit(solution)/shard_map/ppermute | solution.py:108
  37.8 1.9 %collective-permute-start.10 = (bf16[272,128]{1,0:T(8,128)(2,1)S(1)}, bf16[272,128]{1,0:T(8,128)(2,1)S(1)}, u32[]{:S(2)}, u32[]{:S(2)}) collective-permute-start(bf16[272,128]{1,0:T(8,128)(2,1)S(1)} %get-tuple-element.71), channel_id=1, source_target_pairs={{0,4},{1,5},{2,6},{3,7},{4,0},{5,1},{6,2},{7,3},{8,12},{9,13},{10,... | collective-permute-start | bytes 208904 | tf_op jit(solution)/shard_map/ppermute | solution.py:108
  39.7 2.0 %collective-permute-done.8.refs_3_ = bf16[272,128]{1,0:T(8,128)(2,1)S(1)} collective-permute-done((bf16[272,128]{1,0:T(8,128)(2,1)S(1)}, bf16[272,128]{1,0:T(8,128)(2,1)S(1)}, u32[]{:S(2)}, u32[]{:S(2)}) %collective-permute-start.8) | collective-permute-done | bytes 69664 | tf_op jit(solution)/shard_map/ppermute | solution.py:108
  41.7 1.7 %collective-permute-done.9.refs_1_ = bf16[272,128]{1,0:T(8,128)(2,1)S(1)} collective-permute-done((bf16[272,128]{1,0:T(8,128)(2,1)S(1)}, bf16[272,128]{1,0:T(8,128)(2,1)S(1)}, u32[]{:S(2)}, u32[]{:S(2)}) %collective-permute-start.9) | collective-permute-done | bytes 69664 | tf_op jit(solution)/shard_map/ppermute | solution.py:108
  43.4 1.5 %collective-permute-start.13 = (bf16[64,256]{1,0:T(8,128)(2,1)S(1)}, bf16[64,256]{1,0:T(8,128)(2,1)S(1)}, u32[]{:S(2)}, u32[]{:S(2)}) collective-permute-start(bf16[64,256]{1,0:T(8,128)(2,1)S(1)} %piece.1.refs_0_), channel_id=1, source_target_pairs={{0,24},{8,16},{16,8},{24,0},{1,25},{9,17},{17,9},{25,1},{2,26},{10... | collective-permute-start | bytes 98312 | tf_op jit(solution)/shard_map/ppermute | solution.py:108
  44.9 1.4 %collective-permute-start.12 = (bf16[64,256]{1,0:T(8,128)(2,1)S(1)}, bf16[64,256]{1,0:T(8,128)(2,1)S(1)}, u32[]{:S(2)}, u32[]{:S(2)}) collective-permute-start(bf16[64,256]{1,0:T(8,128)(2,1)S(1)} %piece.1.refs_0_), channel_id=1, source_target_pairs={{0,16},{8,24},{16,0},{24,8},{1,17},{9,25},{17,1},{25,9},{2,18},{10... | collective-permute-start | bytes 98312 | tf_op jit(solution)/shard_map/ppermute | solution.py:108
  46.3 0.7 %collective-permute-start.11 = (bf16[64,256]{1,0:T(8,128)(2,1)S(1)}, bf16[64,256]{1,0:T(8,128)(2,1)S(1)}, u32[]{:S(2)}, u32[]{:S(2)}) collective-permute-start(bf16[64,256]{1,0:T(8,128)(2,1)S(1)} %piece.1.refs_0_), channel_id=1, source_target_pairs={{0,8},{8,0},{16,24},{24,16},{1,9},{9,1},{17,25},{25,17},{2,10},{10... | collective-permute-start | bytes 98312 | tf_op jit(solution)/shard_map/ppermute | solution.py:108
  47.0 1.3 %finish.1 = (bf16[16,32,256]{2,1,0:T(8,128)(2,1)}, f32[1,256]{1,0:T(1,128)}) custom-call(s32[1,8]{1,0:T(1,128)S(1)} %copy-done.5, f32[512,256]{1,0:T(8,128)S(1)} %get-tuple-element.73.self_term, bf16[272,128]{1,0:T(8,128)(2,1)S(1)} %get-tuple-element.69.refs_0_, bf16[272,128]{1,0:T(8,128)(2,1)S(1)} %collective-permute-done.9.refs_1_, ...), custom_call_target="tpu_custom_call" | custom-call | bytes 1066016 | tf_op jit(solution)/shard_map/finish/pallas_call | solution.py:28
  48.8 1.4 %collective-permute-done.11.refs_1_ = bf16[64,256]{1,0:T(8,128)(2,1)S(1)} collective-permute-done((bf16[64,256]{1,0:T(8,128)(2,1)S(1)}, bf16[64,256]{1,0:T(8,128)(2,1)S(1)}, u32[]{:S(2)}, u32[]{:S(2)}) %collective-permute-start.11) | collective-permute-done | bytes 32800 | tf_op jit(solution)/shard_map/ppermute | solution.py:108
  50.3 1.3 %collective-permute-done.14.other = bf16[256,256]{1,0:T(8,128)(2,1)S(1)} collective-permute-done((bf16[256,256]{1,0:T(8,128)(2,1)S(1)}, bf16[256,256]{1,0:T(8,128)(2,1)S(1)}, u32[]{:S(2)}, u32[]{:S(2)}) %collective-permute-start.14) | collective-permute-done | bytes 131104 | tf_op jit(solution)/shard_map/ppermute | solution.py:108
  51.7 0.8 %widen.1 = (f32[256,256]{1,0:T(8,128)}, f32[256,256]{1,0:T(8,128)}) custom-call(bf16[256,256]{1,0:T(8,128)(2,1)S(1)} %gather_pieces.1.mine, bf16[256,256]{1,0:T(8,128)(2,1)S(1)} %collective-permute-done.14.other), custom_call_target="tpu_custom_call" | custom-call | bytes 786432 | tf_op jit(solution)/shard_map/widen/pallas_call | solution.py:28
  (27 shorter events, 2.0 us)
Async XLA Ops:
  0.6 0.7 %copy-start.5 = (s32[1,8]{1,0:T(1,128)S(1)}, s32[1,8]{1,0:T(1,128)}, u32[]{:S(2)}) copy-start(s32[1,8]{1,0:T(1,128)} %requests_in.3) | copy-start | bytes 100
  2.6 18.1 %copy-start.6 = (f32[256]{0:T(256)S(1)}, f32[256]{0:T(256)}, u32[]{:S(2)}) copy-start(f32[256]{0:T(256)} %param.16) | copy-start | bytes 3076
  2.6 1.7 %collective-permute-start = (bf16[4,128,256]{2,1,0:T(8,128)(2,1)S(1)}, bf16[4,128,256]{2,1,0:T(8,128)(2,1)S(1)}, u32[]{:S(2)}, u32[]{:S(2)}) collective-permute-start(bf16[4,128,256]{2,1,0:T(8,128)(2,1)S(1)} %get-tuple-element.46), channel_id=1, source_target_pairs={{0,1},{1,0},{2,3},{3,2},{4,5},{5,4},{6,7},{7,6},{8,9},{9,8},{10,11... | collective-permute-start | bytes 786440 | tf_op jit(solution)/shard_map/ppermute | solution.py:108
  4.3 13.6 %collective-permute-start.1 = (bf16[2,128,256]{2,1,0:T(8,128)(2,1)S(1)}, bf16[2,128,256]{2,1,0:T(8,128)(2,1)S(1)}, u32[]{:S(2)}, u32[]{:S(2)}) collective-permute-start(bf16[2,128,256]{2,1,0:T(8,128)(2,1)S(1)} %get-tuple-element.47), channel_id=1, source_target_pairs={{0,7},{1,6},{2,5},{3,4},{4,3},{5,2},{6,1},{7,0},{8,15},{9,14},{10,... | collective-permute-start | bytes 393224 | tf_op jit(solution)/shard_map/ppermute | solution.py:108
  9.1 8.9 %collective-permute-start.2 = (bf16[2,128,256]{2,1,0:T(8,128)(2,1)S(1)}, bf16[2,128,256]{2,1,0:T(8,128)(2,1)S(1)}, u32[]{:S(2)}, u32[]{:S(2)}) collective-permute-start(bf16[2,128,256]{2,1,0:T(8,128)(2,1)S(1)} %get-tuple-element.50), channel_id=1, source_target_pairs={{0,2},{1,3},{2,0},{3,1},{4,6},{5,7},{6,4},{7,5},{8,10},{9,11},{10,... | collective-permute-start | bytes 393224 | tf_op jit(solution)/shard_map/ppermute | solution.py:108
  9.1 11.6 %collective-permute-start.3 = (bf16[2,128,256]{2,1,0:T(8,128)(2,1)S(1)}, bf16[2,128,256]{2,1,0:T(8,128)(2,1)S(1)}, u32[]{:S(2)}, u32[]{:S(2)}) collective-permute-start(bf16[2,128,256]{2,1,0:T(8,128)(2,1)S(1)} %get-tuple-element.51), channel_id=1, source_target_pairs={{0,5},{1,4},{2,7},{3,6},{4,1},{5,0},{6,3},{7,2},{8,13},{9,12},{10,... | collective-permute-start | bytes 393224 | tf_op jit(solution)/shard_map/ppermute | solution.py:108
  9.4 1.2 %copy-start = (bf16[16,128,256]{2,1,0:T(8,128)(2,1)S(1)}, bf16[16,128,256]{2,1,0:T(8,128)(2,1)}, u32[]{:S(2)}) copy-start(bf16[16,128,256]{2,1,0:T(8,128)(2,1)} %refs_3_.1) | copy-start | bytes 3145732
  10.7 0.9 %copy-start.1 = (bf16[256,256]{1,0:T(8,128)(2,1)S(1)}, bf16[256,256]{1,0:T(8,128)(2,1)}, u32[]{:S(2)}) copy-start(bf16[256,256]{1,0:T(8,128)(2,1)} %w_self.1) | copy-start | bytes 393220
  11.6 1.0 %copy-start.2 = (bf16[1,64,32,128]{3,2,1,0:T(8,128)(2,1)S(1)}, bf16[1,64,32,128]{3,2,1,0:T(8,128)(2,1)}, u32[]{:S(2)}) copy-start(bf16[1,64,32,128]{3,2,1,0:T(8,128)(2,1)} %refs_2_.1) | copy-start | bytes 1572868
  12.6 0.9 %copy-start.3 = (bf16[16,32,256]{2,1,0:T(8,128)(2,1)S(1)}, bf16[16,32,256]{2,1,0:T(8,128)(2,1)}, u32[]{:S(2)}) copy-start(bf16[16,32,256]{2,1,0:T(8,128)(2,1)} %refs_6_.1) | copy-start | bytes 786436
  13.6 0.9 %copy-start.4 = (bf16[256,256]{1,0:T(8,128)(2,1)S(1)}, bf16[256,256]{1,0:T(8,128)(2,1)}, u32[]{:S(2)}) copy-start(bf16[256,256]{1,0:T(8,128)(2,1)} %refs_5_.1) | copy-start | bytes 393220
  14.5 0.7 %copy-start.7 = (s32[1,64]{1,0:T(1,128)S(1)}, s32[1,64]{1,0:T(1,128)}, u32[]{:S(2)}) copy-start(s32[1,64]{1,0:T(1,128)} %refs_0_.1) | copy-start | bytes 772
  15.1 0.7 %copy-start.8 = (s32[1,64]{1,0:T(1,128)S(1)}, s32[1,64]{1,0:T(1,128)}, u32[]{:S(2)}) copy-start(s32[1,64]{1,0:T(1,128)} %refs_1_.1) | copy-start | bytes 772
  22.0 1.8 %collective-permute-start.4 = (bf16[784,256]{1,0:T(8,128)(2,1)S(1)}, bf16[784,256]{1,0:T(8,128)(2,1)S(1)}, u32[]{:S(2)}, u32[]{:S(2)}) collective-permute-start(bf16[784,256]{1,0:T(8,128)(2,1)S(1)} %get-tuple-element.54), channel_id=1, source_target_pairs={{0,1},{1,0},{2,3},{3,2},{4,5},{5,4},{6,7},{7,6},{8,9},{9,8},{10,11... | collective-permute-start | bytes 1204232 | tf_op jit(solution)/shard_map/ppermute | solution.py:108
  23.9 7.2 %collective-permute-start.5 = (bf16[656,128]{1,0:T(8,128)(2,1)S(1)}, bf16[656,128]{1,0:T(8,128)(2,1)S(1)}, u32[]{:S(2)}, u32[]{:S(2)}) collective-permute-start(bf16[656,128]{1,0:T(8,128)(2,1)S(1)} %get-tuple-element.56), channel_id=1, source_target_pairs={{0,8},{8,0},{16,24},{24,16},{1,9},{9,1},{17,25},{25,17},{2,10},{10... | collective-permute-start | bytes 503816 | tf_op jit(solution)/shard_map/ppermute | solution.py:108
  25.5 9.6 %collective-permute-start.6 = (bf16[656,128]{1,0:T(8,128)(2,1)S(1)}, bf16[656,128]{1,0:T(8,128)(2,1)S(1)}, u32[]{:S(2)}, u32[]{:S(2)}) collective-permute-start(bf16[656,128]{1,0:T(8,128)(2,1)S(1)} %get-tuple-element.57), channel_id=1, source_target_pairs={{0,16},{8,24},{16,0},{24,8},{1,17},{9,25},{17,1},{25,9},{2,18},{10... | collective-permute-start | bytes 503816 | tf_op jit(solution)/shard_map/ppermute | solution.py:108
  27.0 8.1 %collective-permute-start.7 = (bf16[656,128]{1,0:T(8,128)(2,1)S(1)}, bf16[656,128]{1,0:T(8,128)(2,1)S(1)}, u32[]{:S(2)}, u32[]{:S(2)}) collective-permute-start(bf16[656,128]{1,0:T(8,128)(2,1)S(1)} %get-tuple-element.58), channel_id=1, source_target_pairs={{0,24},{8,16},{16,8},{24,0},{1,25},{9,17},{17,9},{25,1},{2,26},{10... | collective-permute-start | bytes 503816 | tf_op jit(solution)/shard_map/ppermute | solution.py:108
  35.3 6.5 %collective-permute-start.8 = (bf16[272,128]{1,0:T(8,128)(2,1)S(1)}, bf16[272,128]{1,0:T(8,128)(2,1)S(1)}, u32[]{:S(2)}, u32[]{:S(2)}) collective-permute-start(bf16[272,128]{1,0:T(8,128)(2,1)S(1)} %get-tuple-element.66), channel_id=1, source_target_pairs={{0,6},{1,7},{2,4},{3,5},{4,2},{5,3},{6,0},{7,1},{8,14},{9,15},{10,... | collective-permute-start | bytes 208904 | tf_op jit(solution)/shard_map/ppermute | solution.py:108
  37.8 5.6 %collective-permute-start.9 = (bf16[272,128]{1,0:T(8,128)(2,1)S(1)}, bf16[272,128]{1,0:T(8,128)(2,1)S(1)}, u32[]{:S(2)}, u32[]{:S(2)}) collective-permute-start(bf16[272,128]{1,0:T(8,128)(2,1)S(1)} %get-tuple-element.70), channel_id=1, source_target_pairs={{0,2},{1,3},{2,0},{3,1},{4,6},{5,7},{6,4},{7,5},{8,10},{9,11},{10,... | collective-permute-start | bytes 208904 | tf_op jit(solution)/shard_map/ppermute | solution.py:108
  37.8 5.6 %collective-permute-start.10 = (bf16[272,128]{1,0:T(8,128)(2,1)S(1)}, bf16[272,128]{1,0:T(8,128)(2,1)S(1)}, u32[]{:S(2)}, u32[]{:S(2)}) collective-permute-start(bf16[272,128]{1,0:T(8,128)(2,1)S(1)} %get-tuple-element.71), channel_id=1, source_target_pairs={{0,4},{1,5},{2,6},{3,7},{4,0},{5,1},{6,2},{7,3},{8,12},{9,13},{10,... | collective-permute-start | bytes 208904 | tf_op jit(solution)/shard_map/ppermute | solution.py:108
  43.4 4.9 %collective-permute-start.13 = (bf16[64,256]{1,0:T(8,128)(2,1)S(1)}, bf16[64,256]{1,0:T(8,128)(2,1)S(1)}, u32[]{:S(2)}, u32[]{:S(2)}) collective-permute-start(bf16[64,256]{1,0:T(8,128)(2,1)S(1)} %piece.1.refs_0_), channel_id=1, source_target_pairs={{0,24},{8,16},{16,8},{24,0},{1,25},{9,17},{17,9},{25,1},{2,26},{10... | collective-permute-start | bytes 98312 | tf_op jit(solution)/shard_map/ppermute | solution.py:108
  44.9 3.9 %collective-permute-start.12 = (bf16[64,256]{1,0:T(8,128)(2,1)S(1)}, bf16[64,256]{1,0:T(8,128)(2,1)S(1)}, u32[]{:S(2)}, u32[]{:S(2)}) collective-permute-start(bf16[64,256]{1,0:T(8,128)(2,1)S(1)} %piece.1.refs_0_), channel_id=1, source_target_pairs={{0,16},{8,24},{16,0},{24,8},{1,17},{9,25},{17,1},{25,9},{2,18},{10... | collective-permute-start | bytes 98312 | tf_op jit(solution)/shard_map/ppermute | solution.py:108
  46.3 3.9 %collective-permute-start.11 = (bf16[64,256]{1,0:T(8,128)(2,1)S(1)}, bf16[64,256]{1,0:T(8,128)(2,1)S(1)}, u32[]{:S(2)}, u32[]{:S(2)}) collective-permute-start(bf16[64,256]{1,0:T(8,128)(2,1)S(1)} %piece.1.refs_0_), channel_id=1, source_target_pairs={{0,8},{8,0},{16,24},{24,16},{1,9},{9,1},{17,25},{25,17},{2,10},{10... | collective-permute-start | bytes 98312 | tf_op jit(solution)/shard_map/ppermute | solution.py:108
  50.2 1.4 %collective-permute-start.14 = (bf16[256,256]{1,0:T(8,128)(2,1)S(1)}, bf16[256,256]{1,0:T(8,128)(2,1)S(1)}, u32[]{:S(2)}, u32[]{:S(2)}) collective-permute-start(bf16[256,256]{1,0:T(8,128)(2,1)S(1)} %gather_pieces.1.mine), channel_id=1, source_target_pairs={{0,1},{1,0},{2,3},{3,2},{4,5},{5,4},{6,7},{7,6},{8,9},{9,8},{10,11... | collective-permute-start | bytes 393224 | tf_op jit(solution)/shard_map/ppermute | solution.py:108
